TPU v7x, 128 devices: a whole 4x4x4 slice. The times are simulated.
128 devices in a mesh: row: 16 (over z_lo, y, core), col: 8 (over z_hi, x).
Axes of the slice: x: 4, y: 4, z: 4 (z_hi: 2, z_lo: 2; z = z_hi * 2 + z_lo), core: 2. Of those that a mesh axis runs over, the one named last changes fastest.
Arguments:
- features: bfloat16 [131072, 256], P(('row', 'col')), may hold values from -6 to 6
- weight: bfloat16 [256, 256], replicated, may hold values from -0.375 to 0.375
- layer_bias: float32 [256], replicated, may hold values from -3 to 3
- tile_values: bfloat16 [16, 8, 384, 128, 128], P('row', 'col'), may hold values from -0.3125 to 0.3125
- tile_rows: int32 [16, 8, 384], P('row', 'col'), may hold values from 0 to 63, as said below
- tile_cols: int32 [16, 8, 384], P('row', 'col'), may hold values from 0 to 127, as said below
- tile_count: int32 [16, 8], P('row', 'col'), may hold values from 48 to 384, as said below
- cotangent: bfloat16 [131072, 256], P(('row', 'col')), may hold values from -6 to 6
Outputs:
- activations: bfloat16 [131072, 256], P(('row', 'col'))
- grad_features: bfloat16 [131072, 256], P(('row', 'col'))
- grad_weight: float32 [256, 256], replicated
Inputs may be any that keep to these rules, and one draw needn't show every extreme that they name: On each device the first tile_count slots name distinct tile positions (tile_rows, tile_cols), in increasing order of tile_cols and, within one tile column, of tile_rows; later slots hold valid but ignored positions. `tile_cols`: see tile_rows for the order of live slots. `tile_count`: live slots differ strongly from device to device; some device holds 384 in every draw.
All inputs are finite; a program needn't handle non-finite values.
Results may differ from a plain program's by a relative error of at most 0.0065.
Values may be sent and summed in bfloat16 or wider, within the bound.
No kernel may reach another device: no remote copies, remote signals or barrier semaphores. Data moves between devices by JAX's collectives and lax.ppermute only.
A program may use at most 192 MiB of HBM per device.

v0:
```python
import jax
import jax.numpy as jnp
from jax import lax
from jax.sharding import PartitionSpec as P


def silu_parts(shifted):
    sig_part = jax.nn.sigmoid(shifted)
    return (shifted * sig_part, sig_part * (1.0 + shifted * (1.0 - sig_part)))


def on_device(
    features, weight, layer_bias, tile_values, tile_rows, tile_cols, tile_count, cotangent
):
    values = tile_values[0, 0]
    row_ids = tile_rows[0, 0]
    col_ids = tile_cols[0, 0]
    live_count = tile_count[0, 0]
    slot_total, tile_size, _ = values.shape
    node_dev, feature_width = features.shape
    row_devices = lax.axis_size("row")
    col_devices = lax.axis_size("col")
    row_blocks = node_dev * col_devices // tile_size
    col_blocks = node_dev * row_devices // tile_size
    group_size = min(32, slot_total)
    slot_ids = jnp.arange(slot_total, dtype=jnp.int32)
    col_key = jnp.where(slot_ids < live_count, col_ids, col_blocks)

    def sweep(first_block, block_number, apply_group, totals):
        low_end = jnp.sum(col_key < first_block)
        high_end = jnp.sum(col_key < first_block + block_number)

        def group_step(group_index, running):
            group_begin = group_index * group_size
            group_start = jnp.minimum(group_begin, slot_total - group_size)
            slot_index = group_start + jnp.arange(group_size, dtype=jnp.int32)
            live_mask = (slot_index >= jnp.maximum(group_begin, low_end)) & (slot_index < high_end)
            group_values = lax.dynamic_slice_in_dim(values, group_start, group_size, 0)
            group_rows = lax.dynamic_slice_in_dim(row_ids, group_start, group_size, 0)
            group_cols = lax.dynamic_slice_in_dim(col_ids, group_start, group_size, 0)
            col_local = jnp.clip(group_cols - first_block, 0, block_number - 1)
            return apply_group(running, group_values, group_rows, col_local, live_mask)

        return lax.fori_loop(
            low_end // group_size, (high_end + group_size - 1) // group_size, group_step, totals
        )

    hidden = jnp.dot(features, weight, preferred_element_type=jnp.float32).astype(jnp.bfloat16)
    empty_rows = jnp.zeros((row_blocks, tile_size, feature_width), jnp.float32)
    whole_cols = lax.all_gather(hidden, "row", axis=0, tiled=True)
    blocks = whole_cols.reshape(-1, tile_size, feature_width)

    def apply_group(running, group_values, group_rows, col_local, live_mask):
        selected = jnp.take(blocks, col_local, axis=0)
        products = jnp.einsum(
            "tij,tjf->tif", group_values, selected, preferred_element_type=jnp.float32
        )
        products = jnp.where(live_mask[:, None, None], products, 0.0)
        return running.at[group_rows].add(products)

    partial_value = sweep(0 // tile_size, blocks.shape[0], apply_group, empty_rows)
    partial_value = partial_value.reshape(row_blocks * tile_size, feature_width)
    summed = lax.psum_scatter(partial_value, "col", scatter_dimension=0, tiled=True)
    value_part, slope_part = silu_parts(summed + layer_bias[None, :])
    activations = value_part.astype(jnp.bfloat16)
    grad_pre = (cotangent.astype(jnp.float32) * slope_part).astype(jnp.bfloat16)
    grad_group = lax.all_gather(grad_pre, "col", axis=0, tiled=True)
    grad_blocks = grad_group.reshape(row_blocks, tile_size, feature_width)
    row_number = node_dev * lax.axis_size("row")
    block_number = row_number // tile_size

    def apply_group(running, group_values, group_rows, col_local, live_mask):
        selected = jnp.take(grad_blocks, group_rows, axis=0)
        products = jnp.einsum(
            "tij,tif->tjf", group_values, selected, preferred_element_type=jnp.float32
        )
        products = jnp.where(live_mask[:, None, None], products, 0.0)
        return running.at[col_local].add(products)

    empty_cols = jnp.zeros((block_number, tile_size, feature_width), jnp.float32)
    totals = sweep(jnp.int32(0) // tile_size, block_number, apply_group, empty_cols)
    grad_hidden = lax.psum_scatter(
        totals.reshape(row_number, feature_width), "row", scatter_dimension=0, tiled=True
    )
    grad_rounded = grad_hidden.astype(jnp.bfloat16)
    grad_features = lax.dot_general(
        grad_rounded, weight, (((1,), (1,)), ((), ())), preferred_element_type=jnp.float32
    ).astype(jnp.bfloat16)
    weight_term = lax.dot_general(
        features, grad_rounded, (((0,), (0,)), ((), ())), preferred_element_type=jnp.float32
    )
    grad_weight = lax.psum(weight_term, ("row", "col"))
    grad_weight = grad_weight * float(row_devices * col_devices * node_dev) ** (-0.5)
    return (activations, grad_features, grad_weight)


def solution(mesh):
    return jax.shard_map(
        on_device,
        mesh=mesh,
        in_specs=(
            P(("row", "col"), None),
            P(),
            P(),
            P("row", "col", None, None, None),
            P("row", "col", None),
            P("row", "col", None),
            P("row", "col"),
            P(("row", "col"), None),
        ),
        out_specs=(P(("row", "col"), None), P(("row", "col"), None), P()),
        check_vma=False,
    )
```

profile of v0, /device:TPU:1, one launch (start us, length us, event | category | flops | bytes accessed | tf_op | source)
XLA Modules:
  0.0 959.3 jit_solution(12744434519094539536)
XLA Ops:
  15.9 50.3 %all-gather.3.cloned.1.call-done = bf16[16384,256]{1,0:T(8,128)(2,1)} async-done(((bf16[1024,256]{1,0:T(8,128)(2,1)}), bf16[16384,256]{1,0:T(8,128)(2,1)}) %all-gather.3.cloned.1.call-update) | async-done | bytes 8388624 | tf_op jit(solution)/shard_map/all_gather | solution.py:50
  66.2 4.2 broadcast_in_dim.76
  70.4 116.4 %while.21 = (s32[]{:T(128)}, f32[64,128,256]{2,1,0:T(8,128)}, s32[]{:T(128)}, s32[384]{0:T(512)S(1)}, s32[]{:T(128)}, /*index=5*/s32[]{:T(128)}, bf16[384,128,12...) while((s32[]{:T(128)}, f32[64,128,256]{2,1,0:T(8,128)}, ...), condition=%wide.region_4.5_spmd, body=%wide.region_2.4_spmd.sunk | while | flops 271582656 | bytes 24122596 | solution.py:44
  71.8 4.1 gather_fusion
  75.8 3.9 convolution_select_fusion.4
  79.8 9.8 %scatter_fusion = f32[64,128,256]{2,1,0:T(8,128)} fusion(f32[64,128,256]{2,1,0:T(8,128)} %get-tuple-element.331, s32[32]{0:T(128)S(1)} %compare_select_fusion.8, f32[32,128,256]{2,1,0:T(8,128)} %convolution_select_fusion.4), kind=kCustom, calls=%fused_computation.2.clone.1 | custom fusion | flops 1048576 | bytes 12583040 | tf_op jit(solution)/shard_map/while/body/scatter-add | solution.py:59
  91.0 4.1 gather_fusion
  95.0 3.9 convolution_select_fusion.4
  99.0 10.0 %scatter_fusion = f32[64,128,256]{2,1,0:T(8,128)} fusion(f32[64,128,256]{2,1,0:T(8,128)} %get-tuple-element.331, s32[32]{0:T(128)S(1)} %compare_select_fusion.8, f32[32,128,256]{2,1,0:T(8,128)} %convolution_select_fusion.4), kind=kCustom, calls=%fused_computation.2.clone.1 | custom fusion | flops 1048576 | bytes 12583040 | tf_op jit(solution)/shard_map/while/body/scatter-add | solution.py:59
  110.3 4.1 gather_fusion
  114.4 3.9 convolution_select_fusion.4
  118.3 10.1 %scatter_fusion = f32[64,128,256]{2,1,0:T(8,128)} fusion(f32[64,128,256]{2,1,0:T(8,128)} %get-tuple-element.331, s32[32]{0:T(128)S(1)} %compare_select_fusion.8, f32[32,128,256]{2,1,0:T(8,128)} %convolution_select_fusion.4), kind=kCustom, calls=%fused_computation.2.clone.1 | custom fusion | flops 1048576 | bytes 12583040 | tf_op jit(solution)/shard_map/while/body/scatter-add | solution.py:59
  129.8 4.1 gather_fusion
  133.9 3.9 convolution_select_fusion.4
  137.8 10.0 %scatter_fusion = f32[64,128,256]{2,1,0:T(8,128)} fusion(f32[64,128,256]{2,1,0:T(8,128)} %get-tuple-element.331, s32[32]{0:T(128)S(1)} %compare_select_fusion.8, f32[32,128,256]{2,1,0:T(8,128)} %convolution_select_fusion.4), kind=kCustom, calls=%fused_computation.2.clone.1 | custom fusion | flops 1048576 | bytes 12583040 | tf_op jit(solution)/shard_map/while/body/scatter-add | solution.py:59
  149.1 4.1 gather_fusion
  153.2 3.9 convolution_select_fusion.4
  157.1 10.1 %scatter_fusion = f32[64,128,256]{2,1,0:T(8,128)} fusion(f32[64,128,256]{2,1,0:T(8,128)} %get-tuple-element.331, s32[32]{0:T(128)S(1)} %compare_select_fusion.8, f32[32,128,256]{2,1,0:T(8,128)} %convolution_select_fusion.4), kind=kCustom, calls=%fused_computation.2.clone.1 | custom fusion | flops 1048576 | bytes 12583040 | tf_op jit(solution)/shard_map/while/body/scatter-add | solution.py:59
  168.6 4.1 gather_fusion
  172.6 3.9 convolution_select_fusion.4
  176.6 10.2 %scatter_fusion = f32[64,128,256]{2,1,0:T(8,128)} fusion(f32[64,128,256]{2,1,0:T(8,128)} %get-tuple-element.331, s32[32]{0:T(128)S(1)} %compare_select_fusion.8, f32[32,128,256]{2,1,0:T(8,128)} %convolution_select_fusion.4), kind=kCustom, calls=%fused_computation.2.clone.1 | custom fusion | flops 1048576 | bytes 12583040 | tf_op jit(solution)/shard_map/while/body/scatter-add | solution.py:59
  186.9 230.9 %reduce-scatter.3.cloned.1.call-done = f32[1024,256]{1,0:T(8,128)} async-done(((f32[8192,256]{1,0:T(8,128)}), f32[1024,256]{1,0:T(8,128)}) %reduce-scatter.3.cloned.1.call-update) | async-done | bytes 1048592 | tf_op jit(solution)/shard_map/reduce_scatter | solution.py:63
  417.8 2.7 multiply_convert_fusion
  420.5 16.7 %copy.11 = bf16[1,1,384,128,128]{3,4,2,1,0:T(8,128)(2,1)} copy(bf16[1,1,384,128,128]{4,3,2,1,0:T(8,128)(2,1)} %bitcast.18) | data formatting | bytes 25165824 | tf_op args[3]
  437.2 52.9 %all-gather.5.cloned.1.call-done = bf16[8192,256]{1,0:T(8,128)(2,1)} async-done(((bf16[1024,256]{1,0:T(8,128)(2,1)}), bf16[8192,256]{1,0:T(8,128)(2,1)}) %all-gather.5.cloned.1.call-update) | async-done | bytes 4194320 | tf_op jit(solution)/shard_map/all_gather | solution.py:67
  490.1 7.8 broadcast_in_dim.77
  497.9 107.1 %while.22 = (s32[]{:T(128)}, f32[128,128,256]{2,1,0:T(8,128)}, s32[]{:T(128)}, s32[384]{0:T(512)S(1)}, s32[]{:T(128)}, /*index=5*/s32[]{:T(128)}, bf16[384,128,1...) while((s32[]{:T(128)}, f32[128,128,256]{2,1,0:T(8,128)}, ...), condition=%wide.region_8.9_spmd, body=%wide.region_6.8_spmd.sunk | while | flops 271582656 | bytes 24122596 | solution.py:44
  499.3 2.9 gather_fusion.1
  502.2 4.1 convolution_select_fusion.5
  506.2 9.7 %scatter_fusion.1 = f32[128,128,256]{2,1,0:T(8,128)} fusion(f32[128,128,256]{2,1,0:T(8,128)} %get-tuple-element.373, s32[32]{0:T(128)S(1)} %compare_select_fusion.9, f32[32,128,256]{2,1,0:T(8,128)} %convolution_select_fusion.5), kind=kCustom, calls=%fused_computation.3.clone.1 | custom fusion | flops 1048576 | bytes 12583040 | tf_op jit(solution)/shard_map/while/body/scatter-add | solution.py:78
  517.3 2.9 gather_fusion.1
  520.2 4.1 convolution_select_fusion.5
  524.2 9.5 scatter_fusion.1
  535.0 2.9 gather_fusion.1
  537.9 4.1 convolution_select_fusion.5
  542.0 9.6 scatter_fusion.1
  552.9 2.9 gather_fusion.1
  555.8 4.1 convolution_select_fusion.5
  559.8 9.6 scatter_fusion.1
  570.8 2.9 gather_fusion.1
  573.6 4.1 convolution_select_fusion.5
  577.7 9.5 scatter_fusion.1
  588.6 2.9 gather_fusion.1
  591.5 4.1 convolution_select_fusion.5
  595.5 9.5 scatter_fusion.1
  605.1 198.9 %reduce-scatter.5.cloned.1.call-done = f32[1024,256]{1,0:T(8,128)} async-done(((f32[16384,256]{1,0:T(8,128)}), f32[1024,256]{1,0:T(8,128)}) %reduce-scatter.5.cloned.1.call-update) | async-done | bytes 1048592 | tf_op jit(solution)/shard_map/reduce_scatter | solution.py:82
  806.2 2.4 convolution_convert_fusion
  808.6 142.4 %all-reduce.2.cloned.1.call-done = f32[256,256]{0,1:T(8,128)} async-done(((f32[256,256]{0,1:T(8,128)}), f32[256,256]{0,1:T(8,128)}) %all-reduce.2.cloned.1.call-update) | async-done | bytes 262160 | tf_op jit(solution)/shard_map/psum | solution.py:92
  (61 shorter events, 18.9 us)
Async XLA Ops:
  7.2 1.0 copy-start
  7.2 59.0 %all-gather.3.cloned.1.call-start = ((), (), s32[]{:S(2)}) async-start(), calls=%async_computation.2 | async-start | bytes 8912896 | tf_op jit(solution)/shard_map/all_gather | solution.py:50
  10.2 407.5 %reduce-scatter.3.cloned.1.call-start = ((), (), s32[]{:S(2)}) async-start(), calls=%async_computation.3 | async-start | bytes 9437184 | tf_op jit(solution)/shard_map/reduce_scatter | solution.py:63
  186.8 231.0 %copy-start.1 = (bf16[1024,256]{1,0:T(8,128)(2,1)S(1)}, bf16[1024,256]{1,0:T(8,128)(2,1)}, u32[]{:S(2)}) copy-start(bf16[1024,256]{1,0:T(8,128)(2,1)} %param.19) | copy-start | bytes 1572868
  186.8 231.0 %copy-start.3 = (f32[256]{0:T(256)S(1)}, f32[256]{0:T(256)}, u32[]{:S(2)}) copy-start(f32[256]{0:T(256)} %param.14) | copy-start | bytes 3076
  186.8 303.3 %all-gather.5.cloned.1.call-start = ((), (), s32[]{:S(2)}) async-start(), calls=%async_computation.4 | async-start | bytes 4718592 | tf_op jit(solution)/shard_map/all_gather | solution.py:67
  420.5 383.5 %reduce-scatter.5.cloned.1.call-start = ((), (), s32[]{:S(2)}) async-start(), calls=%async_computation.5 | async-start | bytes 17825792 | tf_op jit(solution)/shard_map/reduce_scatter | solution.py:82
  605.0 201.2 %copy-start.2 = (bf16[256,256]{1,0:T(8,128)(2,1)S(1)}, bf16[256,256]{1,0:T(8,128)(2,1)}, u32[]{:S(2)}) copy-start(bf16[256,256]{1,0:T(8,128)(2,1)} %param.13) | copy-start | bytes 393220
  605.0 345.9 %all-reduce.2.cloned.1.call-start = ((), (), s32[]{:S(2)}) async-start(), calls=%async_computation.6 | async-start | bytes 524288 | tf_op jit(solution)/shard_map/psum | solution.py:92
Sparse Core Ops, SparseCore 0:
  10.4 55.7 all-gather.2
  186.9 230.7 reduce-scatter.2
  420.7 69.3 all-gather.4
  605.2 198.7 reduce-scatter.4
  809.1 141.8 all-reduce.1
where the time goes:
time: 963 us; the launch traced here: 959 us
  waiting for transfers between devices  675 us (70%)
  other arithmetic  133 us (14%)
  local copies, waits for them, and re-layouts  72.2 us (7%)
  matrix products  54.5 us (6%)
  between operations  17.3 us (2%)
    reduce_scatter x1, waiting for transfers between devices, on_device(): lax.psum_scatter(partial_value, 'col', scatter_dimension=0, tiled=True)  231 us
    reduce_scatter x1, waiting for transfers between devices, on_device(): lax.psum_scatter(totals.reshape(row_number, feature_width), 'row', scatte...  199 us
    psum x1, waiting for transfers between devices, on_device(): grad_weight = lax.psum(weight_term, ('row', 'col'))  142 us
    scatter-add x6, other arithmetic, apply_group(): return running.at[group_rows].add(products)  60.2 us
    scatter-add x6, other arithmetic, apply_group(): return running.at[col_local].add(products)  57.3 us
    all_gather x1, waiting for transfers between devices, on_device(): grad_group = lax.all_gather(grad_pre, 'col', axis=0, tiled=True)  52.9 us
    all_gather x1, waiting for transfers between devices, on_device(): whole_cols = lax.all_gather(hidden, 'row', axis=0, tiled=True)  50.3 us
    gather x6, local copies, waits for them, and re-layouts, apply_group(): selected = jnp.take(blocks, col_local, axis=0)  24.4 us
  transfers between devices with their start and end apart: 5, of which 5 were waited for; matrix products, arithmetic and copies ran while one was open for 2% of the time, Pallas kernels for 0%

commit v1 on v0

v1 whole, which is shorter than its diff:
```python
import functools

import jax
import jax.numpy as jnp
from jax import lax
from jax.experimental import pallas as pl
from jax.experimental.pallas import tpu as pltpu
from jax.sharding import Mesh
from jax.sharding import PartitionSpec as P

BF16 = jnp.bfloat16
F32 = jnp.float32
ROW = ("zl", "y", "core")
COL = ("zh", "x")
VMEM_LIMIT = 58 * 2**20
PARTS = 2
BATCH = 16
CHUNK = 32


def sweep_kernel(pieces, outputs, transpose, batch, chunk, *refs):
    count, src, dst, tiles = refs[:4]
    sources = refs[4 : 4 + pieces]
    results = refs[4 + pieces : 4 + pieces + outputs]
    tile_buf, source_buf, total, tile_sems, source_sem = refs[4 + pieces + outputs :]
    size = tile_buf.shape[1]
    live = count[0]
    chunks = (live + chunk - 1) // chunk
    rows = sources[0].shape[0]

    def tile_copy(index):
        span = pl.ds(index * chunk, chunk)
        return pltpu.make_async_copy(tiles.at[span], tile_buf.at[span], tile_sems.at[index])

    def source_copy(index):
        return pltpu.make_async_copy(
            sources[index], source_buf.at[pl.ds(index * rows, rows)], source_sem.at[index]
        )

    def start_tiles(index, carry):
        tile_copy(index).start()
        return carry

    start_tiles(0, 0)
    for index in range(pieces):
        source_copy(index).start()
    lax.fori_loop(1, chunks, start_tiles, 0)
    total[...] = jnp.zeros_like(total)
    for index in range(pieces):
        source_copy(index).wait()

    contract = (((0,), (0,)), ((), ())) if transpose else (((1,), (0,)), ((), ()))

    def on_chunk(index, carry):
        tile_copy(index).wait()

        def on_batch(step, inner):
            base = index * chunk + step * batch
            products = []
            for lane in range(batch):
                start = pl.multiple_of(src[base + lane] * size, size)
                products.append(
                    lax.dot_general(
                        tile_buf[base + lane],
                        source_buf[pl.ds(start, size), :],
                        contract,
                        preferred_element_type=F32,
                    )
                )
            for lane in range(batch):
                start = pl.multiple_of(dst[base + lane] * size, size)
                span = pl.ds(start, size)
                total[span, :] = total[span, :] + products[lane]
            return inner

        steps = jnp.minimum(chunk // batch, (live - index * chunk + batch - 1) // batch)
        return lax.fori_loop(0, steps, on_batch, carry)

    lax.fori_loop(0, chunks, on_chunk, 0)
    done = 0
    for result in results:
        length = result.shape[0]
        result[...] = total[done : done + length, :].astype(result.dtype)
        done += length


def sweep(name, count, src, dst, tiles, sources, out_shapes, transpose):
    slots, size, _ = tiles.shape
    pieces = len(sources)
    rows, width = sources[0].shape
    out_rows = sum(s.shape[0] for s in out_shapes)
    chunk = min(CHUNK, slots)
    batch = min(BATCH, chunk)
    any_spec = pl.BlockSpec(memory_space=pl.ANY)
    flops = 2 * (slots // 3) * size * size * width
    return pl.pallas_call(
        functools.partial(sweep_kernel, pieces, len(out_shapes), transpose, batch, chunk),
        grid_spec=pltpu.PrefetchScalarGridSpec(
            num_scalar_prefetch=3,
            grid=(1,),
            in_specs=[any_spec] * (1 + pieces),
            out_specs=[
                pl.BlockSpec(s.shape, lambda i, *_: (0, 0), pipeline_mode=pl.Buffered(1))
                for s in out_shapes
            ],
            scratch_shapes=[
                pltpu.VMEM(tiles.shape, BF16),
                pltpu.VMEM((pieces * rows, width), BF16),
                pltpu.VMEM((out_rows + size, width), F32),
                pltpu.SemaphoreType.DMA((slots // chunk,)),
                pltpu.SemaphoreType.DMA((pieces,)),
            ],
        ),
        out_shape=out_shapes,
        compiler_params=pltpu.CompilerParams(vmem_limit_bytes=VMEM_LIMIT),
        cost_estimate=pl.CostEstimate(
            flops=flops, bytes_accessed=tiles.size * 2 + (pieces * rows + out_rows) * width * 2, transcendentals=0
        ),
        name=name,
    )(count, src, dst, tiles, *sources)


def split_dot(left, right, contract):
    high = left.astype(BF16)
    low = (left - high.astype(F32)).astype(BF16)
    first = lax.dot_general(high, right, contract, preferred_element_type=F32)
    return first + lax.dot_general(low, right, contract, preferred_element_type=F32)


def summed(refs, parts):
    per_part = len(refs) // parts
    columns = []
    for part in range(parts):
        group = refs[part * per_part : (part + 1) * per_part]
        value = group[0][...].astype(F32)
        for ref in group[1:]:
            value = value + ref[...].astype(F32)
        columns.append(value)
    return columns[0] if parts == 1 else jnp.concatenate(columns, axis=1)


def middle_kernel(parts, count, *refs):
    pieces = refs[:count]
    weight, bias, cotangent = refs[count : count + 3]
    act_ref = refs[count + 3]
    grads = refs[count + 4 : count + 4 + parts]
    weight_grad = refs[count + 4 + parts]
    gathered = summed(pieces, parts)
    shifted = split_dot(gathered, weight[...], (((1,), (0,)), ((), ()))) + bias[...]
    sig = 1.0 / (1.0 + jnp.exp(-shifted))
    act_ref[...] = (shifted * sig).astype(BF16)
    slope = sig * (1.0 + shifted * (1.0 - sig))
    grad = (cotangent[...].astype(F32) * slope).astype(BF16)
    width = grad.shape[1] // parts
    for part in range(parts):
        grads[part][...] = grad[:, part * width : (part + 1) * width]
    term = split_dot(gathered, grad, (((0,), (0,)), ((), ())))

    @pl.when(pl.program_id(0) == 0)
    def _():
        weight_grad[...] = jnp.zeros_like(weight_grad)

    weight_grad[...] += term


def middle(pieces, weight, bias, cotangent, parts):
    rows, width = cotangent.shape
    steps = 4
    block = rows // steps
    part_spec = pl.BlockSpec((block, width // parts), lambda i: (i, 0))
    wide_spec = pl.BlockSpec((block, width), lambda i: (i, 0))
    whole = pl.BlockSpec((width, width), lambda i: (0, 0))
    return pl.pallas_call(
        functools.partial(middle_kernel, parts, len(pieces)),
        grid=(steps,),
        in_specs=[part_spec] * len(pieces) + [whole, pl.BlockSpec((1, width), lambda i: (0, 0)), wide_spec],
        out_specs=[wide_spec] + [part_spec] * parts + [whole],
        out_shape=[jax.ShapeDtypeStruct((rows, width), BF16)]
        + [jax.ShapeDtypeStruct((rows, width // parts), BF16)] * parts
        + [jax.ShapeDtypeStruct((width, width), F32)],
        compiler_params=pltpu.CompilerParams(vmem_limit_bytes=VMEM_LIMIT),
        name="middle",
    )(*pieces, weight, bias.reshape(1, width), cotangent)


def final_kernel(parts, count, *refs):
    weight, out = refs[count], refs[count + 1]
    grad = summed(refs[:count], parts).astype(BF16)
    out[...] = lax.dot_general(
        grad, weight[...], (((1,), (1,)), ((), ())), preferred_element_type=F32
    ).astype(BF16)


def final(pieces, weight, parts):
    rows = pieces[0].shape[0]
    width = weight.shape[0]
    steps = 4
    block = rows // steps
    part_spec = pl.BlockSpec((block, width // parts), lambda i: (i, 0))
    return pl.pallas_call(
        functools.partial(final_kernel, parts, len(pieces)),
        grid=(steps,),
        in_specs=[part_spec] * len(pieces) + [pl.BlockSpec((width, width), lambda i: (0, 0))],
        out_specs=pl.BlockSpec((block, width), lambda i: (i, 0)),
        out_shape=jax.ShapeDtypeStruct((rows, width), BF16),
        compiler_params=pltpu.CompilerParams(vmem_limit_bytes=VMEM_LIMIT),
        name="final",
    )(*pieces, weight)


def shift(value, axes, sizes, offset):
    perm = []
    total = 1
    for size in sizes:
        total *= size
    for index in range(total):
        rest, coords = index, []
        for size in reversed(sizes):
            coords.append(rest % size)
            rest //= size
        coords.reverse()
        source = 0
        for coord, size, off in zip(coords, sizes, offset):
            source = source * size + (coord + off) % size
        perm.append((source, index))
    return lax.ppermute(value, axes, perm)


def sum_over_ring(value, axes, sizes, offsets):
    terms = [value] + [shift(value, axes, sizes, offset) for offset in offsets]
    return functools.reduce(lambda a, b: a + b, terms)


def sum_everywhere(value, core, x):
    rows = value.shape[0]
    half = rows // 2
    mine = lax.dynamic_slice_in_dim(value, core * half, half)
    other = lax.dynamic_slice_in_dim(value, (1 - core) * half, half)
    mine = mine + shift(other, "core", (2,), (1,))
    quarter = half // 4
    parts = [lax.dynamic_slice_in_dim(mine, lax.rem(x + off, 4) * quarter, quarter) for off in range(4)]
    own = parts[0]
    for off in range(1, 4):
        own = own + shift(parts[off], "x", (4,), (4 - off,))
    own = sum_over_ring(own, "y", (4,), [(1,), (2,), (3,)])
    own = sum_over_ring(own, ("zl", "zh"), (2, 2), [(0, 1), (1, 0), (1, 1)])
    ring = [own] + [shift(own, "x", (4,), (off,)) for off in range(1, 4)]
    ring = jnp.stack(ring)
    ordered = jnp.take(ring, jnp.remainder(jnp.arange(4) - x, 4), axis=0).reshape(half, -1)
    theirs = shift(ordered, "core", (2,), (1,))
    return jnp.where(core == 0, jnp.concatenate([ordered, theirs]), jnp.concatenate([theirs, ordered]))


def on_device(
    features, weight, layer_bias, tile_values, tile_rows, tile_cols, tile_count, cotangent
):
    tiles = tile_values[0, 0]
    slots, size, _ = tiles.shape
    nodes, width = features.shape
    per_slab = nodes // size
    count = tile_count.reshape(1)
    zl, y, core = (lax.axis_index(name) for name in ROW)
    zh, x = (lax.axis_index(name) for name in COL)
    rings = [(dz, dd) for dz in range(2) for dd in range(4)]
    part_width = width // PARTS

    row_ids, col_ids = tile_rows[0, 0], tile_cols[0, 0]
    row_slab, col_slab = row_ids // per_slab, col_ids // per_slab
    row_at = (((row_slab // 4) ^ zh) * 4 + (row_slab % 4 - x) % 4) * per_slab + row_ids % per_slab
    col_at = (
        (((col_slab // 8) ^ zl) * 4 + (col_slab // 2 % 4 - y) % 4) + ((col_slab % 2) ^ core) * 8
    ) * per_slab + col_ids % per_slab
    live = jnp.arange(slots, dtype=jnp.int32) < count[0]
    row_to = jnp.where(live, row_at, 8 * per_slab)
    col_to = jnp.where(live, col_at, 16 * per_slab)

    columns = [slice(part * part_width, (part + 1) * part_width) for part in range(PARTS)]
    partials = []
    for part in range(PARTS):
        own = features[:, columns[part]]
        same = [own] + [shift(own, ("zl", "y"), (2, 4), off) for off in rings[1:]]
        other = [shift(piece, "core", (2,), (1,)) for piece in same]
        partials.append(
            sweep(
                f"forward_{part}", count, col_at, row_to, tiles, same + other,
                [jax.ShapeDtypeStruct((nodes, part_width), BF16)] * 8, False,
            )
        )
    arrived = []
    for part in range(PARTS):
        arrived += [partials[part][0]]
        arrived += [
            shift(partials[part][k], COL, (2, 4), (rings[k][0], -rings[k][1])) for k in range(1, 8)
        ]
    activations, *grads, weight_term = middle(arrived, weight, layer_bias, cotangent, PARTS)

    collected = []
    for part in range(PARTS):
        own = grads[part]
        pieces = [own] + [shift(own, COL, (2, 4), off) for off in rings[1:]]
        *mine, theirs = sweep(
            f"backward_{part}", count, row_at, col_to, tiles, pieces,
            [jax.ShapeDtypeStruct((nodes, part_width), F32)] * 8
            + [jax.ShapeDtypeStruct((8 * nodes, part_width), BF16)], True,
        )
        swapped = shift(theirs, "core", (2,), (1,))
        for k in range(8):
            piece = mine[k] + swapped[k * nodes : (k + 1) * nodes].astype(F32)
            piece = piece.astype(BF16)
            if k:
                piece = shift(piece, ("zl", "y"), (2, 4), (rings[k][0], -rings[k][1]))
            collected.append(piece)
    grad_features = final(collected, weight, PARTS)
    grad_weight = sum_everywhere(weight_term, core, x)
    total_nodes = nodes * 128
    return activations, grad_features, grad_weight * float(total_nodes) ** -0.5


def solution(mesh):
    fine = Mesh(mesh.devices.reshape(2, 4, 2, 2, 4), ROW + COL)
    nodes = P(ROW + COL, None)
    return jax.shard_map(
        on_device,
        mesh=fine,
        in_specs=(
            nodes,
            P(),
            P(),
            P(ROW, COL, None, None, None),
            P(ROW, COL, None),
            P(ROW, COL, None),
            P(ROW, COL),
            nodes,
        ),
        out_specs=(nodes, nodes, P()),
        check_vma=False,
    )
```

time: 963 us -> 357 us (0.37)
  waiting for transfers between devices: 675 us -> 118 us
  starting transfers between devices: 0.21 us -> 171 us
  other arithmetic: 133 us -> 10.7 us
  local copies, waits for them, and re-layouts: 72.2 us -> 5.82 us
  matrix products: 54.5 us -> 0 us
  Pallas kernels: 0 us -> 45.7 us
  between operations: 17.3 us -> 2.37 us
    reduce_scatter x2 -> x0, waiting for transfers between devices: 430 us -> none  [the longest x1 231 us: on_device(): lax.psum_scatter(partial_value, 'col', scatter_dimension=0, tiled=True)]
    ppermute x0 -> x88, starting transfers between devices: none -> 171 us  [shift(): return lax.ppermute(value, axes, perm)]
    psum x1 -> x0, waiting for transfers between devices: 142 us -> none  [on_device(): grad_weight = lax.psum(weight_term, ('row', 'col'))]
    ppermute x0 -> x88, waiting for transfers between devices: none -> 118 us  [shift(): return lax.ppermute(value, axes, perm)]
    scatter-add x12 -> x0, other arithmetic: 118 us -> none  [the longest x6 60.2 us: apply_group(): return running.at[group_rows].add(products)]
    all_gather x2 -> x0, waiting for transfers between devices: 103 us -> none  [the longest x1 52.9 us: on_device(): grad_group = lax.all_gather(grad_pre, 'col', axis=0, tiled=True)]
    dot_general x15 -> x0, matrix products: 54.5 us -> none  [the longest x6 24.3 us: apply_group(): jnp.einsum('tij,tif->tjf', group_values, selected, preferred_element_type...]
    pallas_call x0 -> x6, Pallas kernels: none -> 45.7 us  [the longest x4 35.5 us: sweep(): pl.pallas_call(functools.partial(sweep_kernel, pieces, len(out_shapes), t...]
  transfers between devices with their start and end apart: 5 -> 88, of which waited for: 5 -> 34; matrix products, arithmetic and copies ran while one was open for 2% -> 4% of each run, Pallas kernels for 0% -> 10%
where the time goes in v1:
time: 357 us; the launch traced here: 354 us
  starting transfers between devices  171 us (48%)
  waiting for transfers between devices  118 us (33%)
  Pallas kernels  45.7 us (13%)
  other arithmetic  10.7 us (3%)
  local copies, waits for them, and re-layouts  5.82 us (2%)
    ppermute x88, starting transfers between devices, shift(): return lax.ppermute(value, axes, perm)  171 us
    ppermute x88, waiting for transfers between devices, shift(): return lax.ppermute(value, axes, perm)  118 us
    pallas_call x4, Pallas kernels, sweep(): pl.pallas_call(functools.partial(sweep_kernel, pieces, len(out_shapes), t...  35.5 us
  transfers between devices with their start and end apart: 88, of which 34 were waited for; matrix products, arithmetic and copies ran while one was open for 4% of the time, Pallas kernels for 10%

profile of v1, /device:TPU:1, one launch (start us, length us, event | category | flops | bytes accessed | tf_op | source)
XLA Modules:
  0.0 353.6 jit_solution(1211959010165640307)
XLA Ops:
  1.7 3.6 %collective-permute-start.22 = (bf16[1024,128]{1,0:T(8,128)(2,1)S(1)}, bf16[1024,128]{1,0:T(8,128)(2,1)S(1)}, u32[]{:S(2)}, u32[]{:S(2)}) collective-permute-start(bf16[1024,128]{1,0:T(8,128)(2,1)S(1)} %get-tuple-element.99.refs_4_), channel_id=1, source_target_pairs={{16,0},{32,16},{48,32},{0,48},{80,64},{96,80},{112,96},{64,112},{1... | collective-permute-start | bytes 786440 | tf_op jit(solution)/shard_map/ppermute | solution.py:226
  9.7 5.0 %collective-permute-done.22.refs_5_ = bf16[1024,128]{1,0:T(8,128)(2,1)S(1)} collective-permute-done((bf16[1024,128]{1,0:T(8,128)(2,1)S(1)}, bf16[1024,128]{1,0:T(8,128)(2,1)S(1)}, u32[]{:S(2)}, u32[]{:S(2)}) %collective-permute-start.22) | collective-permute-done | bytes 262176 | tf_op jit(solution)/shard_map/ppermute | solution.py:226
  14.7 5.4 %collective-permute-start.28 = (bf16[1024,128]{1,0:T(8,128)(2,1)S(1)}, bf16[1024,128]{1,0:T(8,128)(2,1)}, u32[]{:S(2)}, u32[]{:S(2)}) collective-permute-start(bf16[1024,128]{1,0:T(8,128)(2,1)S(1)} %get-tuple-element.99.refs_4_), channel_id=1, source_target_pairs={{112,0},{64,16},{80,32},{96,48},{48,64},{0,80},{16,96},{32,112},{1... | collective-permute-start | bytes 786440 | tf_op jit(solution)/shard_map/ppermute | solution.py:226
  27.1 6.9 %collective-permute-start.4 = (bf16[1024,128]{1,0:T(8,128)(2,1)S(1)}, bf16[1024,128]{1,0:T(8,128)(2,1)S(1)}, u32[]{:S(2)}, u32[]{:S(2)}) collective-permute-start(bf16[1024,128]{1,0:T(8,128)(2,1)S(1)} %get-tuple-element.100.refs_4_), channel_id=1, source_target_pairs={{80,0},{96,16},{112,32},{64,48},{16,64},{32,80},{48,96},{0,112},{8... | collective-permute-start | bytes 786440 | tf_op jit(solution)/shard_map/ppermute | solution.py:226
  34.8 4.7 %collective-permute-start.5 = (bf16[1024,128]{1,0:T(8,128)(2,1)S(1)}, bf16[1024,128]{1,0:T(8,128)(2,1)S(1)}, u32[]{:S(2)}, u32[]{:S(2)}) collective-permute-start(bf16[1024,128]{1,0:T(8,128)(2,1)S(1)} %get-tuple-element.100.refs_4_), channel_id=1, source_target_pairs={{96,0},{112,16},{64,32},{80,48},{32,64},{48,80},{0,96},{16,112},{9... | collective-permute-start | bytes 786440 | tf_op jit(solution)/shard_map/ppermute | solution.py:226
  41.4 15.8 %collective-permute-done.3.refs_8_ = bf16[1024,128]{1,0:T(8,128)(2,1)S(1)} collective-permute-done((bf16[1024,128]{1,0:T(8,128)(2,1)S(1)}, bf16[1024,128]{1,0:T(8,128)(2,1)S(1)}, u32[]{:S(2)}, u32[]{:S(2)}) %collective-permute-start.3) | collective-permute-done | bytes 262176 | tf_op jit(solution)/shard_map/ppermute | solution.py:226
  61.0 5.0 %collective-permute-done.1.refs_6_ = bf16[1024,128]{1,0:T(8,128)(2,1)S(1)} collective-permute-done((bf16[1024,128]{1,0:T(8,128)(2,1)S(1)}, bf16[1024,128]{1,0:T(8,128)(2,1)S(1)}, u32[]{:S(2)}, u32[]{:S(2)}) %collective-permute-start.1) | collective-permute-done | bytes 262176 | tf_op jit(solution)/shard_map/ppermute | solution.py:226
  73.5 6.5 %forward_1.1 = (bf16[1024,128]{1,0:T(8,128)(2,1)}, bf16[1024,128]{1,0:T(8,128)(2,1)}, bf16[1024,128]{1,0:T(8,128)(2,1)}, bf16[1024,128]{1,0:T(8,128)(2,1)}, bf16...) custom-call(s32[1]{0:T(128)} %bitcast.13.refs_0_, ...), custom_call_target="tpu_custom_call" | custom-call | flops 536870912 | bytes 18874368 | tf_op jit(solution)/shard_map/forward_1/pallas_call | solution.py:96
  81.6 4.3 %collective-permute-start.38 = (bf16[1024,128]{1,0:T(8,128)(2,1)}, bf16[1024,128]{1,0:T(8,128)(2,1)S(1)}, u32[]{:S(2)}, u32[]{:S(2)}) collective-permute-start(bf16[1024,128]{1,0:T(8,128)(2,1)} %get-tuple-element.51), channel_id=1, source_target_pairs={{2,0},{3,1},{0,2},{1,3},{6,4},{7,5},{4,6},{5,7},{10,8},{11,9},{8,1... | collective-permute-start | bytes 786440 | tf_op jit(solution)/shard_map/ppermute | solution.py:226
  85.9 8.1 %collective-permute-start.40 = (bf16[1024,128]{1,0:T(8,128)(2,1)}, bf16[1024,128]{1,0:T(8,128)(2,1)S(1)}, u32[]{:S(2)}, u32[]{:S(2)}) collective-permute-start(bf16[1024,128]{1,0:T(8,128)(2,1)} %get-tuple-element.53), channel_id=1, source_target_pairs={{4,0},{5,1},{6,2},{7,3},{0,4},{1,5},{2,6},{3,7},{12,8},{13,9},{14,... | collective-permute-start | bytes 786440 | tf_op jit(solution)/shard_map/ppermute | solution.py:226
  94.8 6.5 %forward_0.1 = (bf16[1024,128]{1,0:T(8,128)(2,1)}, bf16[1024,128]{1,0:T(8,128)(2,1)}, bf16[1024,128]{1,0:T(8,128)(2,1)}, bf16[1024,128]{1,0:T(8,128)(2,1)}, bf16...) custom-call(s32[1]{0:T(128)} %bitcast.12.refs_0_, ...), custom_call_target="tpu_custom_call" | custom-call | flops 536870912 | bytes 18874368 | tf_op jit(solution)/shard_map/forward_0/pallas_call | solution.py:96
  101.4 9.4 %collective-permute-start.42 = (bf16[1024,128]{1,0:T(8,128)(2,1)S(1)}, bf16[1024,128]{1,0:T(8,128)(2,1)S(1)}, u32[]{:S(2)}, u32[]{:S(2)}) collective-permute-start(bf16[1024,128]{1,0:T(8,128)(2,1)S(1)} %copy-done.72), channel_id=1, source_target_pairs={{6,0},{7,1},{4,2},{5,3},{2,4},{3,5},{0,6},{1,7},{14,8},{15,9},{12,... | collective-permute-start | bytes 786440 | tf_op jit(solution)/shard_map/ppermute | solution.py:226
  114.7 2.8 collective-permute-start.18
  117.5 3.8 %collective-permute-done.43.refs_15_ = bf16[1024,128]{1,0:T(8,128)(2,1)S(1)} collective-permute-done((bf16[1024,128]{1,0:T(8,128)(2,1)S(1)}, bf16[1024,128]{1,0:T(8,128)(2,1)S(1)}, u32[]{:S(2)}, u32[]{:S(2)}) %collective-permute-start.43) | collective-permute-done | bytes 262176 | tf_op jit(solution)/shard_map/ppermute | solution.py:226
  122.9 4.6 %collective-permute-start.20 = (bf16[1024,128]{1,0:T(8,128)(2,1)}, bf16[1024,128]{1,0:T(8,128)(2,1)S(1)}, u32[]{:S(2)}, u32[]{:S(2)}) collective-permute-start(bf16[1024,128]{1,0:T(8,128)(2,1)} %get-tuple-element.47), channel_id=1, source_target_pairs={{6,0},{7,1},{4,2},{5,3},{2,4},{3,5},{0,6},{1,7},{14,8},{15,9},{12,... | collective-permute-start | bytes 786440 | tf_op jit(solution)/shard_map/ppermute | solution.py:226
  127.5 2.7 collective-permute-start.21
  130.2 2.5 collective-permute-done.19.refs_5_
  132.7 7.0 %collective-permute-done.20.refs_6_ = bf16[1024,128]{1,0:T(8,128)(2,1)S(1)} collective-permute-done((bf16[1024,128]{1,0:T(8,128)(2,1)}, bf16[1024,128]{1,0:T(8,128)(2,1)S(1)}, u32[]{:S(2)}, u32[]{:S(2)}) %collective-permute-start.20) | collective-permute-done | bytes 262176 | tf_op jit(solution)/shard_map/ppermute | solution.py:226
  139.6 6.6 %collective-permute-done.21.refs_7_ = bf16[1024,128]{1,0:T(8,128)(2,1)S(1)} collective-permute-done((bf16[1024,128]{1,0:T(8,128)(2,1)}, bf16[1024,128]{1,0:T(8,128)(2,1)S(1)}, u32[]{:S(2)}, u32[]{:S(2)}) %collective-permute-start.21) | collective-permute-done | bytes 262176 | tf_op jit(solution)/shard_map/ppermute | solution.py:226
  147.0 5.8 %middle.1 = (bf16[1024,256]{1,0:T(8,128)(2,1)}, bf16[1024,128]{1,0:T(8,128)(2,1)}, bf16[1024,128]{1,0:T(8,128)(2,1)}, f32[256,256]{1,0:T(8,128)}) custom-call(bf16[1024,128]{1,0:T(8,128)(2,1)} %get-tuple-element.41.refs_0_, bf16[1024,128]{1,0:T(8,128)(2,1)} %copy-done.63, bf16[1024,128]{1,0:T(8,128)(2,1)} %copy-done.64, bf16[1024,128]{1,0:T(8,128)(2,1)} %copy-done.65, ...), custom_call_target="tpu_custom_call" | custom-call | tf_op jit(solution)/shard_map/middle/pallas_call | solution.py:173
  154.9 4.7 %collective-permute-start.62 = (bf16[1024,128]{1,0:T(8,128)(2,1)}, bf16[1024,128]{1,0:T(8,128)(2,1)S(1)}, u32[]{:S(2)}, u32[]{:S(2)}) collective-permute-start(bf16[1024,128]{1,0:T(8,128)(2,1)} %get-tuple-element.68.refs_4_), channel_id=1, source_target_pairs={{4,0},{5,1},{6,2},{7,3},{0,4},{1,5},{2,6},{3,7},{12,8},{13,9},{14,... | collective-permute-start | bytes 786440 | tf_op jit(solution)/shard_map/ppermute | solution.py:226
  161.3 4.6 %collective-permute-start.64 = (bf16[1024,128]{1,0:T(8,128)(2,1)}, bf16[1024,128]{1,0:T(8,128)(2,1)S(1)}, u32[]{:S(2)}, u32[]{:S(2)}) collective-permute-start(bf16[1024,128]{1,0:T(8,128)(2,1)} %get-tuple-element.68.refs_4_), channel_id=1, source_target_pairs={{6,0},{7,1},{4,2},{5,3},{2,4},{3,5},{0,6},{1,7},{14,8},{15,9},{12,... | collective-permute-start | bytes 786440 | tf_op jit(solution)/shard_map/ppermute | solution.py:226
  165.9 5.1 %collective-permute-start.65 = (bf16[1024,128]{1,0:T(8,128)(2,1)}, bf16[1024,128]{1,0:T(8,128)(2,1)S(1)}, u32[]{:S(2)}, u32[]{:S(2)}) collective-permute-start(bf16[1024,128]{1,0:T(8,128)(2,1)} %get-tuple-element.68.refs_4_), channel_id=1, source_target_pairs={{7,0},{4,1},{5,2},{6,3},{3,4},{0,5},{1,6},{2,7},{15,8},{12,9},{13,... | collective-permute-start | bytes 786440 | tf_op jit(solution)/shard_map/ppermute | solution.py:226
  171.8 3.7 %collective-permute-start.46 = (bf16[1024,128]{1,0:T(8,128)(2,1)}, bf16[1024,128]{1,0:T(8,128)(2,1)S(1)}, u32[]{:S(2)}, u32[]{:S(2)}) collective-permute-start(bf16[1024,128]{1,0:T(8,128)(2,1)} %get-tuple-element.58.refs_4_), channel_id=1, source_target_pairs={{3,0},{0,1},{1,2},{2,3},{7,4},{4,5},{5,6},{6,7},{11,8},{8,9},{9,10... | collective-permute-start | bytes 786440 | tf_op jit(solution)/shard_map/ppermute | solution.py:226
  176.2 2.3 collective-permute-start.47
  178.5 4.6 %collective-permute-done.65.refs_11_ = bf16[1024,128]{1,0:T(8,128)(2,1)S(1)} collective-permute-done((bf16[1024,128]{1,0:T(8,128)(2,1)}, bf16[1024,128]{1,0:T(8,128)(2,1)S(1)}, u32[]{:S(2)}, u32[]{:S(2)}) %collective-permute-start.65) | collective-permute-done | bytes 262176 | tf_op jit(solution)/shard_map/ppermute | solution.py:226
  183.9 7.3 %backward_1.1 = (f32[1024,128]{1,0:T(8,128)}, f32[1024,128]{1,0:T(8,128)}, f32[1024,128]{1,0:T(8,128)}, f32[1024,128]{1,0:T(8,128)}, f32[1024,128]{1,0:T(8,128)}...) custom-call(s32[1]{0:T(128)} %bitcast.15.refs_0_, ...), custom_call_target="tpu_custom_call" | custom-call | flops 536870912 | bytes 18874368 | tf_op jit(solution)/shard_map/backward_1/pallas_call | solution.py:96
  192.5 5.8 %collective-permute-start.48 = (bf16[1024,128]{1,0:T(8,128)(2,1)S(1)}, bf16[1024,128]{1,0:T(8,128)(2,1)}, u32[]{:S(2)}, u32[]{:S(2)}) collective-permute-start(bf16[1024,128]{1,0:T(8,128)(2,1)S(1)} %copy-done.18), channel_id=1, source_target_pairs={{5,0},{6,1},{7,2},{4,3},{1,4},{2,5},{3,6},{0,7},{13,8},{14,9},{15,... | collective-permute-start | bytes 786440 | tf_op jit(solution)/shard_map/ppermute | solution.py:226
  198.3 13.6 %collective-permute-start.49 = (bf16[1024,128]{1,0:T(8,128)(2,1)S(1)}, bf16[1024,128]{1,0:T(8,128)(2,1)}, u32[]{:S(2)}, u32[]{:S(2)}) collective-permute-start(bf16[1024,128]{1,0:T(8,128)(2,1)S(1)} %copy-done.18), channel_id=1, source_target_pairs={{6,0},{7,1},{4,2},{5,3},{2,4},{3,5},{0,6},{1,7},{14,8},{15,9},{12,... | collective-permute-start | bytes 786440 | tf_op jit(solution)/shard_map/ppermute | solution.py:226
  213.7 4.8 %collective-permute-done.49.refs_10_ = bf16[1024,128]{1,0:T(8,128)(2,1)} collective-permute-done((bf16[1024,128]{1,0:T(8,128)(2,1)S(1)}, bf16[1024,128]{1,0:T(8,128)(2,1)}, u32[]{:S(2)}, u32[]{:S(2)}) %collective-permute-start.49) | collective-permute-done | bytes 262176 | tf_op jit(solution)/shard_map/ppermute | solution.py:226
  218.5 5.5 %collective-permute-done.50.refs_11_ = bf16[1024,128]{1,0:T(8,128)(2,1)} collective-permute-done((bf16[1024,128]{1,0:T(8,128)(2,1)S(1)}, bf16[1024,128]{1,0:T(8,128)(2,1)}, u32[]{:S(2)}, u32[]{:S(2)}) %collective-permute-start.50) | collective-permute-done | bytes 262176 | tf_op jit(solution)/shard_map/ppermute | solution.py:226
  224.0 15.1 %backward_0.1 = (f32[1024,128]{1,0:T(8,128)}, f32[1024,128]{1,0:T(8,128)}, f32[1024,128]{1,0:T(8,128)}, f32[1024,128]{1,0:T(8,128)}, f32[1024,128]{1,0:T(8,128)}...) custom-call(s32[1]{0:T(128)} %bitcast.14.refs_0_, ...), custom_call_target="tpu_custom_call" | custom-call | flops 536870912 | bytes 18874368 | tf_op jit(solution)/shard_map/backward_0/pallas_call | solution.py:96
  240.8 12.6 %collective-permute-start.75 = (f32[32,256]{1,0:T(8,128)S(1)}, f32[32,256]{1,0:T(8,128)S(1)}, u32[]{:S(2)}, u32[]{:S(2)}) collective-permute-start(f32[32,256]{1,0:T(8,128)S(1)} %get-tuple-element.101), channel_id=1, source_target_pairs={{3,0},{0,1},{1,2},{2,3},{7,4},{4,5},{5,6},{6,7},{11,8},{8,9},{9,10... | collective-permute-start | bytes 98312 | tf_op jit(solution)/shard_map/ppermute | solution.py:226
  253.4 2.5 collective-permute-start.77
  262.9 3.8 %collective-permute-start.81 = (f32[32,256]{1,0:T(8,128)S(1)}, f32[32,256]{1,0:T(8,128)S(1)}, u32[]{:S(2)}, u32[]{:S(2)}) collective-permute-start(f32[32,256]{1,0:T(8,128)S(1)} %add_add_fusion.1), channel_id=1, source_target_pairs={{4,0},{0,4},{68,64},{64,68},{5,1},{1,5},{69,65},{65,69},{6,2},{2,6... | collective-permute-start | bytes 98312 | tf_op jit(solution)/shard_map/ppermute | solution.py:226
  270.7 2.3 collective-permute-done.83
  276.3 3.3 collective-permute-done.85
  280.3 6.4 %collective-permute-start.87 = (f32[128,256]{1,0:T(8,128)S(1)}, f32[128,256]{1,0:T(8,128)S(1)}, u32[]{:S(2)}, u32[]{:S(2)}) collective-permute-start(f32[128,256]{1,0:T(8,128)S(1)} %bitcast_select_fusion), channel_id=1, source_target_pairs={{8,0},{0,8},{9,1},{1,9},{10,2},{2,10},{11,3},{3,11},{12,4},{4,12},... | collective-permute-start | bytes 393224 | tf_op jit(solution)/shard_map/ppermute | solution.py:226
  286.8 3.2 add_convert_fusion
  292.7 2.7 add_convert_fusion.8
  297.2 7.5 %collective-permute-done.67.refs_9_ = bf16[1024,128]{1,0:T(8,128)(2,1)S(1)} collective-permute-done((bf16[1024,128]{1,0:T(8,128)(2,1)S(1)}, bf16[1024,128]{1,0:T(8,128)(2,1)S(1)}, u32[]{:S(2)}, u32[]{:S(2)}) %collective-permute-start.67) | collective-permute-done | bytes 262176 | tf_op jit(solution)/shard_map/ppermute | solution.py:226
  305.6 4.4 %collective-permute-start.53 = (bf16[1024,128]{1,0:T(8,128)(2,1)S(1)}, bf16[1024,128]{1,0:T(8,128)(2,1)S(1)}, u32[]{:S(2)}, u32[]{:S(2)}) collective-permute-start(bf16[1024,128]{1,0:T(8,128)(2,1)S(1)} %get-tuple-element.96), channel_id=1, source_target_pairs={{32,0},{48,16},{0,32},{16,48},{96,64},{112,80},{64,96},{80,112},{3... | collective-permute-start | bytes 786440 | tf_op jit(solution)/shard_map/ppermute | solution.py:226
  311.1 5.4 %collective-permute-start.54 = (bf16[1024,128]{1,0:T(8,128)(2,1)S(1)}, bf16[1024,128]{1,0:T(8,128)(2,1)}, u32[]{:S(2)}, u32[]{:S(2)}) collective-permute-start(bf16[1024,128]{1,0:T(8,128)(2,1)S(1)} %get-tuple-element.95), channel_id=1, source_target_pairs={{16,0},{32,16},{48,32},{0,48},{80,64},{96,80},{112,96},{64,112},{1... | collective-permute-start | bytes 786440 | tf_op jit(solution)/shard_map/ppermute | solution.py:226
  316.5 3.0 collective-permute-done.72.refs_14_
  320.8 7.7 %collective-permute-done.52.refs_1_ = bf16[1024,128]{1,0:T(8,128)(2,1)S(1)} collective-permute-done((bf16[1024,128]{1,0:T(8,128)(2,1)S(1)}, bf16[1024,128]{1,0:T(8,128)(2,1)S(1)}, u32[]{:S(2)}, u32[]{:S(2)}) %collective-permute-start.52) | collective-permute-done | bytes 262176 | tf_op jit(solution)/shard_map/ppermute | solution.py:226
  333.3 9.6 %collective-permute-done.56.refs_5_ = bf16[1024,128]{1,0:T(8,128)(2,1)} collective-permute-done((bf16[1024,128]{1,0:T(8,128)(2,1)S(1)}, bf16[1024,128]{1,0:T(8,128)(2,1)}, u32[]{:S(2)}, u32[]{:S(2)}) %collective-permute-start.56) | collective-permute-done | bytes 262176 | tf_op jit(solution)/shard_map/ppermute | solution.py:226
  342.9 6.0 %collective-permute-done.57.refs_6_ = bf16[1024,128]{1,0:T(8,128)(2,1)} collective-permute-done((bf16[1024,128]{1,0:T(8,128)(2,1)S(1)}, bf16[1024,128]{1,0:T(8,128)(2,1)}, u32[]{:S(2)}, u32[]{:S(2)}) %collective-permute-start.57) | collective-permute-done | bytes 262176 | tf_op jit(solution)/shard_map/ppermute | solution.py:226
  349.0 4.5 %final.1 = bf16[1024,256]{1,0:T(8,128)(2,1)} custom-call(bf16[1024,128]{1,0:T(8,128)(2,1)} %get-tuple-element.98.refs_0_, bf16[1024,128]{1,0:T(8,128)(2,1)} %copy-done.53, bf16[1024,128]{1,0:T(8,128)(2,1)} %copy-done.54, bf16[1024,128]{1,0:T(8,128)(2,1)} %collective-permute-done.54.refs_3_, bf16[1024,128]{1,0:T(8,128)(2,1)} %collective-permute-done.55.refs_4_, ...), custom_call_target="tpu_custom_call" | custom-call | tf_op jit(solution)/shard_map/final/pallas_call | solution.py:200
  (301 shorter events, 72.1 us)
Async XLA Ops:
  5.7 16.3 %collective-permute-start.24 = (bf16[1024,128]{1,0:T(8,128)(2,1)S(1)}, bf16[1024,128]{1,0:T(8,128)(2,1)S(1)}, u32[]{:S(2)}, u32[]{:S(2)}) collective-permute-start(bf16[1024,128]{1,0:T(8,128)(2,1)S(1)} %get-tuple-element.99.refs_4_), channel_id=1, source_target_pairs={{48,0},{0,16},{16,32},{32,48},{112,64},{64,80},{80,96},{96,112},{4... | collective-permute-start | bytes 786440 | tf_op jit(solution)/shard_map/ppermute | solution.py:226
  6.4 17.7 %collective-permute-start.25 = (bf16[1024,128]{1,0:T(8,128)(2,1)S(1)}, bf16[1024,128]{1,0:T(8,128)(2,1)S(1)}, u32[]{:S(2)}, u32[]{:S(2)}) collective-permute-start(bf16[1024,128]{1,0:T(8,128)(2,1)S(1)} %get-tuple-element.99.refs_4_), channel_id=1, source_target_pairs={{64,0},{80,16},{96,32},{112,48},{0,64},{16,80},{32,96},{48,112},{6... | collective-permute-start | bytes 786440 | tf_op jit(solution)/shard_map/ppermute | solution.py:226
  8.0 16.4 %collective-permute-start.26 = (bf16[1024,128]{1,0:T(8,128)(2,1)S(1)}, bf16[1024,128]{1,0:T(8,128)(2,1)S(1)}, u32[]{:S(2)}, u32[]{:S(2)}) collective-permute-start(bf16[1024,128]{1,0:T(8,128)(2,1)S(1)} %get-tuple-element.99.refs_4_), channel_id=1, source_target_pairs={{80,0},{96,16},{112,32},{64,48},{16,64},{32,80},{48,96},{0,112},{8... | collective-permute-start | bytes 786440 | tf_op jit(solution)/shard_map/ppermute | solution.py:226
  14.7 20.0 %collective-permute-start.28 = (bf16[1024,128]{1,0:T(8,128)(2,1)S(1)}, bf16[1024,128]{1,0:T(8,128)(2,1)}, u32[]{:S(2)}, u32[]{:S(2)}) collective-permute-start(bf16[1024,128]{1,0:T(8,128)(2,1)S(1)} %get-tuple-element.99.refs_4_), channel_id=1, source_target_pairs={{112,0},{64,16},{80,32},{96,48},{48,64},{0,80},{16,96},{32,112},{1... | collective-permute-start | bytes 786440 | tf_op jit(solution)/shard_map/ppermute | solution.py:226
  22.0 17.4 %collective-permute-start.29 = (bf16[1024,128]{1,0:T(8,128)(2,1)S(1)}, bf16[1024,128]{1,0:T(8,128)(2,1)}, u32[]{:S(2)}, u32[]{:S(2)}) collective-permute-start(bf16[1024,128]{1,0:T(8,128)(2,1)S(1)} %get-tuple-element.99.refs_4_), channel_id=1, source_target_pairs={{8,0},{0,8},{9,1},{1,9},{10,2},{2,10},{11,3},{3,11},{12,4},{4,12},... | collective-permute-start | bytes 786440 | tf_op jit(solution)/shard_map/ppermute | solution.py:226
  24.1 15.3 %collective-permute-start.2 = (bf16[1024,128]{1,0:T(8,128)(2,1)S(1)}, bf16[1024,128]{1,0:T(8,128)(2,1)S(1)}, u32[]{:S(2)}, u32[]{:S(2)}) collective-permute-start(bf16[1024,128]{1,0:T(8,128)(2,1)S(1)} %get-tuple-element.100.refs_4_), channel_id=1, source_target_pairs={{48,0},{0,16},{16,32},{32,48},{112,64},{64,80},{80,96},{96,112},{4... | collective-permute-start | bytes 786440 | tf_op jit(solution)/shard_map/ppermute | solution.py:226
  24.4 32.8 %collective-permute-start.3 = (bf16[1024,128]{1,0:T(8,128)(2,1)S(1)}, bf16[1024,128]{1,0:T(8,128)(2,1)S(1)}, u32[]{:S(2)}, u32[]{:S(2)}) collective-permute-start(bf16[1024,128]{1,0:T(8,128)(2,1)S(1)} %get-tuple-element.100.refs_4_), channel_id=1, source_target_pairs={{64,0},{80,16},{96,32},{112,48},{0,64},{16,80},{32,96},{48,112},{6... | collective-permute-start | bytes 786440 | tf_op jit(solution)/shard_map/ppermute | solution.py:226
  27.1 32.2 %collective-permute-start.4 = (bf16[1024,128]{1,0:T(8,128)(2,1)S(1)}, bf16[1024,128]{1,0:T(8,128)(2,1)S(1)}, u32[]{:S(2)}, u32[]{:S(2)}) collective-permute-start(bf16[1024,128]{1,0:T(8,128)(2,1)S(1)} %get-tuple-element.100.refs_4_), channel_id=1, source_target_pairs={{80,0},{96,16},{112,32},{64,48},{16,64},{32,80},{48,96},{0,112},{8... | collective-permute-start | bytes 786440 | tf_op jit(solution)/shard_map/ppermute | solution.py:226
  34.8 25.7 %collective-permute-start.5 = (bf16[1024,128]{1,0:T(8,128)(2,1)S(1)}, bf16[1024,128]{1,0:T(8,128)(2,1)S(1)}, u32[]{:S(2)}, u32[]{:S(2)}) collective-permute-start(bf16[1024,128]{1,0:T(8,128)(2,1)S(1)} %get-tuple-element.100.refs_4_), channel_id=1, source_target_pairs={{96,0},{112,16},{64,32},{80,48},{32,64},{48,80},{0,96},{16,112},{9... | collective-permute-start | bytes 786440 | tf_op jit(solution)/shard_map/ppermute | solution.py:226
  39.4 21.1 %collective-permute-start.6 = (bf16[1024,128]{1,0:T(8,128)(2,1)S(1)}, bf16[1024,128]{1,0:T(8,128)(2,1)S(1)}, u32[]{:S(2)}, u32[]{:S(2)}) collective-permute-start(bf16[1024,128]{1,0:T(8,128)(2,1)S(1)} %get-tuple-element.100.refs_4_), channel_id=1, source_target_pairs={{112,0},{64,16},{80,32},{96,48},{48,64},{0,80},{16,96},{32,112},{1... | collective-permute-start | bytes 786440 | tf_op jit(solution)/shard_map/ppermute | solution.py:226
  39.4 21.5 %collective-permute-start = (bf16[1024,128]{1,0:T(8,128)(2,1)S(1)}, bf16[1024,128]{1,0:T(8,128)(2,1)S(1)}, u32[]{:S(2)}, u32[]{:S(2)}) collective-permute-start(bf16[1024,128]{1,0:T(8,128)(2,1)S(1)} %get-tuple-element.100.refs_4_), channel_id=1, source_target_pairs={{16,0},{32,16},{48,32},{0,48},{80,64},{96,80},{112,96},{64,112},{1... | collective-permute-start | bytes 786440 | tf_op jit(solution)/shard_map/ppermute | solution.py:226
  73.1 21.0 %collective-permute-start.9 = (bf16[1024,128]{1,0:T(8,128)(2,1)}, bf16[1024,128]{1,0:T(8,128)(2,1)S(1)}, u32[]{:S(2)}, u32[]{:S(2)}) collective-permute-start(bf16[1024,128]{1,0:T(8,128)(2,1)} %copy-done.24), channel_id=1, source_target_pairs={{8,0},{0,8},{9,1},{1,9},{10,2},{2,10},{11,3},{3,11},{12,4},{4,12},... | collective-permute-start | bytes 786440 | tf_op jit(solution)/shard_map/ppermute | solution.py:226
  80.0 21.3 %collective-permute-start.37 = (bf16[1024,128]{1,0:T(8,128)(2,1)}, bf16[1024,128]{1,0:T(8,128)(2,1)S(1)}, u32[]{:S(2)}, u32[]{:S(2)}) collective-permute-start(bf16[1024,128]{1,0:T(8,128)(2,1)} %get-tuple-element.50), channel_id=1, source_target_pairs={{3,0},{0,1},{1,2},{2,3},{7,4},{4,5},{5,6},{6,7},{11,8},{8,9},{9,10... | collective-permute-start | bytes 786440 | tf_op jit(solution)/shard_map/ppermute | solution.py:226
  81.6 29.2 %collective-permute-start.38 = (bf16[1024,128]{1,0:T(8,128)(2,1)}, bf16[1024,128]{1,0:T(8,128)(2,1)S(1)}, u32[]{:S(2)}, u32[]{:S(2)}) collective-permute-start(bf16[1024,128]{1,0:T(8,128)(2,1)} %get-tuple-element.51), channel_id=1, source_target_pairs={{2,0},{3,1},{0,2},{1,3},{6,4},{7,5},{4,6},{5,7},{10,8},{11,9},{8,1... | collective-permute-start | bytes 786440 | tf_op jit(solution)/shard_map/ppermute | solution.py:226
  85.9 25.0 %collective-permute-start.39 = (bf16[1024,128]{1,0:T(8,128)(2,1)}, bf16[1024,128]{1,0:T(8,128)(2,1)S(1)}, u32[]{:S(2)}, u32[]{:S(2)}) collective-permute-start(bf16[1024,128]{1,0:T(8,128)(2,1)} %get-tuple-element.52), channel_id=1, source_target_pairs={{1,0},{2,1},{3,2},{0,3},{5,4},{6,5},{7,6},{4,7},{9,8},{10,9},{11,1... | collective-permute-start | bytes 786440 | tf_op jit(solution)/shard_map/ppermute | solution.py:226
  85.9 25.0 %collective-permute-start.40 = (bf16[1024,128]{1,0:T(8,128)(2,1)}, bf16[1024,128]{1,0:T(8,128)(2,1)S(1)}, u32[]{:S(2)}, u32[]{:S(2)}) collective-permute-start(bf16[1024,128]{1,0:T(8,128)(2,1)} %get-tuple-element.53), channel_id=1, source_target_pairs={{4,0},{5,1},{6,2},{7,3},{0,4},{1,5},{2,6},{3,7},{12,8},{13,9},{14,... | collective-permute-start | bytes 786440 | tf_op jit(solution)/shard_map/ppermute | solution.py:226
  94.1 18.3 %collective-permute-start.41 = (bf16[1024,128]{1,0:T(8,128)(2,1)}, bf16[1024,128]{1,0:T(8,128)(2,1)S(1)}, u32[]{:S(2)}, u32[]{:S(2)}) collective-permute-start(bf16[1024,128]{1,0:T(8,128)(2,1)} %get-tuple-element.54), channel_id=1, source_target_pairs={{7,0},{4,1},{5,2},{6,3},{3,4},{0,5},{1,6},{2,7},{15,8},{12,9},{13,... | collective-permute-start | bytes 786440 | tf_op jit(solution)/shard_map/ppermute | solution.py:226
  111.0 16.5 %collective-permute-start.16 = (bf16[1024,128]{1,0:T(8,128)(2,1)}, bf16[1024,128]{1,0:T(8,128)(2,1)S(1)}, u32[]{:S(2)}, u32[]{:S(2)}) collective-permute-start(bf16[1024,128]{1,0:T(8,128)(2,1)} %get-tuple-element.43), channel_id=1, source_target_pairs={{2,0},{3,1},{0,2},{1,3},{6,4},{7,5},{4,6},{5,7},{10,8},{11,9},{8,1... | collective-permute-start | bytes 786440 | tf_op jit(solution)/shard_map/ppermute | solution.py:226
  112.4 17.8 %collective-permute-start.17 = (bf16[1024,128]{1,0:T(8,128)(2,1)}, bf16[1024,128]{1,0:T(8,128)(2,1)S(1)}, u32[]{:S(2)}, u32[]{:S(2)}) collective-permute-start(bf16[1024,128]{1,0:T(8,128)(2,1)} %get-tuple-element.44), channel_id=1, source_target_pairs={{1,0},{2,1},{3,2},{0,3},{5,4},{6,5},{7,6},{4,7},{9,8},{10,9},{11,1... | collective-permute-start | bytes 786440 | tf_op jit(solution)/shard_map/ppermute | solution.py:226
  114.7 15.5 %collective-permute-start.18 = (bf16[1024,128]{1,0:T(8,128)(2,1)}, bf16[1024,128]{1,0:T(8,128)(2,1)S(1)}, u32[]{:S(2)}, u32[]{:S(2)}) collective-permute-start(bf16[1024,128]{1,0:T(8,128)(2,1)} %get-tuple-element.45), channel_id=1, source_target_pairs={{4,0},{5,1},{6,2},{7,3},{0,4},{1,5},{2,6},{3,7},{12,8},{13,9},{14,... | collective-permute-start | bytes 786440 | tf_op jit(solution)/shard_map/ppermute | solution.py:226
  122.9 16.7 %collective-permute-start.20 = (bf16[1024,128]{1,0:T(8,128)(2,1)}, bf16[1024,128]{1,0:T(8,128)(2,1)S(1)}, u32[]{:S(2)}, u32[]{:S(2)}) collective-permute-start(bf16[1024,128]{1,0:T(8,128)(2,1)} %get-tuple-element.47), channel_id=1, source_target_pairs={{6,0},{7,1},{4,2},{5,3},{2,4},{3,5},{0,6},{1,7},{14,8},{15,9},{12,... | collective-permute-start | bytes 786440 | tf_op jit(solution)/shard_map/ppermute | solution.py:226
  127.5 18.8 %collective-permute-start.21 = (bf16[1024,128]{1,0:T(8,128)(2,1)}, bf16[1024,128]{1,0:T(8,128)(2,1)S(1)}, u32[]{:S(2)}, u32[]{:S(2)}) collective-permute-start(bf16[1024,128]{1,0:T(8,128)(2,1)} %get-tuple-element.48), channel_id=1, source_target_pairs={{5,0},{6,1},{7,2},{4,3},{1,4},{2,5},{3,6},{0,7},{13,8},{14,9},{15,... | collective-permute-start | bytes 786440 | tf_op jit(solution)/shard_map/ppermute | solution.py:226
  154.3 16.7 %collective-permute-start.61 = (bf16[1024,128]{1,0:T(8,128)(2,1)}, bf16[1024,128]{1,0:T(8,128)(2,1)S(1)}, u32[]{:S(2)}, u32[]{:S(2)}) collective-permute-start(bf16[1024,128]{1,0:T(8,128)(2,1)} %get-tuple-element.68.refs_4_), channel_id=1, source_target_pairs={{3,0},{0,1},{1,2},{2,3},{7,4},{4,5},{5,6},{6,7},{11,8},{8,9},{9,10... | collective-permute-start | bytes 786440 | tf_op jit(solution)/shard_map/ppermute | solution.py:226
  154.9 16.0 %collective-permute-start.62 = (bf16[1024,128]{1,0:T(8,128)(2,1)}, bf16[1024,128]{1,0:T(8,128)(2,1)S(1)}, u32[]{:S(2)}, u32[]{:S(2)}) collective-permute-start(bf16[1024,128]{1,0:T(8,128)(2,1)} %get-tuple-element.68.refs_4_), channel_id=1, source_target_pairs={{4,0},{5,1},{6,2},{7,3},{0,4},{1,5},{2,6},{3,7},{12,8},{13,9},{14,... | collective-permute-start | bytes 786440 | tf_op jit(solution)/shard_map/ppermute | solution.py:226
  161.3 15.0 %collective-permute-start.64 = (bf16[1024,128]{1,0:T(8,128)(2,1)}, bf16[1024,128]{1,0:T(8,128)(2,1)S(1)}, u32[]{:S(2)}, u32[]{:S(2)}) collective-permute-start(bf16[1024,128]{1,0:T(8,128)(2,1)} %get-tuple-element.68.refs_4_), channel_id=1, source_target_pairs={{6,0},{7,1},{4,2},{5,3},{2,4},{3,5},{0,6},{1,7},{14,8},{15,9},{12,... | collective-permute-start | bytes 786440 | tf_op jit(solution)/shard_map/ppermute | solution.py:226
  165.9 17.3 %collective-permute-start.65 = (bf16[1024,128]{1,0:T(8,128)(2,1)}, bf16[1024,128]{1,0:T(8,128)(2,1)S(1)}, u32[]{:S(2)}, u32[]{:S(2)}) collective-permute-start(bf16[1024,128]{1,0:T(8,128)(2,1)} %get-tuple-element.68.refs_4_), channel_id=1, source_target_pairs={{7,0},{4,1},{5,2},{6,3},{3,4},{0,5},{1,6},{2,7},{15,8},{12,9},{13,... | collective-permute-start | bytes 786440 | tf_op jit(solution)/shard_map/ppermute | solution.py:226
  170.9 21.5 %collective-permute-start.44 = (bf16[1024,128]{1,0:T(8,128)(2,1)}, bf16[1024,128]{1,0:T(8,128)(2,1)S(1)}, u32[]{:S(2)}, u32[]{:S(2)}) collective-permute-start(bf16[1024,128]{1,0:T(8,128)(2,1)} %get-tuple-element.58.refs_4_), channel_id=1, source_target_pairs={{1,0},{2,1},{3,2},{0,3},{5,4},{6,5},{7,6},{4,7},{9,8},{10,9},{11,1... | collective-permute-start | bytes 786440 | tf_op jit(solution)/shard_map/ppermute | solution.py:226
  171.0 27.4 %collective-permute-start.45 = (bf16[1024,128]{1,0:T(8,128)(2,1)}, bf16[1024,128]{1,0:T(8,128)(2,1)S(1)}, u32[]{:S(2)}, u32[]{:S(2)}) collective-permute-start(bf16[1024,128]{1,0:T(8,128)(2,1)} %get-tuple-element.58.refs_4_), channel_id=1, source_target_pairs={{2,0},{3,1},{0,2},{1,3},{6,4},{7,5},{4,6},{5,7},{10,8},{11,9},{8,1... | collective-permute-start | bytes 786440 | tf_op jit(solution)/shard_map/ppermute | solution.py:226
  171.8 40.1 %collective-permute-start.46 = (bf16[1024,128]{1,0:T(8,128)(2,1)}, bf16[1024,128]{1,0:T(8,128)(2,1)S(1)}, u32[]{:S(2)}, u32[]{:S(2)}) collective-permute-start(bf16[1024,128]{1,0:T(8,128)(2,1)} %get-tuple-element.58.refs_4_), channel_id=1, source_target_pairs={{3,0},{0,1},{1,2},{2,3},{7,4},{4,5},{5,6},{6,7},{11,8},{8,9},{9,10... | collective-permute-start | bytes 786440 | tf_op jit(solution)/shard_map/ppermute | solution.py:226
  176.2 36.7 %collective-permute-start.47 = (bf16[1024,128]{1,0:T(8,128)(2,1)}, bf16[1024,128]{1,0:T(8,128)(2,1)S(1)}, u32[]{:S(2)}, u32[]{:S(2)}) collective-permute-start(bf16[1024,128]{1,0:T(8,128)(2,1)} %get-tuple-element.58.refs_4_), channel_id=1, source_target_pairs={{4,0},{5,1},{6,2},{7,3},{0,4},{1,5},{2,6},{3,7},{12,8},{13,9},{14,... | collective-permute-start | bytes 786440 | tf_op jit(solution)/shard_map/ppermute | solution.py:226
  191.3 95.4 %collective-permute-start.66 = (bf16[8192,128]{1,0:T(8,128)(2,1)}, bf16[8192,128]{1,0:T(8,128)(2,1)S(1)}, u32[]{:S(2)}, u32[]{:S(2)}) collective-permute-start(bf16[8192,128]{1,0:T(8,128)(2,1)} %get-tuple-element.70), channel_id=1, source_target_pairs={{8,0},{0,8},{9,1},{1,9},{10,2},{2,10},{11,3},{3,11},{12,4},{4,12},... | collective-permute-start | bytes 6291464 | tf_op jit(solution)/shard_map/ppermute | solution.py:226
  192.5 21.2 %collective-permute-start.48 = (bf16[1024,128]{1,0:T(8,128)(2,1)S(1)}, bf16[1024,128]{1,0:T(8,128)(2,1)}, u32[]{:S(2)}, u32[]{:S(2)}) collective-permute-start(bf16[1024,128]{1,0:T(8,128)(2,1)S(1)} %copy-done.18), channel_id=1, source_target_pairs={{5,0},{6,1},{7,2},{4,3},{1,4},{2,5},{3,6},{0,7},{13,8},{14,9},{15,... | collective-permute-start | bytes 786440 | tf_op jit(solution)/shard_map/ppermute | solution.py:226
  198.3 20.1 %collective-permute-start.49 = (bf16[1024,128]{1,0:T(8,128)(2,1)S(1)}, bf16[1024,128]{1,0:T(8,128)(2,1)}, u32[]{:S(2)}, u32[]{:S(2)}) collective-permute-start(bf16[1024,128]{1,0:T(8,128)(2,1)S(1)} %copy-done.18), channel_id=1, source_target_pairs={{6,0},{7,1},{4,2},{5,3},{2,4},{3,5},{0,6},{1,7},{14,8},{15,9},{12,... | collective-permute-start | bytes 786440 | tf_op jit(solution)/shard_map/ppermute | solution.py:226
  213.0 26.8 %collective-permute-start.74 = (f32[128,256]{1,0:T(8,128)S(1)}, f32[128,256]{1,0:T(8,128)}, u32[]{:S(2)}, u32[]{:S(2)}) collective-permute-start(f32[128,256]{1,0:T(8,128)S(1)} %constant_dynamic-slice_fusion.3), channel_id=1, source_target_pairs={{8,0},{0,8},{9,1},{1,9},{10,2},{2,10},{11,3},{3,11},{12,4},{4,12},... | collective-permute-start | bytes 393224 | tf_op jit(solution)/shard_map/ppermute | solution.py:226
  239.2 53.5 %collective-permute-start.51 = (bf16[8192,128]{1,0:T(8,128)(2,1)}, bf16[8192,128]{1,0:T(8,128)(2,1)}, u32[]{:S(2)}, u32[]{:S(2)}) collective-permute-start(bf16[8192,128]{1,0:T(8,128)(2,1)} %get-tuple-element.60), channel_id=1, source_target_pairs={{8,0},{0,8},{9,1},{1,9},{10,2},{2,10},{11,3},{3,11},{12,4},{4,12},... | collective-permute-start | bytes 6291464 | tf_op jit(solution)/shard_map/ppermute | solution.py:226
  240.8 15.1 %collective-permute-start.75 = (f32[32,256]{1,0:T(8,128)S(1)}, f32[32,256]{1,0:T(8,128)S(1)}, u32[]{:S(2)}, u32[]{:S(2)}) collective-permute-start(f32[32,256]{1,0:T(8,128)S(1)} %get-tuple-element.101), channel_id=1, source_target_pairs={{3,0},{0,1},{1,2},{2,3},{7,4},{4,5},{5,6},{6,7},{11,8},{8,9},{9,10... | collective-permute-start | bytes 98312 | tf_op jit(solution)/shard_map/ppermute | solution.py:226
  280.3 15.2 %collective-permute-start.87 = (f32[128,256]{1,0:T(8,128)S(1)}, f32[128,256]{1,0:T(8,128)S(1)}, u32[]{:S(2)}, u32[]{:S(2)}) collective-permute-start(f32[128,256]{1,0:T(8,128)S(1)} %bitcast_select_fusion), channel_id=1, source_target_pairs={{8,0},{0,8},{9,1},{1,9},{10,2},{2,10},{11,3},{3,11},{12,4},{4,12},... | collective-permute-start | bytes 393224 | tf_op jit(solution)/shard_map/ppermute | solution.py:226
  289.9 14.7 %collective-permute-start.67 = (bf16[1024,128]{1,0:T(8,128)(2,1)S(1)}, bf16[1024,128]{1,0:T(8,128)(2,1)S(1)}, u32[]{:S(2)}, u32[]{:S(2)}) collective-permute-start(bf16[1024,128]{1,0:T(8,128)(2,1)S(1)} %get-tuple-element.89), channel_id=1, source_target_pairs={{48,0},{0,16},{16,32},{32,48},{112,64},{64,80},{80,96},{96,112},{4... | collective-permute-start | bytes 786440 | tf_op jit(solution)/shard_map/ppermute | solution.py:226
  289.9 14.7 %collective-permute-start.68 = (bf16[1024,128]{1,0:T(8,128)(2,1)S(1)}, bf16[1024,128]{1,0:T(8,128)(2,1)S(1)}, u32[]{:S(2)}, u32[]{:S(2)}) collective-permute-start(bf16[1024,128]{1,0:T(8,128)(2,1)S(1)} %get-tuple-element.88), channel_id=1, source_target_pairs={{32,0},{48,16},{0,32},{16,48},{96,64},{112,80},{64,96},{80,112},{3... | collective-permute-start | bytes 786440 | tf_op jit(solution)/shard_map/ppermute | solution.py:226
  295.4 15.7 %collective-permute-start.71 = (bf16[1024,128]{1,0:T(8,128)(2,1)S(1)}, bf16[1024,128]{1,0:T(8,128)(2,1)S(1)}, u32[]{:S(2)}, u32[]{:S(2)}) collective-permute-start(bf16[1024,128]{1,0:T(8,128)(2,1)S(1)} %get-tuple-element.85), channel_id=1, source_target_pairs={{112,0},{64,16},{80,32},{96,48},{48,64},{0,80},{16,96},{32,112},{1... | collective-permute-start | bytes 786440 | tf_op jit(solution)/shard_map/ppermute | solution.py:226
  304.7 14.9 %collective-permute-start.72 = (bf16[1024,128]{1,0:T(8,128)(2,1)S(1)}, bf16[1024,128]{1,0:T(8,128)(2,1)S(1)}, u32[]{:S(2)}, u32[]{:S(2)}) collective-permute-start(bf16[1024,128]{1,0:T(8,128)(2,1)S(1)} %get-tuple-element.84), channel_id=1, source_target_pairs={{96,0},{112,16},{64,32},{80,48},{32,64},{48,80},{0,96},{16,112},{9... | collective-permute-start | bytes 786440 | tf_op jit(solution)/shard_map/ppermute | solution.py:226
  304.7 15.0 %collective-permute-start.73 = (bf16[1024,128]{1,0:T(8,128)(2,1)S(1)}, bf16[1024,128]{1,0:T(8,128)(2,1)S(1)}, u32[]{:S(2)}, u32[]{:S(2)}) collective-permute-start(bf16[1024,128]{1,0:T(8,128)(2,1)S(1)} %get-tuple-element.83), channel_id=1, source_target_pairs={{80,0},{96,16},{112,32},{64,48},{16,64},{32,80},{48,96},{0,112},{8... | collective-permute-start | bytes 786440 | tf_op jit(solution)/shard_map/ppermute | solution.py:226
  305.0 23.6 %collective-permute-start.52 = (bf16[1024,128]{1,0:T(8,128)(2,1)S(1)}, bf16[1024,128]{1,0:T(8,128)(2,1)S(1)}, u32[]{:S(2)}, u32[]{:S(2)}) collective-permute-start(bf16[1024,128]{1,0:T(8,128)(2,1)S(1)} %get-tuple-element.97), channel_id=1, source_target_pairs={{48,0},{0,16},{16,32},{32,48},{112,64},{64,80},{80,96},{96,112},{4... | collective-permute-start | bytes 786440 | tf_op jit(solution)/shard_map/ppermute | solution.py:226
  305.6 25.3 %collective-permute-start.53 = (bf16[1024,128]{1,0:T(8,128)(2,1)S(1)}, bf16[1024,128]{1,0:T(8,128)(2,1)S(1)}, u32[]{:S(2)}, u32[]{:S(2)}) collective-permute-start(bf16[1024,128]{1,0:T(8,128)(2,1)S(1)} %get-tuple-element.96), channel_id=1, source_target_pairs={{32,0},{48,16},{0,32},{16,48},{96,64},{112,80},{64,96},{80,112},{3... | collective-permute-start | bytes 786440 | tf_op jit(solution)/shard_map/ppermute | solution.py:226
  311.1 22.2 %collective-permute-start.54 = (bf16[1024,128]{1,0:T(8,128)(2,1)S(1)}, bf16[1024,128]{1,0:T(8,128)(2,1)}, u32[]{:S(2)}, u32[]{:S(2)}) collective-permute-start(bf16[1024,128]{1,0:T(8,128)(2,1)S(1)} %get-tuple-element.95), channel_id=1, source_target_pairs={{16,0},{32,16},{48,32},{0,48},{80,64},{96,80},{112,96},{64,112},{1... | collective-permute-start | bytes 786440 | tf_op jit(solution)/shard_map/ppermute | solution.py:226
  319.7 23.2 %collective-permute-start.56 = (bf16[1024,128]{1,0:T(8,128)(2,1)S(1)}, bf16[1024,128]{1,0:T(8,128)(2,1)}, u32[]{:S(2)}, u32[]{:S(2)}) collective-permute-start(bf16[1024,128]{1,0:T(8,128)(2,1)S(1)} %get-tuple-element.93), channel_id=1, source_target_pairs={{112,0},{64,16},{80,32},{96,48},{48,64},{0,80},{16,96},{32,112},{1... | collective-permute-start | bytes 786440 | tf_op jit(solution)/shard_map/ppermute | solution.py:226
  328.6 20.3 %collective-permute-start.57 = (bf16[1024,128]{1,0:T(8,128)(2,1)S(1)}, bf16[1024,128]{1,0:T(8,128)(2,1)}, u32[]{:S(2)}, u32[]{:S(2)}) collective-permute-start(bf16[1024,128]{1,0:T(8,128)(2,1)S(1)} %get-tuple-element.92), channel_id=1, source_target_pairs={{96,0},{112,16},{64,32},{80,48},{32,64},{48,80},{0,96},{16,112},{9... | collective-permute-start | bytes 786440 | tf_op jit(solution)/shard_map/ppermute | solution.py:226
  331.6 17.3 %collective-permute-start.58 = (bf16[1024,128]{1,0:T(8,128)(2,1)S(1)}, bf16[1024,128]{1,0:T(8,128)(2,1)}, u32[]{:S(2)}, u32[]{:S(2)}) collective-permute-start(bf16[1024,128]{1,0:T(8,128)(2,1)S(1)} %get-tuple-element.91), channel_id=1, source_target_pairs={{80,0},{96,16},{112,32},{64,48},{16,64},{32,80},{48,96},{0,112},{8... | collective-permute-start | bytes 786440 | tf_op jit(solution)/shard_map/ppermute | solution.py:226
  (113 other events, 1952.9 us)

commit v2 on v1

--- a/solution.py
+++ b/solution.py
@@ -18,7 +18,9 @@
 CHUNK = 32
 
 
-def sweep_kernel(pieces, outputs, transpose, batch, chunk, *refs):
+def sweep_kernel(plan, transpose, batch, chunk, *refs):
+    source_plan, result_plan, slab = plan
+    pieces, outputs = len(source_plan), len(result_plan)
     count, src, dst, tiles = refs[:4]
     sources = refs[4 : 4 + pieces]
     results = refs[4 + pieces : 4 + pieces + outputs]
@@ -26,28 +28,33 @@
     size = tile_buf.shape[1]
     live = count[0]
     chunks = (live + chunk - 1) // chunk
-    rows = sources[0].shape[0]
 
     def tile_copy(index):
         span = pl.ds(index * chunk, chunk)
         return pltpu.make_async_copy(tiles.at[span], tile_buf.at[span], tile_sems.at[index])
 
-    def source_copy(index):
-        return pltpu.make_async_copy(
-            sources[index], source_buf.at[pl.ds(index * rows, rows)], source_sem.at[index]
-        )
+    source_copies = []
+    for source, places in zip(sources, source_plan):
+        for offset, place, slabs, column in places:
+            source_copies.append(
+                pltpu.make_async_copy(
+                    source.at[pl.ds(offset * slab, slabs * slab)],
+                    source_buf.at[pl.ds(place * slab, slabs * slab), pl.ds(column, source.shape[1])],
+                    source_sem.at[len(source_copies)],
+                )
+            )
 
     def start_tiles(index, carry):
         tile_copy(index).start()
         return carry
 
     start_tiles(0, 0)
-    for index in range(pieces):
-        source_copy(index).start()
+    for copy in source_copies:
+        copy.start()
     lax.fori_loop(1, chunks, start_tiles, 0)
     total[...] = jnp.zeros_like(total)
-    for index in range(pieces):
-        source_copy(index).wait()
+    for copy in source_copies:
+        copy.wait()
 
     contract = (((0,), (0,)), ((), ())) if transpose else (((1,), (0,)), ((), ()))
 
@@ -77,44 +84,49 @@
         return lax.fori_loop(0, steps, on_batch, carry)
 
     lax.fori_loop(0, chunks, on_chunk, 0)
-    done = 0
-    for result in results:
-        length = result.shape[0]
-        result[...] = total[done : done + length, :].astype(result.dtype)
-        done += length
-
-
-def sweep(name, count, src, dst, tiles, sources, out_shapes, transpose):
+    for result, (slabs, column) in zip(results, result_plan):
+        for index, place in enumerate(slabs):
+            result[index * slab : (index + 1) * slab, :] = total[
+                place * slab : (place + 1) * slab, column : column + result.shape[1]
+            ].astype(result.dtype)
+
+
+def sweep(name, count, src, dst, tiles, sources, source_plan, result_plan, result_types, slab, width, transpose):
     slots, size, _ = tiles.shape
-    pieces = len(sources)
-    rows, width = sources[0].shape
-    out_rows = sum(s.shape[0] for s in out_shapes)
+    part_width = width // PARTS
+    source_slabs = max(p + n for places in source_plan for _, p, n, _ in places)
+    result_slabs = max(max(slabs) for slabs, _ in result_plan) + 1
+    copies = sum(len(places) for places in source_plan)
     chunk = min(CHUNK, slots)
     batch = min(BATCH, chunk)
     any_spec = pl.BlockSpec(memory_space=pl.ANY)
-    flops = 2 * (slots // 3) * size * size * width
+    out_shapes = [
+        jax.ShapeDtypeStruct((len(slabs) * slab, part_width), kind)
+        for (slabs, _), kind in zip(result_plan, result_types)
+    ]
+    moved, flops = 1024, 1024
     return pl.pallas_call(
-        functools.partial(sweep_kernel, pieces, len(out_shapes), transpose, batch, chunk),
+        functools.partial(sweep_kernel, (source_plan, result_plan, slab), transpose, batch, chunk),
         grid_spec=pltpu.PrefetchScalarGridSpec(
             num_scalar_prefetch=3,
             grid=(1,),
-            in_specs=[any_spec] * (1 + pieces),
+            in_specs=[any_spec] * (1 + len(sources)),
             out_specs=[
                 pl.BlockSpec(s.shape, lambda i, *_: (0, 0), pipeline_mode=pl.Buffered(1))
                 for s in out_shapes
             ],
             scratch_shapes=[
                 pltpu.VMEM(tiles.shape, BF16),
-                pltpu.VMEM((pieces * rows, width), BF16),
-                pltpu.VMEM((out_rows + size, width), F32),
+                pltpu.VMEM((source_slabs * slab, width), BF16),
+                pltpu.VMEM((result_slabs * slab + size, width), F32),
                 pltpu.SemaphoreType.DMA((slots // chunk,)),
-                pltpu.SemaphoreType.DMA((pieces,)),
+                pltpu.SemaphoreType.DMA((copies,)),
             ],
         ),
         out_shape=out_shapes,
         compiler_params=pltpu.CompilerParams(vmem_limit_bytes=VMEM_LIMIT),
         cost_estimate=pl.CostEstimate(
-            flops=flops, bytes_accessed=tiles.size * 2 + (pieces * rows + out_rows) * width * 2, transcendentals=0
+            flops=flops, bytes_accessed=moved, transcendentals=0
         ),
         name=name,
     )(count, src, dst, tiles, *sources)
@@ -192,7 +204,7 @@
 
 
 def final(pieces, weight, parts):
-    rows = pieces[0].shape[0]
+    rows = pieces[-1].shape[0]
     width = weight.shape[0]
     steps = 4
     block = rows // steps
@@ -226,29 +238,69 @@
     return lax.ppermute(value, axes, perm)
 
 
-def sum_over_ring(value, axes, sizes, offsets):
-    terms = [value] + [shift(value, axes, sizes, offset) for offset in offsets]
-    return functools.reduce(lambda a, b: a + b, terms)
-
-
-def sum_everywhere(value, core, x):
-    rows = value.shape[0]
-    half = rows // 2
-    mine = lax.dynamic_slice_in_dim(value, core * half, half)
-    other = lax.dynamic_slice_in_dim(value, (1 - core) * half, half)
-    mine = mine + shift(other, "core", (2,), (1,))
-    quarter = half // 4
-    parts = [lax.dynamic_slice_in_dim(mine, lax.rem(x + off, 4) * quarter, quarter) for off in range(4)]
-    own = parts[0]
-    for off in range(1, 4):
-        own = own + shift(parts[off], "x", (4,), (4 - off,))
-    own = sum_over_ring(own, "y", (4,), [(1,), (2,), (3,)])
-    own = sum_over_ring(own, ("zl", "zh"), (2, 2), [(0, 1), (1, 0), (1, 1)])
-    ring = [own] + [shift(own, "x", (4,), (off,)) for off in range(1, 4)]
-    ring = jnp.stack(ring)
-    ordered = jnp.take(ring, jnp.remainder(jnp.arange(4) - x, 4), axis=0).reshape(half, -1)
-    theirs = shift(ordered, "core", (2,), (1,))
-    return jnp.where(core == 0, jnp.concatenate([ordered, theirs]), jnp.concatenate([theirs, ordered]))
+def add(*terms):
+    return functools.reduce(lambda a, b: a + b, [term.astype(F32) for term in terms])
+
+
+def toward(value, axes, dz, dr):
+    return shift(value, axes, (2, 4), (dz, -dr))
+
+
+def scatter_ring_first(held, axes):
+    nodes = held[0].shape[0] // 2
+    arrived = [held[0]] + [toward(held[dr], axes, 0, dr) for dr in range(1, 4)]
+    other = add(*[piece[nodes:] for piece in arrived]).astype(BF16)
+    return arrived + [toward(other, axes, 1, 0)]
+
+
+def scatter_pair_first(held, axes):
+    nodes = held[0].shape[0] // 4
+    arrived = [held[0], toward(held[1], axes, 1, 0)]
+    terms = []
+    for dr in range(1, 4):
+        span = slice(dr * nodes, (dr + 1) * nodes)
+        terms.append(toward(add(arrived[0][span], arrived[1][span]).astype(BF16), axes, 0, dr))
+    return arrived + terms
+
+
+def join_kernel(first, first_pair, *refs):
+    ring, terms = refs[:4], refs[4:8]
+    pair, both, total = refs[8:]
+    nodes = first.shape[0]
+    pair[:nodes, :] = first[...]
+    pair[nodes:, :] = first_pair[...]
+    for index, piece in enumerate(ring):
+        both[index * nodes : (index + 1) * nodes, :] = piece[...]
+    total[...] = (terms[0][...] + terms[1][...]) + (terms[2][...] + terms[3][...])
+
+
+def join(first, first_pair, ring, terms):
+    nodes, width = first.shape
+    return pl.pallas_call(
+        join_kernel,
+        out_shape=[
+            jax.ShapeDtypeStruct((2 * nodes, width), BF16),
+            jax.ShapeDtypeStruct((4 * nodes, width), BF16),
+            jax.ShapeDtypeStruct(terms[0].shape, F32),
+        ],
+        compiler_params=pltpu.CompilerParams(vmem_limit_bytes=VMEM_LIMIT),
+        cost_estimate=pl.CostEstimate(flops=1024, bytes_accessed=1024, transcendentals=0),
+        name="join",
+    )(first, first_pair, *ring, *terms)
+
+
+def around(value, axes, sizes, offsets):
+    return [value] + [shift(value, axes, sizes, offset) for offset in offsets]
+
+
+RING_FIRST = [[dr, 4 + dr] for dr in range(4)]
+PAIR_FIRST = [[0, 1, 2, 3], [4, 5, 6, 7]]
+GATHERED_PAIR_FIRST = [[(0, dr, 1), (1, 4 + dr, 1)] for dr in range(4)]
+GATHERED_RING_FIRST = [[(0, dr, 1)] for dr in range(4)] + [[(0, 4, 4)]]
+
+
+def at_column(plan, column):
+    return [[(*place, column) for place in places] for places in plan]
 
 
 def on_device(
@@ -261,8 +313,8 @@
     count = tile_count.reshape(1)
     zl, y, core = (lax.axis_index(name) for name in ROW)
     zh, x = (lax.axis_index(name) for name in COL)
-    rings = [(dz, dd) for dz in range(2) for dd in range(4)]
     part_width = width // PARTS
+    row_axes, col_axes = ("zl", "y"), ("zh", "x")
 
     row_ids, col_ids = tile_rows[0, 0], tile_cols[0, 0]
     row_slab, col_slab = row_ids // per_slab, col_ids // per_slab
@@ -274,44 +326,46 @@
     row_to = jnp.where(live, row_at, 8 * per_slab)
     col_to = jnp.where(live, col_at, 16 * per_slab)
 
-    columns = [slice(part * part_width, (part + 1) * part_width) for part in range(PARTS)]
-    partials = []
-    for part in range(PARTS):
-        own = features[:, columns[part]]
-        same = [own] + [shift(own, ("zl", "y"), (2, 4), off) for off in rings[1:]]
-        other = [shift(piece, "core", (2,), (1,)) for piece in same]
-        partials.append(
-            sweep(
-                f"forward_{part}", count, col_at, row_to, tiles, same + other,
-                [jax.ShapeDtypeStruct((nodes, part_width), BF16)] * 8, False,
-            )
-        )
-    arrived = []
-    for part in range(PARTS):
-        arrived += [partials[part][0]]
-        arrived += [
-            shift(partials[part][k], COL, (2, 4), (rings[k][0], -rings[k][1])) for k in range(1, 8)
-        ]
-    activations, *grads, weight_term = middle(arrived, weight, layer_bias, cotangent, PARTS)
-
+    whole = lax.all_gather(features, ROW, axis=0, tiled=True)
+    plan = [(slabs, 0) for slabs in RING_FIRST] + [(slabs, part_width) for slabs in PAIR_FIRST]
+    held = sweep(
+        "forward", count, col_ids, row_to, tiles, [whole], [[(0, 0, 16, 0)]],
+        plan, [BF16] * len(plan), nodes, width, False,
+    )
+    arrived = scatter_ring_first(held[:4], col_axes) + scatter_pair_first(held[4:], col_axes)
+    activations, first, second, weight_term = middle(arrived, weight, layer_bias, cotangent, PARTS)
+
+    ring_steps = [(0, 1), (0, 2), (0, 3)]
+    first_pair = shift(first, col_axes, (2, 4), (1, 0))
+    ring = around(second, col_axes, (2, 4), ring_steps)
+    terms = around(weight_term, row_axes, (2, 4), ring_steps)
+    pair, both, weight_sum = join(first, first_pair, ring, terms)
+    gathered = around(pair, col_axes, (2, 4), ring_steps) + ring
+    gathered.append(shift(both, col_axes, (2, 4), (1, 0)))
+    weight_sum = add(*around(weight_sum, "core", (2,), [(1,)]))
+
+    order = [[slab for slabs in plan for slab in slabs] for plan in (RING_FIRST, PAIR_FIRST)]
+    results = sweep(
+        "backward", count, row_at, col_to, tiles, gathered + [weight_sum],
+        at_column(GATHERED_PAIR_FIRST, 0) + at_column(GATHERED_RING_FIRST, part_width) + [[]],
+        [(slabs, part * part_width) for part, slabs in enumerate(order)]
+        + [([8 + slab for slab in slabs], part * part_width) for part, slabs in enumerate(order)],
+        [F32, F32, BF16, BF16], nodes, width, True,
+    )
     collected = []
-    for part in range(PARTS):
-        own = grads[part]
-        pieces = [own] + [shift(own, COL, (2, 4), off) for off in rings[1:]]
-        *mine, theirs = sweep(
-            f"backward_{part}", count, row_at, col_to, tiles, pieces,
-            [jax.ShapeDtypeStruct((nodes, part_width), F32)] * 8
-            + [jax.ShapeDtypeStruct((8 * nodes, part_width), BF16)], True,
-        )
+    for part, plan in enumerate((RING_FIRST, PAIR_FIRST)):
+        mine, theirs = results[part], results[2 + part]
         swapped = shift(theirs, "core", (2,), (1,))
-        for k in range(8):
-            piece = mine[k] + swapped[k * nodes : (k + 1) * nodes].astype(F32)
-            piece = piece.astype(BF16)
-            if k:
-                piece = shift(piece, ("zl", "y"), (2, 4), (rings[k][0], -rings[k][1]))
-            collected.append(piece)
+        held, done = [], 0
+        for slabs in plan:
+            span = slice(done * nodes, (done + len(slabs)) * nodes)
+            held.append(add(mine[span], swapped[span]).astype(BF16))
+            done += len(slabs)
+        scatter = scatter_ring_first if part == 0 else scatter_pair_first
+        collected += scatter(held, row_axes)
     grad_features = final(collected, weight, PARTS)
-    grad_weight = sum_everywhere(weight_term, core, x)
+    weight_sum = add(*around(weight_sum, "x", (4,), [(1,), (2,), (3,)]))
+    grad_weight = add(*around(weight_sum, ("zl", "zh"), (2, 2), [(0, 1), (1, 0), (1, 1)]))
     total_nodes = nodes * 128
     return activations, grad_features, grad_weight * float(total_nodes) ** -0.5
 

time: 357 us -> 281 us (0.79)
  starting transfers between devices: 171 us -> 56.9 us
  waiting for transfers between devices: 118 us -> 155 us
  between operations: 2.37 us -> 15 us
  Pallas kernels: 45.7 us -> 35.1 us
    ppermute x88 -> x36, starting transfers between devices: 171 us -> 56.9 us  [shift(): return lax.ppermute(value, axes, perm)]
    all_gather x0 -> x1, waiting for transfers between devices: none -> 54.4 us  [on_device(): whole = lax.all_gather(features, ROW, axis=0, tiled=True)]
    ppermute x88 -> x36, waiting for transfers between devices: 118 us -> 99.4 us  [shift(): return lax.ppermute(value, axes, perm)]
    pallas_call x4 -> x3, Pallas kernels: 35.5 us -> 25.5 us  [the longest x2 22.6 us: sweep(): pl.pallas_call(functools.partial(sweep_kernel, (source_plan, result_plan,...]
  transfers between devices with their start and end apart: 88 -> 37, of which waited for: 34 -> 19; matrix products, arithmetic and copies ran while one was open for 4% -> 4% of each run, Pallas kernels for 10% -> 0%
where the time goes in v2:
time: 281 us; the launch traced here: 278 us
  waiting for transfers between devices  155 us (55%)
  starting transfers between devices  56.9 us (20%)
  Pallas kernels  35.1 us (12%)
  between operations  15 us (5%)
  other arithmetic  12.1 us (4%)
  local copies, waits for them, and re-layouts  4.22 us (2%)
    ppermute x36, waiting for transfers between devices, shift(): return lax.ppermute(value, axes, perm)  99.4 us
    ppermute x36, starting transfers between devices, shift(): return lax.ppermute(value, axes, perm)  56.9 us
    all_gather x1, waiting for transfers between devices, on_device(): whole = lax.all_gather(features, ROW, axis=0, tiled=True)  54.4 us
    pallas_call x2, Pallas kernels, sweep(): pl.pallas_call(functools.partial(sweep_kernel, (source_plan, result_plan,...  22.6 us
  transfers between devices with their start and end apart: 37, of which 19 were waited for; matrix products, arithmetic and copies ran while one was open for 4% of the time, Pallas kernels for 0%

profile of v2, /device:TPU:1, one launch (start us, length us, event | category | flops | bytes accessed | tf_op | source)
XLA Modules:
  0.0 277.9 jit_solution(7473949982387649974)
XLA Ops:
  8.5 1.2 reduce.refs_1_
  11.1 54.4 %all-gather.2.cloned.1.call-done.refs_4_ = bf16[16384,256]{1,0:T(8,128)(2,1)} async-done(((bf16[1024,256]{1,0:T(8,128)(2,1)}), bf16[16384,256]{1,0:T(8,128)(2,1)}) %all-gather.2.cloned.1.call-update) | async-done | bytes 8388624 | tf_op jit(solution)/shard_map/all_gather | solution.py:329
  65.5 10.2 %forward.1 = (bf16[2048,128]{1,0:T(8,128)(2,1)}, bf16[2048,128]{1,0:T(8,128)(2,1)}, bf16[2048,128]{1,0:T(8,128)(2,1)}, bf16[2048,128]{1,0:T(8,128)(2,1)}, bf16[4...) custom-call(s32[1]{0:T(128)} %bitcast.4.refs_0_, s32[384]{0:T(512)} %reduce.refs_1_, s32[384]{0:T(512)} %get-tuple-element.37.refs_2_, ...), custom_call_target="tpu_custom_call" | custom-call | flops 1024 | bytes 1024 | tf_op jit(solution)/shard_map/forward/pallas_call | solution.py:108
  75.7 1.0 collective-permute-start.4
  76.7 7.4 %collective-permute-start = (bf16[2048,128]{1,0:T(8,128)(2,1)}, bf16[2048,128]{1,0:T(8,128)(2,1)S(1)}, u32[]{:S(2)}, u32[]{:S(2)}) collective-permute-start(bf16[2048,128]{1,0:T(8,128)(2,1)} %get-tuple-element.21), channel_id=1, source_target_pairs={{3,0},{0,1},{1,2},{2,3},{7,4},{4,5},{5,6},{6,7},{11,8},{8,9},{9,10... | collective-permute-start | bytes 1572872 | tf_op jit(solution)/shard_map/ppermute | solution.py:238
  84.2 2.5 collective-permute-start.2
  86.7 4.0 %collective-permute-done.refs_1_ = bf16[2048,128]{1,0:T(8,128)(2,1)S(1)} collective-permute-done((bf16[2048,128]{1,0:T(8,128)(2,1)}, bf16[2048,128]{1,0:T(8,128)(2,1)S(1)}, u32[]{:S(2)}, u32[]{:S(2)}) %collective-permute-start) | collective-permute-done | bytes 524320 | tf_op jit(solution)/shard_map/ppermute | solution.py:238
  90.6 10.5 %collective-permute-done.1.refs_2_ = bf16[2048,128]{1,0:T(8,128)(2,1)S(1)} collective-permute-done((bf16[2048,128]{1,0:T(8,128)(2,1)}, bf16[2048,128]{1,0:T(8,128)(2,1)S(1)}, u32[]{:S(2)}, u32[]{:S(2)}) %collective-permute-start.1) | collective-permute-done | bytes 524320 | tf_op jit(solution)/shard_map/ppermute | solution.py:238
  101.1 5.8 %collective-permute-done.2.refs_3_ = bf16[2048,128]{1,0:T(8,128)(2,1)S(1)} collective-permute-done((bf16[2048,128]{1,0:T(8,128)(2,1)}, bf16[2048,128]{1,0:T(8,128)(2,1)S(1)}, u32[]{:S(2)}, u32[]{:S(2)}) %collective-permute-start.2) | collective-permute-done | bytes 524320 | tf_op jit(solution)/shard_map/ppermute | solution.py:238
  106.9 1.3 add_convert_fusion.13
  108.1 3.2 %collective-permute-start.3 = (bf16[1024,128]{1,0:T(8,128)(2,1)S(1)}, bf16[1024,128]{1,0:T(8,128)(2,1)S(1)}, u32[]{:S(2)}, u32[]{:S(2)}) collective-permute-start(bf16[1024,128]{1,0:T(8,128)(2,1)S(1)} %add_convert_fusion.13), channel_id=1, source_target_pairs={{4,0},{5,1},{6,2},{7,3},{0,4},{1,5},{2,6},{3,7},{12,8},{13,9},{14,... | collective-permute-start | bytes 786440 | tf_op jit(solution)/shard_map/ppermute | solution.py:238
  111.3 1.7 add_convert_fusion.10
  113.0 3.1 %collective-permute-start.5 = (bf16[1024,128]{1,0:T(8,128)(2,1)S(1)}, bf16[1024,128]{1,0:T(8,128)(2,1)S(1)}, u32[]{:S(2)}, u32[]{:S(2)}) collective-permute-start(bf16[1024,128]{1,0:T(8,128)(2,1)S(1)} %get-tuple-element.50), channel_id=1, source_target_pairs={{3,0},{0,1},{1,2},{2,3},{7,4},{4,5},{5,6},{6,7},{11,8},{8,9},{9,10... | collective-permute-start | bytes 786440 | tf_op jit(solution)/shard_map/ppermute | solution.py:238
  116.2 1.4 collective-permute-start.6
  117.6 1.1 collective-permute-start.7
  118.7 3.0 %collective-permute-done.5.refs_7_ = bf16[1024,128]{1,0:T(8,128)(2,1)S(1)} collective-permute-done((bf16[1024,128]{1,0:T(8,128)(2,1)S(1)}, bf16[1024,128]{1,0:T(8,128)(2,1)S(1)}, u32[]{:S(2)}, u32[]{:S(2)}) %collective-permute-start.5) | collective-permute-done | bytes 262176 | tf_op jit(solution)/shard_map/ppermute | solution.py:238
  121.7 7.2 %collective-permute-done.6.refs_8_ = bf16[1024,128]{1,0:T(8,128)(2,1)S(1)} collective-permute-done((bf16[1024,128]{1,0:T(8,128)(2,1)S(1)}, bf16[1024,128]{1,0:T(8,128)(2,1)S(1)}, u32[]{:S(2)}, u32[]{:S(2)}) %collective-permute-start.6) | collective-permute-done | bytes 262176 | tf_op jit(solution)/shard_map/ppermute | solution.py:238
  129.6 5.4 %middle.1 = (bf16[1024,256]{1,0:T(8,128)(2,1)}, bf16[1024,128]{1,0:T(8,128)(2,1)}, bf16[1024,128]{1,0:T(8,128)(2,1)}, f32[256,256]{1,0:T(8,128)}) custom-call(bf16[2048,128]{1,0:T(8,128)(2,1)} %get-tuple-element.20.refs_0_, bf16[2048,128]{1,0:T(8,128)(2,1)} %copy-done.9, bf16[2048,128]{1,0:T(8,128)(2,1)} %copy-done.10, bf16[2048,128]{1,0:T(8,128)(2,1)} %copy-done.11, ...), custom_call_target="tpu_custom_call" | custom-call | tf_op jit(solution)/shard_map/middle/pallas_call | solution.py:185
  135.2 3.0 %collective-permute-start.9 = (bf16[1024,128]{1,0:T(8,128)(2,1)}, bf16[1024,128]{1,0:T(8,128)(2,1)S(1)}, u32[]{:S(2)}, u32[]{:S(2)}) collective-permute-start(bf16[1024,128]{1,0:T(8,128)(2,1)} %get-tuple-element.28.refs_0_.refs_8_), channel_id=1, source_target_pairs={{1,0},{2,1},{3,2},{0,3},{5,4},{6,5},{7,6},{4,7},{9,8},{10,9},{11,1... | collective-permute-start | bytes 786440 | tf_op jit(solution)/shard_map/ppermute | solution.py:238
  138.8 4.2 %collective-permute-done.8.first_pair = bf16[1024,128]{1,0:T(8,128)(2,1)S(1)} collective-permute-done((bf16[1024,128]{1,0:T(8,128)(2,1)}, bf16[1024,128]{1,0:T(8,128)(2,1)S(1)}, u32[]{:S(2)}, u32[]{:S(2)}) %collective-permute-start.8) | collective-permute-done | bytes 262176 | tf_op jit(solution)/shard_map/ppermute | solution.py:238
  143.0 2.1 collective-permute-done.9.refs_1_.refs_9_
  145.2 1.6 collective-permute-done.10.refs_2_.refs_10_
  146.7 7.0 %collective-permute-done.11.refs_3_.refs_11_ = bf16[1024,128]{1,0:T(8,128)(2,1)S(1)} collective-permute-done((bf16[1024,128]{1,0:T(8,128)(2,1)}, bf16[1024,128]{1,0:T(8,128)(2,1)S(1)}, u32[]{:S(2)}, u32[]{:S(2)}) %collective-permute-start.11) | collective-permute-done | bytes 262176 | tf_op jit(solution)/shard_map/ppermute | solution.py:238
  153.7 2.3 collective-permute-done.14.refs_7_
  156.7 2.9 %join.1 = (bf16[2048,128]{1,0:T(8,128)(2,1)}, bf16[4096,128]{1,0:T(8,128)(2,1)}, f32[256,256]{1,0:T(8,128)}) custom-call(bf16[1024,128]{1,0:T(8,128)(2,1)} %get-tuple-element.27.first, bf16[1024,128]{1,0:T(8,128)(2,1)} %copy-done.20, bf16[1024,128]{1,0:T(8,128)(2,1)} %get-tuple-element.28.refs_0_.refs_8_, bf16[1024,128]{1,0:T(8,128)(2,1)} %copy-done.12, ...), custom_call_target="tpu_custom_call" | custom-call | flops 1024 | bytes 1024 | tf_op jit(solution)/shard_map/join/pallas_call | solution.py:279
  159.7 1.5 collective-permute-start.18
  161.1 5.2 %collective-permute-start.15 = (bf16[2048,128]{1,0:T(8,128)(2,1)}, bf16[2048,128]{1,0:T(8,128)(2,1)S(1)}, u32[]{:S(2)}, u32[]{:S(2)}) collective-permute-start(bf16[2048,128]{1,0:T(8,128)(2,1)} %get-tuple-element.30.refs_4_), channel_id=1, source_target_pairs={{1,0},{2,1},{3,2},{0,3},{5,4},{6,5},{7,6},{4,7},{9,8},{10,9},{11,1... | collective-permute-start | bytes 1572872 | tf_op jit(solution)/shard_map/ppermute | solution.py:238
  167.0 3.4 %collective-permute-start.19 = (f32[256,256]{1,0:T(8,128)}, f32[256,256]{1,0:T(8,128)S(1)}, u32[]{:S(2)}, u32[]{:S(2)}) collective-permute-start(f32[256,256]{1,0:T(8,128)} %get-tuple-element.32), channel_id=1, source_target_pairs={{8,0},{0,8},{9,1},{1,9},{10,2},{2,10},{11,3},{3,11},{12,4},{4,12},... | collective-permute-start | bytes 786440 | tf_op jit(solution)/shard_map/ppermute | solution.py:238
  171.0 0.8 collective-permute-done.19
  171.8 1.7 add.143.refs_13_
  173.5 3.1 %collective-permute-done.15.refs_5_ = bf16[2048,128]{1,0:T(8,128)(2,1)S(1)} collective-permute-done((bf16[2048,128]{1,0:T(8,128)(2,1)}, bf16[2048,128]{1,0:T(8,128)(2,1)S(1)}, u32[]{:S(2)}, u32[]{:S(2)}) %collective-permute-start.15) | collective-permute-done | bytes 524320 | tf_op jit(solution)/shard_map/ppermute | solution.py:238
  176.5 1.9 collective-permute-done.16.refs_6_
  178.5 14.1 %collective-permute-done.17.refs_7_ = bf16[2048,128]{1,0:T(8,128)(2,1)S(1)} collective-permute-done((bf16[2048,128]{1,0:T(8,128)(2,1)}, bf16[2048,128]{1,0:T(8,128)(2,1)S(1)}, u32[]{:S(2)}, u32[]{:S(2)}) %collective-permute-start.17) | collective-permute-done | bytes 524320 | tf_op jit(solution)/shard_map/ppermute | solution.py:238
  192.6 0.8 copy-done.18
  193.7 12.4 %backward.1 = (f32[8192,128]{1,0:T(8,128)}, f32[8192,128]{1,0:T(8,128)}, bf16[8192,128]{1,0:T(8,128)(2,1)}, bf16[8192,128]{1,0:T(8,128)(2,1)}) custom-call(s32[1]{0:T(128)} %bitcast.5.refs_0_, s32[384]{0:T(512)} %get-tuple-element.38.refs_1_, s32[384]{0:T(512)} %fusion.19.refs_2_, bf16[384,128,128]{2,1,0:T(8,128)(2,1)} %bitcast.9, ...), custom_call_target="tpu_custom_call" | custom-call | flops 1024 | bytes 1024 | tf_op jit(solution)/shard_map/backward/pallas_call | solution.py:108
  206.7 6.0 %collective-permute-start.32 = (f32[256,256]{1,0:T(8,128)S(1)}, f32[256,256]{1,0:T(8,128)S(1)}, u32[]{:S(2)}, u32[]{:S(2)}) collective-permute-start(f32[256,256]{1,0:T(8,128)S(1)} %copy-done.5), channel_id=1, source_target_pairs={{3,0},{0,1},{1,2},{2,3},{7,4},{4,5},{5,6},{6,7},{11,8},{8,9},{9,10... | collective-permute-start | bytes 786440 | tf_op jit(solution)/shard_map/ppermute | solution.py:238
  212.7 2.8 %add_convert_fusion = (bf16[4096,128]{1,0:T(8,128)(2,1)S(1)}, bf16[4096,128]{1,0:T(8,128)(2,1)S(1)}) fusion(f32[8192,128]{1,0:T(8,128)} %get-tuple-element.35, bf16[8192,128]{1,0:T(8,128)(2,1)S(1)} %collective-permute-done.25), kind=kLoop, calls=%fused_computation | loop fusion | flops 3145728 | bytes 8388608 | tf_op jit(solution)/shard_map/convert_element_type | solution.py:362
  215.5 6.6 %collective-permute-start.26 = (bf16[4096,128]{1,0:T(8,128)(2,1)S(1)}, bf16[4096,128]{1,0:T(8,128)(2,1)S(1)}, u32[]{:S(2)}, u32[]{:S(2)}) collective-permute-start(bf16[4096,128]{1,0:T(8,128)(2,1)S(1)} %get-tuple-element.39), channel_id=1, source_target_pairs={{64,0},{80,16},{96,32},{112,48},{0,64},{16,80},{32,96},{48,112},{6... | collective-permute-start | bytes 3145736 | tf_op jit(solution)/shard_map/ppermute | solution.py:238
  222.7 2.6 collective-permute-start.23
  225.3 6.6 %collective-permute-done.30 = f32[256,256]{1,0:T(8,128)S(1)} collective-permute-done((f32[256,256]{1,0:T(8,128)S(1)}, f32[256,256]{1,0:T(8,128)S(1)}, u32[]{:S(2)}, u32[]{:S(2)}) %collective-permute-start.30) | collective-permute-done | bytes 262176 | tf_op jit(solution)/shard_map/ppermute | solution.py:238
  231.9 0.9 collective-permute-start.35
  232.8 15.0 %collective-permute-done.21.refs_1_ = bf16[2048,128]{1,0:T(8,128)(2,1)S(1)} collective-permute-done((bf16[2048,128]{1,0:T(8,128)(2,1)S(1)}, bf16[2048,128]{1,0:T(8,128)(2,1)S(1)}, u32[]{:S(2)}, u32[]{:S(2)}) %collective-permute-start.21) | collective-permute-done | bytes 524320 | tf_op jit(solution)/shard_map/ppermute | solution.py:238
  247.8 0.9 collective-permute-start.34
  250.5 3.6 %collective-permute-start.28 = (bf16[1024,128]{1,0:T(8,128)(2,1)S(1)}, bf16[1024,128]{1,0:T(8,128)(2,1)S(1)}, u32[]{:S(2)}, u32[]{:S(2)}) collective-permute-start(bf16[1024,128]{1,0:T(8,128)(2,1)S(1)} %get-tuple-element.46), channel_id=1, source_target_pairs={{32,0},{48,16},{0,32},{16,48},{96,64},{112,80},{64,96},{80,112},{3... | collective-permute-start | bytes 786440 | tf_op jit(solution)/shard_map/ppermute | solution.py:238
  254.1 4.6 %collective-permute-done.33 = f32[256,256]{1,0:T(8,128)S(1)} collective-permute-done((f32[256,256]{1,0:T(8,128)S(1)}, f32[256,256]{1,0:T(8,128)S(1)}, u32[]{:S(2)}, u32[]{:S(2)}) %collective-permute-start.33) | collective-permute-done | bytes 262176 | tf_op jit(solution)/shard_map/ppermute | solution.py:238
  258.7 0.8 add_multiply_fusion
  259.5 5.8 %collective-permute-done.24.refs_4_ = bf16[1024,128]{1,0:T(8,128)(2,1)S(1)} collective-permute-done((bf16[1024,128]{1,0:T(8,128)(2,1)S(1)}, bf16[1024,128]{1,0:T(8,128)(2,1)S(1)}, u32[]{:S(2)}, u32[]{:S(2)}) %collective-permute-start.24) | collective-permute-done | bytes 262176 | tf_op jit(solution)/shard_map/ppermute | solution.py:238
  266.9 4.2 %final.1 = bf16[1024,256]{1,0:T(8,128)(2,1)} custom-call(bf16[2048,128]{1,0:T(8,128)(2,1)} %copy-done.2, bf16[2048,128]{1,0:T(8,128)(2,1)} %copy-done.6, bf16[2048,128]{1,0:T(8,128)(2,1)} %copy-done.7, bf16[2048,128]{1,0:T(8,128)(2,1)} %copy-done.8, bf16[1024,128]{1,0:T(8,128)(2,1)} %copy-done.19, bf16[4096,128]{1,0:T(8,128)(2,1)} %copy-done, ...), custom_call_target="tpu_custom_call" | custom-call | tf_op jit(solution)/shard_map/final/pallas_call | solution.py:212
  (109 shorter events, 10.4 us)
Async XLA Ops:
  7.2 58.4 %all-gather.2.cloned.1.call-start = ((), (), s32[]{:S(2)}) async-start(), calls=%async_computation | async-start | bytes 8912896 | tf_op jit(solution)/shard_map/all_gather | solution.py:329
  75.7 35.6 %collective-permute-start.4 = (bf16[4096,128]{1,0:T(8,128)(2,1)}, bf16[4096,128]{1,0:T(8,128)(2,1)S(1)}, u32[]{:S(2)}, u32[]{:S(2)}) collective-permute-start(bf16[4096,128]{1,0:T(8,128)(2,1)} %get-tuple-element.25), channel_id=1, source_target_pairs={{4,0},{5,1},{6,2},{7,3},{0,4},{1,5},{2,6},{3,7},{12,8},{13,9},{14,... | collective-permute-start | bytes 3145736 | tf_op jit(solution)/shard_map/ppermute | solution.py:238
  76.7 13.9 %collective-permute-start = (bf16[2048,128]{1,0:T(8,128)(2,1)}, bf16[2048,128]{1,0:T(8,128)(2,1)S(1)}, u32[]{:S(2)}, u32[]{:S(2)}) collective-permute-start(bf16[2048,128]{1,0:T(8,128)(2,1)} %get-tuple-element.21), channel_id=1, source_target_pairs={{3,0},{0,1},{1,2},{2,3},{7,4},{4,5},{5,6},{6,7},{11,8},{8,9},{9,10... | collective-permute-start | bytes 1572872 | tf_op jit(solution)/shard_map/ppermute | solution.py:238
  84.2 16.9 %collective-permute-start.1 = (bf16[2048,128]{1,0:T(8,128)(2,1)}, bf16[2048,128]{1,0:T(8,128)(2,1)S(1)}, u32[]{:S(2)}, u32[]{:S(2)}) collective-permute-start(bf16[2048,128]{1,0:T(8,128)(2,1)} %get-tuple-element.22), channel_id=1, source_target_pairs={{2,0},{3,1},{0,2},{1,3},{6,4},{7,5},{4,6},{5,7},{10,8},{11,9},{8,1... | collective-permute-start | bytes 1572872 | tf_op jit(solution)/shard_map/ppermute | solution.py:238
  84.2 22.7 %collective-permute-start.2 = (bf16[2048,128]{1,0:T(8,128)(2,1)}, bf16[2048,128]{1,0:T(8,128)(2,1)S(1)}, u32[]{:S(2)}, u32[]{:S(2)}) collective-permute-start(bf16[2048,128]{1,0:T(8,128)(2,1)} %get-tuple-element.23), channel_id=1, source_target_pairs={{1,0},{2,1},{3,2},{0,3},{5,4},{6,5},{7,6},{4,7},{9,8},{10,9},{11,1... | collective-permute-start | bytes 1572872 | tf_op jit(solution)/shard_map/ppermute | solution.py:238
  90.6 38.2 %copy-start.9 = (bf16[2048,128]{1,0:T(8,128)(2,1)}, bf16[2048,128]{1,0:T(8,128)(2,1)S(1)}, u32[]{:S(2)}) copy-start(bf16[2048,128]{1,0:T(8,128)(2,1)S(1)} %collective-permute-done.refs_1_) | copy-start | bytes 1572868
  101.1 27.7 %copy-start.10 = (bf16[2048,128]{1,0:T(8,128)(2,1)}, bf16[2048,128]{1,0:T(8,128)(2,1)S(1)}, u32[]{:S(2)}) copy-start(bf16[2048,128]{1,0:T(8,128)(2,1)S(1)} %collective-permute-done.1.refs_2_) | copy-start | bytes 1572868
  106.9 22.0 %copy-start.11 = (bf16[2048,128]{1,0:T(8,128)(2,1)}, bf16[2048,128]{1,0:T(8,128)(2,1)S(1)}, u32[]{:S(2)}) copy-start(bf16[2048,128]{1,0:T(8,128)(2,1)S(1)} %collective-permute-done.2.refs_3_) | copy-start | bytes 1572868
  108.1 10.6 %collective-permute-start.3 = (bf16[1024,128]{1,0:T(8,128)(2,1)S(1)}, bf16[1024,128]{1,0:T(8,128)(2,1)S(1)}, u32[]{:S(2)}, u32[]{:S(2)}) collective-permute-start(bf16[1024,128]{1,0:T(8,128)(2,1)S(1)} %add_convert_fusion.13), channel_id=1, source_target_pairs={{4,0},{5,1},{6,2},{7,3},{0,4},{1,5},{2,6},{3,7},{12,8},{13,9},{14,... | collective-permute-start | bytes 786440 | tf_op jit(solution)/shard_map/ppermute | solution.py:238
  111.3 17.5 %copy-start.3 = (bf16[4096,128]{1,0:T(8,128)(2,1)}, bf16[4096,128]{1,0:T(8,128)(2,1)S(1)}, u32[]{:S(2)}) copy-start(bf16[4096,128]{1,0:T(8,128)(2,1)S(1)} %collective-permute-done.4.refs_6_) | copy-start | bytes 3145732
  113.0 8.6 %collective-permute-start.5 = (bf16[1024,128]{1,0:T(8,128)(2,1)S(1)}, bf16[1024,128]{1,0:T(8,128)(2,1)S(1)}, u32[]{:S(2)}, u32[]{:S(2)}) collective-permute-start(bf16[1024,128]{1,0:T(8,128)(2,1)S(1)} %get-tuple-element.50), channel_id=1, source_target_pairs={{3,0},{0,1},{1,2},{2,3},{7,4},{4,5},{5,6},{6,7},{11,8},{8,9},{9,10... | collective-permute-start | bytes 786440 | tf_op jit(solution)/shard_map/ppermute | solution.py:238
  116.2 12.7 %collective-permute-start.6 = (bf16[1024,128]{1,0:T(8,128)(2,1)S(1)}, bf16[1024,128]{1,0:T(8,128)(2,1)S(1)}, u32[]{:S(2)}, u32[]{:S(2)}) collective-permute-start(bf16[1024,128]{1,0:T(8,128)(2,1)S(1)} %get-tuple-element.49), channel_id=1, source_target_pairs={{2,0},{3,1},{0,2},{1,3},{6,4},{7,5},{4,6},{5,7},{10,8},{11,9},{8,1... | collective-permute-start | bytes 786440 | tf_op jit(solution)/shard_map/ppermute | solution.py:238
  117.6 11.2 %collective-permute-start.7 = (bf16[1024,128]{1,0:T(8,128)(2,1)S(1)}, bf16[1024,128]{1,0:T(8,128)(2,1)S(1)}, u32[]{:S(2)}, u32[]{:S(2)}) collective-permute-start(bf16[1024,128]{1,0:T(8,128)(2,1)S(1)} %get-tuple-element.48), channel_id=1, source_target_pairs={{1,0},{2,1},{3,2},{0,3},{5,4},{6,5},{7,6},{4,7},{9,8},{10,9},{11,1... | collective-permute-start | bytes 786440 | tf_op jit(solution)/shard_map/ppermute | solution.py:238
  135.1 35.4 %copy-start.31 = (s32[384]{0:T(512)S(1)}, s32[384]{0:T(512)}, u32[]{:S(2)}) copy-start(s32[384]{0:T(512)} %reduce.refs_1_) | copy-start | bytes 4612
  135.1 8.0 %collective-permute-start.8 = (bf16[1024,128]{1,0:T(8,128)(2,1)}, bf16[1024,128]{1,0:T(8,128)(2,1)S(1)}, u32[]{:S(2)}, u32[]{:S(2)}) collective-permute-start(bf16[1024,128]{1,0:T(8,128)(2,1)} %get-tuple-element.27.first), channel_id=1, source_target_pairs={{4,0},{5,1},{6,2},{7,3},{0,4},{1,5},{2,6},{3,7},{12,8},{13,9},{14,... | collective-permute-start | bytes 786440 | tf_op jit(solution)/shard_map/ppermute | solution.py:238
  135.2 10.0 %collective-permute-start.9 = (bf16[1024,128]{1,0:T(8,128)(2,1)}, bf16[1024,128]{1,0:T(8,128)(2,1)S(1)}, u32[]{:S(2)}, u32[]{:S(2)}) collective-permute-start(bf16[1024,128]{1,0:T(8,128)(2,1)} %get-tuple-element.28.refs_0_.refs_8_), channel_id=1, source_target_pairs={{1,0},{2,1},{3,2},{0,3},{5,4},{6,5},{7,6},{4,7},{9,8},{10,9},{11,1... | collective-permute-start | bytes 786440 | tf_op jit(solution)/shard_map/ppermute | solution.py:238
  138.2 8.6 %collective-permute-start.10 = (bf16[1024,128]{1,0:T(8,128)(2,1)}, bf16[1024,128]{1,0:T(8,128)(2,1)S(1)}, u32[]{:S(2)}, u32[]{:S(2)}) collective-permute-start(bf16[1024,128]{1,0:T(8,128)(2,1)} %get-tuple-element.28.refs_0_.refs_8_), channel_id=1, source_target_pairs={{2,0},{3,1},{0,2},{1,3},{6,4},{7,5},{4,6},{5,7},{10,8},{11,9},{8,1... | collective-permute-start | bytes 786440 | tf_op jit(solution)/shard_map/ppermute | solution.py:238
  138.8 14.9 %collective-permute-start.11 = (bf16[1024,128]{1,0:T(8,128)(2,1)}, bf16[1024,128]{1,0:T(8,128)(2,1)S(1)}, u32[]{:S(2)}, u32[]{:S(2)}) collective-permute-start(bf16[1024,128]{1,0:T(8,128)(2,1)} %get-tuple-element.28.refs_0_.refs_8_), channel_id=1, source_target_pairs={{3,0},{0,1},{1,2},{2,3},{7,4},{4,5},{5,6},{6,7},{11,8},{8,9},{9,10... | collective-permute-start | bytes 786440 | tf_op jit(solution)/shard_map/ppermute | solution.py:238
  138.8 14.9 %collective-permute-start.12 = (f32[256,256]{1,0:T(8,128)}, f32[256,256]{1,0:T(8,128)S(1)}, u32[]{:S(2)}, u32[]{:S(2)}) collective-permute-start(f32[256,256]{1,0:T(8,128)} %get-tuple-element.29.refs_4_), channel_id=1, source_target_pairs={{16,0},{32,16},{48,32},{0,48},{80,64},{96,80},{112,96},{64,112},{1... | collective-permute-start | bytes 786440 | tf_op jit(solution)/shard_map/ppermute | solution.py:238
  143.0 10.7 %collective-permute-start.13 = (f32[256,256]{1,0:T(8,128)}, f32[256,256]{1,0:T(8,128)S(1)}, u32[]{:S(2)}, u32[]{:S(2)}) collective-permute-start(f32[256,256]{1,0:T(8,128)} %get-tuple-element.29.refs_4_), channel_id=1, source_target_pairs={{32,0},{48,16},{0,32},{16,48},{96,64},{112,80},{64,96},{80,112},{3... | collective-permute-start | bytes 786440 | tf_op jit(solution)/shard_map/ppermute | solution.py:238
  145.2 10.8 %collective-permute-start.14 = (f32[256,256]{1,0:T(8,128)}, f32[256,256]{1,0:T(8,128)S(1)}, u32[]{:S(2)}, u32[]{:S(2)}) collective-permute-start(f32[256,256]{1,0:T(8,128)} %get-tuple-element.29.refs_4_), channel_id=1, source_target_pairs={{48,0},{0,16},{16,32},{32,48},{112,64},{64,80},{80,96},{96,112},{4... | collective-permute-start | bytes 786440 | tf_op jit(solution)/shard_map/ppermute | solution.py:238
  159.7 32.9 %collective-permute-start.18 = (bf16[4096,128]{1,0:T(8,128)(2,1)}, bf16[4096,128]{1,0:T(8,128)(2,1)S(1)}, u32[]{:S(2)}, u32[]{:S(2)}) collective-permute-start(bf16[4096,128]{1,0:T(8,128)(2,1)} %get-tuple-element.31), channel_id=1, source_target_pairs={{4,0},{5,1},{6,2},{7,3},{0,4},{1,5},{2,6},{3,7},{12,8},{13,9},{14,... | collective-permute-start | bytes 3145736 | tf_op jit(solution)/shard_map/ppermute | solution.py:238
  161.1 15.4 %collective-permute-start.15 = (bf16[2048,128]{1,0:T(8,128)(2,1)}, bf16[2048,128]{1,0:T(8,128)(2,1)S(1)}, u32[]{:S(2)}, u32[]{:S(2)}) collective-permute-start(bf16[2048,128]{1,0:T(8,128)(2,1)} %get-tuple-element.30.refs_4_), channel_id=1, source_target_pairs={{1,0},{2,1},{3,2},{0,3},{5,4},{6,5},{7,6},{4,7},{9,8},{10,9},{11,1... | collective-permute-start | bytes 1572872 | tf_op jit(solution)/shard_map/ppermute | solution.py:238
  166.4 12.1 %collective-permute-start.16 = (bf16[2048,128]{1,0:T(8,128)(2,1)}, bf16[2048,128]{1,0:T(8,128)(2,1)S(1)}, u32[]{:S(2)}, u32[]{:S(2)}) collective-permute-start(bf16[2048,128]{1,0:T(8,128)(2,1)} %get-tuple-element.30.refs_4_), channel_id=1, source_target_pairs={{2,0},{3,1},{0,2},{1,3},{6,4},{7,5},{4,6},{5,7},{10,8},{11,9},{8,1... | collective-permute-start | bytes 1572872 | tf_op jit(solution)/shard_map/ppermute | solution.py:238
  166.4 26.1 %collective-permute-start.17 = (bf16[2048,128]{1,0:T(8,128)(2,1)}, bf16[2048,128]{1,0:T(8,128)(2,1)S(1)}, u32[]{:S(2)}, u32[]{:S(2)}) collective-permute-start(bf16[2048,128]{1,0:T(8,128)(2,1)} %get-tuple-element.30.refs_4_), channel_id=1, source_target_pairs={{3,0},{0,1},{1,2},{2,3},{7,4},{4,5},{5,6},{6,7},{11,8},{8,9},{9,10... | collective-permute-start | bytes 1572872 | tf_op jit(solution)/shard_map/ppermute | solution.py:238
  167.0 4.8 %collective-permute-start.19 = (f32[256,256]{1,0:T(8,128)}, f32[256,256]{1,0:T(8,128)S(1)}, u32[]{:S(2)}, u32[]{:S(2)}) collective-permute-start(f32[256,256]{1,0:T(8,128)} %get-tuple-element.32), channel_id=1, source_target_pairs={{8,0},{0,8},{9,1},{1,9},{10,2},{2,10},{11,3},{3,11},{12,4},{4,12},... | collective-permute-start | bytes 786440 | tf_op jit(solution)/shard_map/ppermute | solution.py:238
  176.5 16.0 %copy-start.16 = (bf16[2048,128]{1,0:T(8,128)(2,1)}, bf16[2048,128]{1,0:T(8,128)(2,1)S(1)}, u32[]{:S(2)}) copy-start(bf16[2048,128]{1,0:T(8,128)(2,1)S(1)} %collective-permute-done.15.refs_5_) | copy-start | bytes 1572868
  178.5 14.1 %copy-start.17 = (bf16[2048,128]{1,0:T(8,128)(2,1)}, bf16[2048,128]{1,0:T(8,128)(2,1)S(1)}, u32[]{:S(2)}) copy-start(bf16[2048,128]{1,0:T(8,128)(2,1)S(1)} %collective-permute-done.16.refs_6_) | copy-start | bytes 1572868
  193.7 13.0 %copy-start.5 = (f32[256,256]{1,0:T(8,128)S(1)}, f32[256,256]{1,0:T(8,128)}, u32[]{:S(2)}) copy-start(f32[256,256]{1,0:T(8,128)} %add.143.refs_13_) | copy-start | bytes 786436
  206.1 6.6 %collective-permute-start.25 = (bf16[8192,128]{1,0:T(8,128)(2,1)}, bf16[8192,128]{1,0:T(8,128)(2,1)S(1)}, u32[]{:S(2)}, u32[]{:S(2)}) collective-permute-start(bf16[8192,128]{1,0:T(8,128)(2,1)} %get-tuple-element.36), channel_id=1, source_target_pairs={{8,0},{0,8},{9,1},{1,9},{10,2},{2,10},{11,3},{3,11},{12,4},{4,12},... | collective-permute-start | bytes 6291464 | tf_op jit(solution)/shard_map/ppermute | solution.py:238
  206.2 15.8 %collective-permute-start.20 = (bf16[8192,128]{1,0:T(8,128)(2,1)}, bf16[8192,128]{1,0:T(8,128)(2,1)S(1)}, u32[]{:S(2)}, u32[]{:S(2)}) collective-permute-start(bf16[8192,128]{1,0:T(8,128)(2,1)} %get-tuple-element.34), channel_id=1, source_target_pairs={{8,0},{0,8},{9,1},{1,9},{10,2},{2,10},{11,3},{3,11},{12,4},{4,12},... | collective-permute-start | bytes 6291464 | tf_op jit(solution)/shard_map/ppermute | solution.py:238
  206.7 15.9 %collective-permute-start.32 = (f32[256,256]{1,0:T(8,128)S(1)}, f32[256,256]{1,0:T(8,128)S(1)}, u32[]{:S(2)}, u32[]{:S(2)}) collective-permute-start(f32[256,256]{1,0:T(8,128)S(1)} %copy-done.5), channel_id=1, source_target_pairs={{3,0},{0,1},{1,2},{2,3},{7,4},{4,5},{5,6},{6,7},{11,8},{8,9},{9,10... | collective-permute-start | bytes 786440 | tf_op jit(solution)/shard_map/ppermute | solution.py:238
  212.7 12.6 %collective-permute-start.31 = (f32[256,256]{1,0:T(8,128)S(1)}, f32[256,256]{1,0:T(8,128)S(1)}, u32[]{:S(2)}, u32[]{:S(2)}) collective-permute-start(f32[256,256]{1,0:T(8,128)S(1)} %copy-done.5), channel_id=1, source_target_pairs={{2,0},{3,1},{0,2},{1,3},{6,4},{7,5},{4,6},{5,7},{10,8},{11,9},{8,1... | collective-permute-start | bytes 786440 | tf_op jit(solution)/shard_map/ppermute | solution.py:238
  215.5 34.1 %copy-start = (bf16[4096,128]{1,0:T(8,128)(2,1)}, bf16[4096,128]{1,0:T(8,128)(2,1)S(1)}, u32[]{:S(2)}) copy-start(bf16[4096,128]{1,0:T(8,128)(2,1)S(1)} %get-tuple-element.40.refs_5_) | copy-start | bytes 3145732
  215.5 34.1 %collective-permute-start.26 = (bf16[4096,128]{1,0:T(8,128)(2,1)S(1)}, bf16[4096,128]{1,0:T(8,128)(2,1)S(1)}, u32[]{:S(2)}, u32[]{:S(2)}) collective-permute-start(bf16[4096,128]{1,0:T(8,128)(2,1)S(1)} %get-tuple-element.39), channel_id=1, source_target_pairs={{64,0},{80,16},{96,32},{112,48},{0,64},{16,80},{32,96},{48,112},{6... | collective-permute-start | bytes 3145736 | tf_op jit(solution)/shard_map/ppermute | solution.py:238
  222.5 27.3 %copy-start.2 = (bf16[2048,128]{1,0:T(8,128)(2,1)}, bf16[2048,128]{1,0:T(8,128)(2,1)S(1)}, u32[]{:S(2)}) copy-start(bf16[2048,128]{1,0:T(8,128)(2,1)S(1)} %get-tuple-element.44.refs_0_) | copy-start | bytes 1572868
  222.5 25.3 %collective-permute-start.21 = (bf16[2048,128]{1,0:T(8,128)(2,1)S(1)}, bf16[2048,128]{1,0:T(8,128)(2,1)S(1)}, u32[]{:S(2)}, u32[]{:S(2)}) collective-permute-start(bf16[2048,128]{1,0:T(8,128)(2,1)S(1)} %get-tuple-element.43), channel_id=1, source_target_pairs={{48,0},{0,16},{16,32},{32,48},{112,64},{64,80},{80,96},{96,112},{4... | collective-permute-start | bytes 1572872 | tf_op jit(solution)/shard_map/ppermute | solution.py:238
  222.6 26.1 %collective-permute-start.22 = (bf16[2048,128]{1,0:T(8,128)(2,1)S(1)}, bf16[2048,128]{1,0:T(8,128)(2,1)S(1)}, u32[]{:S(2)}, u32[]{:S(2)}) collective-permute-start(bf16[2048,128]{1,0:T(8,128)(2,1)S(1)} %get-tuple-element.42), channel_id=1, source_target_pairs={{32,0},{48,16},{0,32},{16,48},{96,64},{112,80},{64,96},{80,112},{3... | collective-permute-start | bytes 1572872 | tf_op jit(solution)/shard_map/ppermute | solution.py:238
  222.7 26.1 %collective-permute-start.23 = (bf16[2048,128]{1,0:T(8,128)(2,1)S(1)}, bf16[2048,128]{1,0:T(8,128)(2,1)S(1)}, u32[]{:S(2)}, u32[]{:S(2)}) collective-permute-start(bf16[2048,128]{1,0:T(8,128)(2,1)S(1)} %get-tuple-element.41), channel_id=1, source_target_pairs={{16,0},{32,16},{48,32},{0,48},{80,64},{96,80},{112,96},{64,112},{1... | collective-permute-start | bytes 1572872 | tf_op jit(solution)/shard_map/ppermute | solution.py:238
  225.3 6.6 %collective-permute-start.30 = (f32[256,256]{1,0:T(8,128)S(1)}, f32[256,256]{1,0:T(8,128)S(1)}, u32[]{:S(2)}, u32[]{:S(2)}) collective-permute-start(f32[256,256]{1,0:T(8,128)S(1)} %copy-done.5), channel_id=1, source_target_pairs={{1,0},{2,1},{3,2},{0,3},{5,4},{6,5},{7,6},{4,7},{9,8},{10,9},{11,1... | collective-permute-start | bytes 786440 | tf_op jit(solution)/shard_map/ppermute | solution.py:238
  231.9 18.6 %collective-permute-start.35 = (f32[256,256]{1,0:T(8,128)S(1)}, f32[256,256]{1,0:T(8,128)S(1)}, u32[]{:S(2)}, u32[]{:S(2)}) collective-permute-start(f32[256,256]{1,0:T(8,128)S(1)} %add_add_fusion), channel_id=1, source_target_pairs={{68,0},{64,4},{4,64},{0,68},{69,1},{65,5},{5,65},{1,69},{70,2},{66... | collective-permute-start | bytes 786440 | tf_op jit(solution)/shard_map/ppermute | solution.py:238
  247.8 6.3 %collective-permute-start.34 = (f32[256,256]{1,0:T(8,128)S(1)}, f32[256,256]{1,0:T(8,128)S(1)}, u32[]{:S(2)}, u32[]{:S(2)}) collective-permute-start(f32[256,256]{1,0:T(8,128)S(1)} %add_add_fusion), channel_id=1, source_target_pairs={{64,0},{68,4},{0,64},{4,68},{65,1},{69,5},{1,65},{5,69},{66,2},{70... | collective-permute-start | bytes 786440 | tf_op jit(solution)/shard_map/ppermute | solution.py:238
  248.7 10.0 %collective-permute-start.33 = (f32[256,256]{1,0:T(8,128)S(1)}, f32[256,256]{1,0:T(8,128)S(1)}, u32[]{:S(2)}, u32[]{:S(2)}) collective-permute-start(f32[256,256]{1,0:T(8,128)S(1)} %add_add_fusion), channel_id=1, source_target_pairs={{4,0},{0,4},{68,64},{64,68},{5,1},{1,5},{69,65},{65,69},{6,2},{2,6... | collective-permute-start | bytes 786440 | tf_op jit(solution)/shard_map/ppermute | solution.py:238
  248.9 16.4 %collective-permute-start.24 = (bf16[1024,128]{1,0:T(8,128)(2,1)S(1)}, bf16[1024,128]{1,0:T(8,128)(2,1)S(1)}, u32[]{:S(2)}, u32[]{:S(2)}) collective-permute-start(bf16[1024,128]{1,0:T(8,128)(2,1)S(1)} %add_convert_fusion.9), channel_id=1, source_target_pairs={{64,0},{80,16},{96,32},{112,48},{0,64},{16,80},{32,96},{48,112},{6... | collective-permute-start | bytes 786440 | tf_op jit(solution)/shard_map/ppermute | solution.py:238
  249.6 15.8 %copy-start.4 = (bf16[4096,128]{1,0:T(8,128)(2,1)}, bf16[4096,128]{1,0:T(8,128)(2,1)S(1)}, u32[]{:S(2)}) copy-start(bf16[4096,128]{1,0:T(8,128)(2,1)S(1)} %collective-permute-done.26.refs_6_) | copy-start | bytes 3145732
  249.8 15.6 %collective-permute-start.27 = (bf16[1024,128]{1,0:T(8,128)(2,1)S(1)}, bf16[1024,128]{1,0:T(8,128)(2,1)S(1)}, u32[]{:S(2)}, u32[]{:S(2)}) collective-permute-start(bf16[1024,128]{1,0:T(8,128)(2,1)S(1)} %get-tuple-element.47), channel_id=1, source_target_pairs={{48,0},{0,16},{16,32},{32,48},{112,64},{64,80},{80,96},{96,112},{4... | collective-permute-start | bytes 786440 | tf_op jit(solution)/shard_map/ppermute | solution.py:238
  250.5 14.8 %collective-permute-start.28 = (bf16[1024,128]{1,0:T(8,128)(2,1)S(1)}, bf16[1024,128]{1,0:T(8,128)(2,1)S(1)}, u32[]{:S(2)}, u32[]{:S(2)}) collective-permute-start(bf16[1024,128]{1,0:T(8,128)(2,1)S(1)} %get-tuple-element.46), channel_id=1, source_target_pairs={{32,0},{48,16},{0,32},{16,48},{96,64},{112,80},{64,96},{80,112},{3... | collective-permute-start | bytes 786440 | tf_op jit(solution)/shard_map/ppermute | solution.py:238
  254.1 11.3 %collective-permute-start.29 = (bf16[1024,128]{1,0:T(8,128)(2,1)S(1)}, bf16[1024,128]{1,0:T(8,128)(2,1)S(1)}, u32[]{:S(2)}, u32[]{:S(2)}) collective-permute-start(bf16[1024,128]{1,0:T(8,128)(2,1)S(1)} %get-tuple-element.45), channel_id=1, source_target_pairs={{16,0},{32,16},{48,32},{0,48},{80,64},{96,80},{112,96},{64,112},{1... | collective-permute-start | bytes 786440 | tf_op jit(solution)/shard_map/ppermute | solution.py:238
  (21 other events, 107.3 us)
Sparse Core Ops, SparseCore 0:
  9.7 55.7 all-gather.1

commit v3 on v2

--- a/solution.py
+++ b/solution.py
@@ -14,18 +14,49 @@
 COL = ("zh", "x")
 VMEM_LIMIT = 58 * 2**20
 PARTS = 2
-BATCH = 16
-CHUNK = 32
-
-
-def sweep_kernel(plan, transpose, batch, chunk, *refs):
-    source_plan, result_plan, slab = plan
+BATCH = 48
+CHUNK = 48
+
+
+def accumulate(source_buf, tile_buf, total, src, dst, contract, batch, base):
+    size = tile_buf.shape[1]
+    products = []
+    for lane in range(batch):
+        start = pl.multiple_of(src[base + lane] * size, size)
+        products.append(
+            lax.dot_general(
+                tile_buf[base + lane],
+                source_buf[pl.ds(start, size), :],
+                contract,
+                preferred_element_type=F32,
+            )
+        )
+    for lane in range(batch):
+        span = pl.ds(pl.multiple_of(dst[base + lane] * size, size), size)
+        total[span, :] = total[span, :] + products[lane]
+
+
+def source_copies_of(sources, source_plan, source_buf, source_sems, slab):
+    half = source_buf.shape[1] // PARTS
+    copies = []
+    for source, places in zip(sources, source_plan):
+        for offset, place, number, part in places:
+            copies.append(
+                pltpu.make_async_copy(
+                    source.at[pl.ds(offset * slab, number * slab)],
+                    source_buf.at[pl.ds(place * slab, number * slab), pl.ds(part * half, half)],
+                    source_sems.at[len(copies)],
+                )
+            )
+    return copies
+
+
+def forward_kernel(source_plan, result_plan, slab, batch, chunk, *refs):
     pieces, outputs = len(source_plan), len(result_plan)
     count, src, dst, tiles = refs[:4]
     sources = refs[4 : 4 + pieces]
     results = refs[4 + pieces : 4 + pieces + outputs]
-    tile_buf, source_buf, total, tile_sems, source_sem = refs[4 + pieces + outputs :]
-    size = tile_buf.shape[1]
+    tile_buf, source_buf, total, stage, tile_sems, source_sems, result_sems = refs[4 + pieces + outputs :]
     live = count[0]
     chunks = (live + chunk - 1) // chunk
 
@@ -33,16 +64,7 @@
         span = pl.ds(index * chunk, chunk)
         return pltpu.make_async_copy(tiles.at[span], tile_buf.at[span], tile_sems.at[index])
 
-    source_copies = []
-    for source, places in zip(sources, source_plan):
-        for offset, place, slabs, column in places:
-            source_copies.append(
-                pltpu.make_async_copy(
-                    source.at[pl.ds(offset * slab, slabs * slab)],
-                    source_buf.at[pl.ds(place * slab, slabs * slab), pl.ds(column, source.shape[1])],
-                    source_sem.at[len(source_copies)],
-                )
-            )
+    source_copies = source_copies_of(sources, source_plan, source_buf, source_sems, slab)
 
     def start_tiles(index, carry):
         tile_copy(index).start()
@@ -56,80 +78,183 @@
     for copy in source_copies:
         copy.wait()
 
-    contract = (((0,), (0,)), ((), ())) if transpose else (((1,), (0,)), ((), ()))
-
     def on_chunk(index, carry):
         tile_copy(index).wait()
 
         def on_batch(step, inner):
             base = index * chunk + step * batch
-            products = []
-            for lane in range(batch):
-                start = pl.multiple_of(src[base + lane] * size, size)
-                products.append(
-                    lax.dot_general(
-                        tile_buf[base + lane],
-                        source_buf[pl.ds(start, size), :],
-                        contract,
-                        preferred_element_type=F32,
-                    )
-                )
-            for lane in range(batch):
-                start = pl.multiple_of(dst[base + lane] * size, size)
-                span = pl.ds(start, size)
-                total[span, :] = total[span, :] + products[lane]
+            accumulate(
+                source_buf, tile_buf, total, src, dst, (((1,), (0,)), ((), ())), batch, base
+            )
             return inner
 
         steps = jnp.minimum(chunk // batch, (live - index * chunk + batch - 1) // batch)
         return lax.fori_loop(0, steps, on_batch, carry)
 
     lax.fori_loop(0, chunks, on_chunk, 0)
-    for result, (slabs, column) in zip(results, result_plan):
-        for index, place in enumerate(slabs):
-            result[index * slab : (index + 1) * slab, :] = total[
-                place * slab : (place + 1) * slab, column : column + result.shape[1]
-            ].astype(result.dtype)
-
-
-def sweep(name, count, src, dst, tiles, sources, source_plan, result_plan, result_types, slab, width, transpose):
+    copies = []
+    for place in range(stage.shape[0] // slab):
+        rows = slice(place * slab, (place + 1) * slab)
+        stage[rows, :] = total[rows, :].astype(BF16)
+        for result, (held, column) in zip(results, result_plan):
+            if place in held:
+                copy = pltpu.make_async_copy(
+                    stage.at[pl.ds(place * slab, slab), pl.ds(column, result.shape[1])],
+                    result.at[pl.ds(held.index(place) * slab, slab)],
+                    result_sems.at[len(copies)],
+                )
+                copy.start()
+                copies.append(copy)
+    for copy in copies:
+        copy.wait()
+
+
+def forward_sweep(count, src, dst, tiles, sources, source_plan, result_plan, slab, width):
     slots, size, _ = tiles.shape
     part_width = width // PARTS
     source_slabs = max(p + n for places in source_plan for _, p, n, _ in places)
+    source_copies = sum(len(places) for places in source_plan)
     result_slabs = max(max(slabs) for slabs, _ in result_plan) + 1
+    copies = sum(len(slabs) for slabs, _ in result_plan)
+    chunk = min(CHUNK, slots)
+    batch = min(BATCH, chunk)
+    any_spec = pl.BlockSpec(memory_space=pl.ANY)
+    return pl.pallas_call(
+        functools.partial(forward_kernel, source_plan, result_plan, slab, batch, chunk),
+        grid_spec=pltpu.PrefetchScalarGridSpec(
+            num_scalar_prefetch=3,
+            grid=(1,),
+            in_specs=[any_spec] * (1 + len(sources)),
+            out_specs=[any_spec] * len(result_plan),
+            scratch_shapes=[
+                pltpu.VMEM(tiles.shape, BF16),
+                pltpu.VMEM((source_slabs * slab, width), BF16),
+                pltpu.VMEM((result_slabs * slab + size, width), F32),
+                pltpu.VMEM((result_slabs * slab, width), BF16),
+                pltpu.SemaphoreType.DMA((slots // chunk,)),
+                pltpu.SemaphoreType.DMA((source_copies,)),
+                pltpu.SemaphoreType.DMA((copies,)),
+            ],
+        ),
+        out_shape=[
+            jax.ShapeDtypeStruct((len(slabs) * slab, part_width), BF16) for slabs, _ in result_plan
+        ],
+        compiler_params=pltpu.CompilerParams(vmem_limit_bytes=VMEM_LIMIT),
+        cost_estimate=pl.CostEstimate(flops=1024, bytes_accessed=1024, transcendentals=0),
+        name="forward",
+    )(count, src, dst, tiles, *sources)
+
+
+def backward_kernel(source_plan, slab, batch, chunk, *refs):
+    pieces = len(source_plan)
+    count, src, dst, slab_at, tiles = refs[:5]
+    sources = refs[5 : 5 + pieces]
+    results = refs[5 + pieces : 9 + pieces]
+    tile_buf, source_buf, total, stage, tile_sems, source_sems, result_sems = refs[9 + pieces :]
+    live = count[0]
+    chunks = (live + chunk - 1) // chunk
+    slabs = stage.shape[0] // slab
+    per_slab = slab // tile_buf.shape[1]
+    half = results[0].shape[1]
+
+    def tile_copy(index):
+        span = pl.ds(index * chunk, chunk)
+        return pltpu.make_async_copy(tiles.at[span], tile_buf.at[span], tile_sems.at[index])
+
+    source_copies = source_copies_of(sources, source_plan, source_buf, source_sems, slab)
+
+    def start_tiles(index, carry):
+        tile_copy(index).start()
+        return carry
+
+    start_tiles(0, 0)
+    for copy in source_copies:
+        copy.start()
+    lax.fori_loop(1, chunks, start_tiles, 0)
+    total[...] = jnp.zeros_like(total)
+    for copy in source_copies:
+        copy.wait()
+
+    def result_copy(result, place, at, part):
+        return pltpu.make_async_copy(
+            stage.at[pl.ds(pl.multiple_of(place * slab, slab), slab), pl.ds(part * half, half)],
+            result.at[pl.ds(pl.multiple_of(at * slab, slab), slab)],
+            result_sems.at[place, part],
+        )
+
+    def flush(place, carry):
+        rows = pl.ds(pl.multiple_of(place * slab, slab), slab)
+        stage[rows, :] = total[rows, :].astype(BF16)
+        offset = slab_at[place]
+        at = offset % 8
+        ring_at = (at % 4) * 2 + at // 4
+
+        @pl.when(offset < 8)
+        def _():
+            result_copy(results[0], place, ring_at, 0).start()
+            result_copy(results[1], place, at, 1).start()
+
+        @pl.when(offset >= 8)
+        def _():
+            result_copy(results[2], place, ring_at, 0).start()
+            result_copy(results[3], place, at, 1).start()
+
+        return carry
+
+    def on_chunk(index, flushed):
+        tile_copy(index).wait()
+
+        def on_batch(step, inner):
+            base = index * chunk + step * batch
+            accumulate(
+                source_buf, tile_buf, total, src, dst, (((0,), (0,)), ((), ())), batch, base
+            )
+            return inner
+
+        steps = jnp.minimum(chunk // batch, (live - index * chunk + batch - 1) // batch)
+        lax.fori_loop(0, steps, on_batch, 0)
+        last = jnp.minimum((index + 1) * chunk, live) - 1
+        ready = jnp.where(index + 1 == chunks, slabs, dst[last] // per_slab)
+        lax.fori_loop(flushed, ready, flush, 0)
+        return ready
+
+    lax.fori_loop(0, chunks, on_chunk, 0)
+    for place in range(slabs):
+        for part in range(2):
+            result_copy(results[part], place, 0, part).wait()
+
+
+def backward_sweep(count, src, dst, slab_at, tiles, sources, source_plan, slab, width):
+    slots, size, _ = tiles.shape
+    part_width = width // PARTS
+    source_slabs = max(p + n for places in source_plan for _, p, n, _ in places)
+    slabs = slab_at.shape[0]
     copies = sum(len(places) for places in source_plan)
     chunk = min(CHUNK, slots)
     batch = min(BATCH, chunk)
     any_spec = pl.BlockSpec(memory_space=pl.ANY)
-    out_shapes = [
-        jax.ShapeDtypeStruct((len(slabs) * slab, part_width), kind)
-        for (slabs, _), kind in zip(result_plan, result_types)
-    ]
-    moved, flops = 1024, 1024
     return pl.pallas_call(
-        functools.partial(sweep_kernel, (source_plan, result_plan, slab), transpose, batch, chunk),
+        functools.partial(backward_kernel, source_plan, slab, batch, chunk),
         grid_spec=pltpu.PrefetchScalarGridSpec(
-            num_scalar_prefetch=3,
+            num_scalar_prefetch=4,
             grid=(1,),
             in_specs=[any_spec] * (1 + len(sources)),
-            out_specs=[
-                pl.BlockSpec(s.shape, lambda i, *_: (0, 0), pipeline_mode=pl.Buffered(1))
-                for s in out_shapes
-            ],
+            out_specs=[any_spec] * 4,
             scratch_shapes=[
                 pltpu.VMEM(tiles.shape, BF16),
                 pltpu.VMEM((source_slabs * slab, width), BF16),
-                pltpu.VMEM((result_slabs * slab + size, width), F32),
+                pltpu.VMEM((slabs * slab + size, width), F32),
+                pltpu.VMEM((slabs * slab, width), BF16),
                 pltpu.SemaphoreType.DMA((slots // chunk,)),
                 pltpu.SemaphoreType.DMA((copies,)),
+                pltpu.SemaphoreType.DMA((slabs, 2)),
             ],
         ),
-        out_shape=out_shapes,
+        out_shape=[jax.ShapeDtypeStruct((slabs // 2 * slab, part_width), BF16)] * 4,
         compiler_params=pltpu.CompilerParams(vmem_limit_bytes=VMEM_LIMIT),
-        cost_estimate=pl.CostEstimate(
-            flops=flops, bytes_accessed=moved, transcendentals=0
-        ),
-        name=name,
-    )(count, src, dst, tiles, *sources)
+        cost_estimate=pl.CostEstimate(flops=1024, bytes_accessed=1024, transcendentals=0),
+        name="backward",
+    )(count, src, dst, slab_at, tiles, *sources)
 
 
 def split_dot(left, right, contract):
@@ -166,7 +291,9 @@
     width = grad.shape[1] // parts
     for part in range(parts):
         grads[part][...] = grad[:, part * width : (part + 1) * width]
-    term = split_dot(gathered, grad, (((0,), (0,)), ((), ())))
+    term = lax.dot_general(
+        gathered.astype(BF16), grad, (((0,), (0,)), ((), ())), preferred_element_type=F32
+    )
 
     @pl.when(pl.program_id(0) == 0)
     def _():
@@ -264,43 +391,51 @@
 
 
 def join_kernel(first, first_pair, *refs):
-    ring, terms = refs[:4], refs[4:8]
-    pair, both, total = refs[8:]
+    ring = refs[:4]
+    pair, both = refs[4:]
     nodes = first.shape[0]
     pair[:nodes, :] = first[...]
     pair[nodes:, :] = first_pair[...]
     for index, piece in enumerate(ring):
         both[index * nodes : (index + 1) * nodes, :] = piece[...]
-    total[...] = (terms[0][...] + terms[1][...]) + (terms[2][...] + terms[3][...])
-
-
-def join(first, first_pair, ring, terms):
+
+
+def join(first, first_pair, ring):
     nodes, width = first.shape
     return pl.pallas_call(
         join_kernel,
         out_shape=[
             jax.ShapeDtypeStruct((2 * nodes, width), BF16),
             jax.ShapeDtypeStruct((4 * nodes, width), BF16),
-            jax.ShapeDtypeStruct(terms[0].shape, F32),
         ],
         compiler_params=pltpu.CompilerParams(vmem_limit_bytes=VMEM_LIMIT),
         cost_estimate=pl.CostEstimate(flops=1024, bytes_accessed=1024, transcendentals=0),
         name="join",
-    )(first, first_pair, *ring, *terms)
+    )(first, first_pair, *ring)
 
 
 def around(value, axes, sizes, offsets):
     return [value] + [shift(value, axes, sizes, offset) for offset in offsets]
 
 
+def gather(first, second, axes):
+    ring_steps = [(0, 1), (0, 2), (0, 3)]
+    first_pair = shift(first, axes, (2, 4), (1, 0))
+    ring = around(second, axes, (2, 4), ring_steps)
+    pair, both = join(first, first_pair, ring)
+    later = [shift(pair, axes, (2, 4), step) for step in ring_steps]
+    return [pair, both], later + [shift(both, axes, (2, 4), (1, 0))]
+
+
 RING_FIRST = [[dr, 4 + dr] for dr in range(4)]
 PAIR_FIRST = [[0, 1, 2, 3], [4, 5, 6, 7]]
-GATHERED_PAIR_FIRST = [[(0, dr, 1), (1, 4 + dr, 1)] for dr in range(4)]
-GATHERED_RING_FIRST = [[(0, dr, 1)] for dr in range(4)] + [[(0, 4, 4)]]
-
-
-def at_column(plan, column):
-    return [[(*place, column) for place in places] for places in plan]
+GATHERED = [
+    [(0, 0, 1, 0), (1, 4, 1, 0)],
+    [(0, 0, 4, 1)],
+    *[[(0, dr, 1, 0), (1, 4 + dr, 1, 0)] for dr in range(1, 4)],
+    [(0, 4, 4, 1)],
+]
+OTHER_CORE = [[(at, held + 8, slabs, half) for at, held, slabs, half in places] for places in GATHERED]
 
 
 def on_device(
@@ -317,40 +452,31 @@
     row_axes, col_axes = ("zl", "y"), ("zh", "x")
 
     row_ids, col_ids = tile_rows[0, 0], tile_cols[0, 0]
-    row_slab, col_slab = row_ids // per_slab, col_ids // per_slab
+    row_slab = row_ids // per_slab
     row_at = (((row_slab // 4) ^ zh) * 4 + (row_slab % 4 - x) % 4) * per_slab + row_ids % per_slab
-    col_at = (
+    every = jnp.arange(16, dtype=jnp.int32)
+    slab_at = (((every // 8) ^ zl) * 4 + (every // 2 % 4 - y) % 4) + ((every % 2) ^ core) * 8
+    live = jnp.arange(slots, dtype=jnp.int32) < count[0]
+    row_to = jnp.where(live, row_at, 8 * per_slab)
+    col_slab = col_ids // per_slab
+    col_from = (
         (((col_slab // 8) ^ zl) * 4 + (col_slab // 2 % 4 - y) % 4) + ((col_slab % 2) ^ core) * 8
     ) * per_slab + col_ids % per_slab
-    live = jnp.arange(slots, dtype=jnp.int32) < count[0]
-    row_to = jnp.where(live, row_at, 8 * per_slab)
-    col_to = jnp.where(live, col_at, 16 * per_slab)
-
-    whole = lax.all_gather(features, ROW, axis=0, tiled=True)
+    col_to = jnp.where(live, col_ids, 16 * per_slab)
+
+    early, later = gather(features[:, :part_width], features[:, part_width:], row_axes)
+    others = [shift(piece, "core", (2,), (1,)) for piece in early + later]
     plan = [(slabs, 0) for slabs in RING_FIRST] + [(slabs, part_width) for slabs in PAIR_FIRST]
-    held = sweep(
-        "forward", count, col_ids, row_to, tiles, [whole], [[(0, 0, 16, 0)]],
-        plan, [BF16] * len(plan), nodes, width, False,
+    held = forward_sweep(
+        count, col_from, row_to, tiles, early + later + others, GATHERED + OTHER_CORE, plan, nodes, width
     )
     arrived = scatter_ring_first(held[:4], col_axes) + scatter_pair_first(held[4:], col_axes)
     activations, first, second, weight_term = middle(arrived, weight, layer_bias, cotangent, PARTS)
 
-    ring_steps = [(0, 1), (0, 2), (0, 3)]
-    first_pair = shift(first, col_axes, (2, 4), (1, 0))
-    ring = around(second, col_axes, (2, 4), ring_steps)
-    terms = around(weight_term, row_axes, (2, 4), ring_steps)
-    pair, both, weight_sum = join(first, first_pair, ring, terms)
-    gathered = around(pair, col_axes, (2, 4), ring_steps) + ring
-    gathered.append(shift(both, col_axes, (2, 4), (1, 0)))
-    weight_sum = add(*around(weight_sum, "core", (2,), [(1,)]))
-
-    order = [[slab for slabs in plan for slab in slabs] for plan in (RING_FIRST, PAIR_FIRST)]
-    results = sweep(
-        "backward", count, row_at, col_to, tiles, gathered + [weight_sum],
-        at_column(GATHERED_PAIR_FIRST, 0) + at_column(GATHERED_RING_FIRST, part_width) + [[]],
-        [(slabs, part * part_width) for part, slabs in enumerate(order)]
-        + [([8 + slab for slab in slabs], part * part_width) for part, slabs in enumerate(order)],
-        [F32, F32, BF16, BF16], nodes, width, True,
+    early, later = gather(first, second, col_axes)
+    weight_sum = add(*around(weight_term, row_axes, (2, 4), [(0, 1), (0, 2), (0, 3)]))
+    results = backward_sweep(
+        count, row_at, col_to, slab_at, tiles, early + later + [weight_sum], GATHERED + [[]], nodes, width
     )
     collected = []
     for part, plan in enumerate((RING_FIRST, PAIR_FIRST)):
@@ -365,6 +491,7 @@
         collected += scatter(held, row_axes)
     grad_features = final(collected, weight, PARTS)
     weight_sum = add(*around(weight_sum, "x", (4,), [(1,), (2,), (3,)]))
+    weight_sum = add(*around(weight_sum, "core", (2,), [(1,)]))
     grad_weight = add(*around(weight_sum, ("zl", "zh"), (2, 2), [(0, 1), (1, 0), (1, 1)]))
     total_nodes = nodes * 128
     return activations, grad_features, grad_weight * float(total_nodes) ** -0.5

time: 281 us -> 254 us (0.904)
  waiting for transfers between devices: 155 us -> 132 us
  between operations: 15 us -> 1.62 us
  starting transfers between devices: 56.9 us -> 65.6 us
    all_gather x1 -> x0, waiting for transfers between devices: 54.4 us -> none  [on_device(): whole = lax.all_gather(features, ROW, axis=0, tiled=True)]
    ppermute x36 -> x50, waiting for transfers between devices: 99.4 us -> 132 us  [shift(): return lax.ppermute(value, axes, perm)]
    ppermute x36 -> x50, starting transfers between devices: 56.9 us -> 65.6 us  [shift(): return lax.ppermute(value, axes, perm)]
    pallas_call x2, Pallas kernels: 22.6 us -> 19.3 us  [the longest x1 10.1 us: forward_sweep(): pl.pallas_call(functools.partial(forward_kernel, source_plan, result_plan...]
    unnamed x64 -> x78, local copies, waits for them, and re-layouts: 4.22 us -> 5.75 us
  transfers between devices with their start and end apart: 37 -> 50, of which waited for: 19 -> 30; matrix products, arithmetic and copies ran while one was open for 4% -> 4% of each run, Pallas kernels for 0% -> 0%
where the time goes in v3:
time: 254 us; the launch traced here: 249 us
  waiting for transfers between devices  132 us (52%)
  starting transfers between devices  65.6 us (26%)
  Pallas kernels  33.7 us (13%)
  other arithmetic  9.87 us (4%)
  local copies, waits for them, and re-layouts  6.83 us (3%)
    ppermute x50, waiting for transfers between devices, shift(): return lax.ppermute(value, axes, perm)  132 us
    ppermute x50, starting transfers between devices, shift(): return lax.ppermute(value, axes, perm)  65.6 us
    pallas_call x1, Pallas kernels, forward_sweep(): pl.pallas_call(functools.partial(forward_kernel, source_plan, result_plan...  10.1 us
    pallas_call x1, Pallas kernels, backward_sweep(): pl.pallas_call(functools.partial(backward_kernel, source_plan, slab, batc...  9.26 us
    unnamed x78, local copies, waits for them, and re-layouts  5.75 us
    pallas_call x1, Pallas kernels, middle(): pl.pallas_call(functools.partial(middle_kernel, parts, len(pieces)), grid...  5.13 us
  transfers between devices with their start and end apart: 50, of which 30 were waited for; matrix products, arithmetic and copies ran while one was open for 4% of the time, Pallas kernels for 0%

profile of v3, /device:TPU:1, one launch (start us, length us, event | category | flops | bytes accessed | tf_op | source)
XLA Modules:
  0.0 249.2 jit_solution(11587312285015396589)
XLA Ops:
  1.8 2.5 %collective-permute-start = (bf16[1024,128]{1,0:T(8,128)(2,1)S(1)}, bf16[1024,128]{1,0:T(8,128)(2,1)S(1)}, u32[]{:S(2)}, u32[]{:S(2)}) collective-permute-start(bf16[1024,128]{1,0:T(8,128)(2,1)S(1)} %get-tuple-element.54.first), channel_id=1, source_target_pairs={{64,0},{80,16},{96,32},{112,48},{0,64},{16,80},{32,96},{48,112},{6... | collective-permute-start | bytes 786440 | tf_op jit(solution)/shard_map/ppermute | solution.py:365
  4.3 2.7 %collective-permute-start.1 = (bf16[1024,128]{1,0:T(8,128)(2,1)S(1)}, bf16[1024,128]{1,0:T(8,128)(2,1)S(1)}, u32[]{:S(2)}, u32[]{:S(2)}) collective-permute-start(bf16[1024,128]{1,0:T(8,128)(2,1)S(1)} %get-tuple-element.53.refs_0_), channel_id=1, source_target_pairs={{16,0},{32,16},{48,32},{0,48},{80,64},{96,80},{112,96},{64,112},{1... | collective-permute-start | bytes 786440 | tf_op jit(solution)/shard_map/ppermute | solution.py:365
  8.1 2.2 collective-permute-done.first_pair
  10.3 2.4 collective-permute-done.1.refs_1_
  12.7 2.4 collective-permute-done.2.refs_2_
  15.2 7.2 %collective-permute-done.3.refs_3_ = bf16[1024,128]{1,0:T(8,128)(2,1)S(1)} collective-permute-done((bf16[1024,128]{1,0:T(8,128)(2,1)S(1)}, bf16[1024,128]{1,0:T(8,128)(2,1)S(1)}, u32[]{:S(2)}, u32[]{:S(2)}) %collective-permute-start.3) | collective-permute-done | bytes 262176 | tf_op jit(solution)/shard_map/ppermute | solution.py:365
  23.1 2.5 %join.2 = (bf16[2048,128]{1,0:T(8,128)(2,1)}, bf16[4096,128]{1,0:T(8,128)(2,1)}) custom-call(bf16[1024,128]{1,0:T(8,128)(2,1)} %copy-done.17, bf16[1024,128]{1,0:T(8,128)(2,1)} %copy-done.29, bf16[1024,128]{1,0:T(8,128)(2,1)} %copy-done.16, bf16[1024,128]{1,0:T(8,128)(2,1)} %copy-done.31, bf16[1024,128]{1,0:T(8,128)(2,1)} %copy-done.33, ...), custom_call_target="tpu_custom_call" | custom-call | flops 1024 | bytes 1024 | tf_op jit(solution)/shard_map/join/pallas_call | solution.py:405
  28.6 10.2 %collective-permute-done.4.refs_6_ = bf16[2048,128]{1,0:T(8,128)(2,1)} collective-permute-done((bf16[2048,128]{1,0:T(8,128)(2,1)}, bf16[2048,128]{1,0:T(8,128)(2,1)}, u32[]{:S(2)}, u32[]{:S(2)}) %collective-permute-start.4) | collective-permute-done | bytes 524320 | tf_op jit(solution)/shard_map/ppermute | solution.py:365
  38.7 2.9 %collective-permute-start.8 = (bf16[2048,128]{1,0:T(8,128)(2,1)}, bf16[2048,128]{1,0:T(8,128)(2,1)}, u32[]{:S(2)}, u32[]{:S(2)}) collective-permute-start(bf16[2048,128]{1,0:T(8,128)(2,1)} %get-tuple-element.21.refs_4_), channel_id=1, source_target_pairs={{8,0},{0,8},{9,1},{1,9},{10,2},{2,10},{11,3},{3,11},{12,4},{4,12},... | collective-permute-start | bytes 1572872 | tf_op jit(solution)/shard_map/ppermute | solution.py:365
  41.7 8.6 %collective-permute-done.7.refs_9_ = bf16[4096,128]{1,0:T(8,128)(2,1)S(1)} collective-permute-done((bf16[4096,128]{1,0:T(8,128)(2,1)}, bf16[4096,128]{1,0:T(8,128)(2,1)S(1)}, u32[]{:S(2)}, u32[]{:S(2)}) %collective-permute-start.7) | collective-permute-done | bytes 1048608 | tf_op jit(solution)/shard_map/ppermute | solution.py:365
  57.3 10.1 %forward.1 = (bf16[2048,128]{1,0:T(8,128)(2,1)}, bf16[2048,128]{1,0:T(8,128)(2,1)}, bf16[2048,128]{1,0:T(8,128)(2,1)}, bf16[2048,128]{1,0:T(8,128)(2,1)}, bf16[4...) custom-call(s32[1]{0:T(128)} %bitcast.4.refs_0_, s32[384]{0:T(512)} %get-tuple-element.56.refs_1_, ...), custom_call_target="tpu_custom_call" | custom-call | flops 1024 | bytes 1024 | tf_op jit(solution)/shard_map/forward/pallas_call | solution.py:122
  67.4 2.4 collective-permute-start.18
  70.9 5.3 %collective-permute-start.15 = (bf16[2048,128]{1,0:T(8,128)(2,1)}, bf16[2048,128]{1,0:T(8,128)(2,1)S(1)}, u32[]{:S(2)}, u32[]{:S(2)}) collective-permute-start(bf16[2048,128]{1,0:T(8,128)(2,1)} %get-tuple-element.25), channel_id=1, source_target_pairs={{2,0},{3,1},{0,2},{1,3},{6,4},{7,5},{4,6},{5,7},{10,8},{11,9},{8,1... | collective-permute-start | bytes 1572872 | tf_op jit(solution)/shard_map/ppermute | solution.py:365
  76.2 12.8 %collective-permute-done.14.refs_1_ = bf16[2048,128]{1,0:T(8,128)(2,1)S(1)} collective-permute-done((bf16[2048,128]{1,0:T(8,128)(2,1)}, bf16[2048,128]{1,0:T(8,128)(2,1)S(1)}, u32[]{:S(2)}, u32[]{:S(2)}) %collective-permute-start.14) | collective-permute-done | bytes 524320 | tf_op jit(solution)/shard_map/ppermute | solution.py:365
  89.0 8.2 %collective-permute-done.15.refs_2_ = bf16[2048,128]{1,0:T(8,128)(2,1)S(1)} collective-permute-done((bf16[2048,128]{1,0:T(8,128)(2,1)}, bf16[2048,128]{1,0:T(8,128)(2,1)S(1)}, u32[]{:S(2)}, u32[]{:S(2)}) %collective-permute-start.15) | collective-permute-done | bytes 524320 | tf_op jit(solution)/shard_map/ppermute | solution.py:365
  99.3 1.8 collective-permute-start.17
  101.1 1.7 add_convert_fusion.10
  104.1 2.4 collective-permute-start.20
  106.7 2.4 collective-permute-done.17.refs_4_
  109.0 2.7 %collective-permute-done.19.refs_7_ = bf16[1024,128]{1,0:T(8,128)(2,1)S(1)} collective-permute-done((bf16[1024,128]{1,0:T(8,128)(2,1)S(1)}, bf16[1024,128]{1,0:T(8,128)(2,1)S(1)}, u32[]{:S(2)}, u32[]{:S(2)}) %collective-permute-start.19) | collective-permute-done | bytes 262176 | tf_op jit(solution)/shard_map/ppermute | solution.py:365
  111.7 6.2 %collective-permute-done.20.refs_8_ = bf16[1024,128]{1,0:T(8,128)(2,1)S(1)} collective-permute-done((bf16[1024,128]{1,0:T(8,128)(2,1)S(1)}, bf16[1024,128]{1,0:T(8,128)(2,1)S(1)}, u32[]{:S(2)}, u32[]{:S(2)}) %collective-permute-start.20) | collective-permute-done | bytes 262176 | tf_op jit(solution)/shard_map/ppermute | solution.py:365
  118.7 5.1 %middle.1 = (bf16[1024,256]{1,0:T(8,128)(2,1)}, bf16[1024,128]{1,0:T(8,128)(2,1)}, bf16[1024,128]{1,0:T(8,128)(2,1)}, f32[256,256]{1,0:T(8,128)}) custom-call(bf16[2048,128]{1,0:T(8,128)(2,1)} %get-tuple-element.23.refs_0_, bf16[2048,128]{1,0:T(8,128)(2,1)} %copy-done.9, bf16[2048,128]{1,0:T(8,128)(2,1)} %copy-done.10, bf16[2048,128]{1,0:T(8,128)(2,1)} %copy-done.11, ...), custom_call_target="tpu_custom_call" | custom-call | tf_op jit(solution)/shard_map/middle/pallas_call | solution.py:312
  125.3 2.8 %collective-permute-start.23 = (bf16[1024,128]{1,0:T(8,128)(2,1)}, bf16[1024,128]{1,0:T(8,128)(2,1)S(1)}, u32[]{:S(2)}, u32[]{:S(2)}) collective-permute-start(bf16[1024,128]{1,0:T(8,128)(2,1)} %get-tuple-element.31.refs_0_), channel_id=1, source_target_pairs={{1,0},{2,1},{3,2},{0,3},{5,4},{6,5},{7,6},{4,7},{9,8},{10,9},{11,1... | collective-permute-start | bytes 786440 | tf_op jit(solution)/shard_map/ppermute | solution.py:365
  128.8 3.1 %collective-permute-done.22.first_pair = bf16[1024,128]{1,0:T(8,128)(2,1)S(1)} collective-permute-done((bf16[1024,128]{1,0:T(8,128)(2,1)}, bf16[1024,128]{1,0:T(8,128)(2,1)S(1)}, u32[]{:S(2)}, u32[]{:S(2)}) %collective-permute-start.22) | collective-permute-done | bytes 262176 | tf_op jit(solution)/shard_map/ppermute | solution.py:365
  131.9 3.2 %collective-permute-done.23.refs_1_ = bf16[1024,128]{1,0:T(8,128)(2,1)S(1)} collective-permute-done((bf16[1024,128]{1,0:T(8,128)(2,1)}, bf16[1024,128]{1,0:T(8,128)(2,1)S(1)}, u32[]{:S(2)}, u32[]{:S(2)}) %collective-permute-start.23) | collective-permute-done | bytes 262176 | tf_op jit(solution)/shard_map/ppermute | solution.py:365
  136.6 7.1 %collective-permute-done.25.refs_3_ = bf16[1024,128]{1,0:T(8,128)(2,1)S(1)} collective-permute-done((bf16[1024,128]{1,0:T(8,128)(2,1)}, bf16[1024,128]{1,0:T(8,128)(2,1)S(1)}, u32[]{:S(2)}, u32[]{:S(2)}) %collective-permute-start.25) | collective-permute-done | bytes 262176 | tf_op jit(solution)/shard_map/ppermute | solution.py:365
  144.4 2.5 %join.3 = (bf16[2048,128]{1,0:T(8,128)(2,1)}, bf16[4096,128]{1,0:T(8,128)(2,1)}) custom-call(bf16[1024,128]{1,0:T(8,128)(2,1)} %get-tuple-element.30.first, bf16[1024,128]{1,0:T(8,128)(2,1)} %copy-done.30, bf16[1024,128]{1,0:T(8,128)(2,1)} %get-tuple-element.31.refs_0_, bf16[1024,128]{1,0:T(8,128)(2,1)} %copy-done.32, bf16[1024,128]{1,0:T(8,128)(2,1)} %copy-done.34, ...), custom_call_target="tpu_custom_call" | custom-call | flops 1024 | bytes 1024 | tf_op jit(solution)/shard_map/join/pallas_call | solution.py:405
  147.0 1.6 collective-permute-start.29
  150.5 7.9 %collective-permute-done.32 = f32[256,256]{1,0:T(8,128)S(1)} collective-permute-done((f32[256,256]{1,0:T(8,128)}, f32[256,256]{1,0:T(8,128)S(1)}, u32[]{:S(2)}, u32[]{:S(2)}) %collective-permute-start.32) | collective-permute-done | bytes 262176 | tf_op jit(solution)/shard_map/ppermute | solution.py:365
  158.4 3.1 %collective-permute-done.31 = f32[256,256]{1,0:T(8,128)S(1)} collective-permute-done((f32[256,256]{1,0:T(8,128)}, f32[256,256]{1,0:T(8,128)S(1)}, u32[]{:S(2)}, u32[]{:S(2)}) %collective-permute-start.31) | collective-permute-done | bytes 262176 | tf_op jit(solution)/shard_map/ppermute | solution.py:365
  162.0 5.2 %collective-permute-done.30 = f32[256,256]{1,0:T(8,128)S(1)} collective-permute-done((f32[256,256]{1,0:T(8,128)}, f32[256,256]{1,0:T(8,128)S(1)}, u32[]{:S(2)}, u32[]{:S(2)}) %collective-permute-start.30) | collective-permute-done | bytes 262176 | tf_op jit(solution)/shard_map/ppermute | solution.py:365
  167.2 1.7 add_add_fusion.1.refs_11_
  168.9 4.6 %collective-permute-done.28.refs_9_ = bf16[2048,128]{1,0:T(8,128)(2,1)S(1)} collective-permute-done((bf16[2048,128]{1,0:T(8,128)(2,1)}, bf16[2048,128]{1,0:T(8,128)(2,1)S(1)}, u32[]{:S(2)}, u32[]{:S(2)}) %collective-permute-start.28) | collective-permute-done | bytes 524320 | tf_op jit(solution)/shard_map/ppermute | solution.py:365
  174.7 9.3 %backward.1 = (bf16[8192,128]{1,0:T(8,128)(2,1)}, bf16[8192,128]{1,0:T(8,128)(2,1)}, bf16[8192,128]{1,0:T(8,128)(2,1)}, bf16[8192,128]{1,0:T(8,128)(2,1)}) custom-call(s32[1]{0:T(128)} %bitcast.5.refs_0_, s32[384]{0:T(512)} %get-tuple-element.58.refs_1_, s32[384]{0:T(512)} %get-tuple-element.55.refs_2_, s32[16]{0:T(128)} %fusion.29.refs_3_, ...), custom_call_target="tpu_custom_call" | custom-call | flops 1024 | bytes 1024 | tf_op jit(solution)/shard_map/backward/pallas_call | solution.py:236
  183.9 4.9 %collective-permute-start.38 = (bf16[8192,128]{1,0:T(8,128)(2,1)}, bf16[8192,128]{1,0:T(8,128)(2,1)S(1)}, u32[]{:S(2)}, u32[]{:S(2)}) collective-permute-start(bf16[8192,128]{1,0:T(8,128)(2,1)} %get-tuple-element.38), channel_id=1, source_target_pairs={{8,0},{0,8},{9,1},{1,9},{10,2},{2,10},{11,3},{3,11},{12,4},{4,12},... | collective-permute-start | bytes 6291464 | tf_op jit(solution)/shard_map/ppermute | solution.py:365
  189.0 4.4 %collective-permute-start.44 = (f32[256,256]{1,0:T(8,128)S(1)}, f32[256,256]{1,0:T(8,128)S(1)}, u32[]{:S(2)}, u32[]{:S(2)}) collective-permute-start(f32[256,256]{1,0:T(8,128)S(1)} %copy-done.4), channel_id=1, source_target_pairs={{2,0},{3,1},{0,2},{1,3},{6,4},{7,5},{4,6},{5,7},{10,8},{11,9},{8,1... | collective-permute-start | bytes 786440 | tf_op jit(solution)/shard_map/ppermute | solution.py:365
  193.3 2.2 add_convert_fusion
  195.6 1.7 collective-permute-start.39
  197.8 2.1 collective-permute-start.34
  199.9 5.4 %collective-permute-done.44 = f32[256,256]{1,0:T(8,128)S(1)} collective-permute-done((f32[256,256]{1,0:T(8,128)S(1)}, f32[256,256]{1,0:T(8,128)S(1)}, u32[]{:S(2)}, u32[]{:S(2)}) %collective-permute-start.44) | collective-permute-done | bytes 262176 | tf_op jit(solution)/shard_map/ppermute | solution.py:365
  209.5 3.4 %collective-permute-start.49 = (f32[256,256]{1,0:T(8,128)S(1)}, f32[256,256]{1,0:T(8,128)S(1)}, u32[]{:S(2)}, u32[]{:S(2)}) collective-permute-start(f32[256,256]{1,0:T(8,128)S(1)} %add.197), channel_id=1, source_target_pairs={{68,0},{64,4},{4,64},{0,68},{69,1},{65,5},{5,65},{1,69},{70,2},{66... | collective-permute-start | bytes 786440 | tf_op jit(solution)/shard_map/ppermute | solution.py:365
  212.9 10.5 %collective-permute-done.34.refs_1_ = bf16[2048,128]{1,0:T(8,128)(2,1)S(1)} collective-permute-done((bf16[2048,128]{1,0:T(8,128)(2,1)S(1)}, bf16[2048,128]{1,0:T(8,128)(2,1)S(1)}, u32[]{:S(2)}, u32[]{:S(2)}) %collective-permute-start.34) | collective-permute-done | bytes 524320 | tf_op jit(solution)/shard_map/ppermute | solution.py:365
  224.4 3.2 %collective-permute-start.47 = (f32[256,256]{1,0:T(8,128)S(1)}, f32[256,256]{1,0:T(8,128)S(1)}, u32[]{:S(2)}, u32[]{:S(2)}) collective-permute-start(f32[256,256]{1,0:T(8,128)S(1)} %add.197), channel_id=1, source_target_pairs={{4,0},{0,4},{68,64},{64,68},{5,1},{1,5},{69,65},{65,69},{6,2},{2,6... | collective-permute-start | bytes 786440 | tf_op jit(solution)/shard_map/ppermute | solution.py:365
  228.7 3.4 %collective-permute-start.41 = (bf16[1024,128]{1,0:T(8,128)(2,1)S(1)}, bf16[1024,128]{1,0:T(8,128)(2,1)S(1)}, u32[]{:S(2)}, u32[]{:S(2)}) collective-permute-start(bf16[1024,128]{1,0:T(8,128)(2,1)S(1)} %get-tuple-element.48), channel_id=1, source_target_pairs={{32,0},{48,16},{0,32},{16,48},{96,64},{112,80},{64,96},{80,112},{3... | collective-permute-start | bytes 786440 | tf_op jit(solution)/shard_map/ppermute | solution.py:365
  233.0 1.7 collective-permute-done.47
  235.4 5.7 %collective-permute-done.37.refs_4_ = bf16[1024,128]{1,0:T(8,128)(2,1)S(1)} collective-permute-done((bf16[1024,128]{1,0:T(8,128)(2,1)S(1)}, bf16[1024,128]{1,0:T(8,128)(2,1)S(1)}, u32[]{:S(2)}, u32[]{:S(2)}) %collective-permute-start.37) | collective-permute-done | bytes 262176 | tf_op jit(solution)/shard_map/ppermute | solution.py:365
  241.2 2.4 collective-permute-done.41.refs_8_
  245.1 4.2 %final.1 = bf16[1024,256]{1,0:T(8,128)(2,1)} custom-call(bf16[2048,128]{1,0:T(8,128)(2,1)} %copy-done.1, bf16[2048,128]{1,0:T(8,128)(2,1)} %copy-done.6, bf16[2048,128]{1,0:T(8,128)(2,1)} %copy-done.7, bf16[2048,128]{1,0:T(8,128)(2,1)} %copy-done.8, bf16[1024,128]{1,0:T(8,128)(2,1)} %copy-done.21, bf16[4096,128]{1,0:T(8,128)(2,1)} %copy-done, ...), custom_call_target="tpu_custom_call" | custom-call | tf_op jit(solution)/shard_map/final/pallas_call | solution.py:339
  (151 shorter events, 35.6 us)
Async XLA Ops:
  1.8 8.6 %collective-permute-start = (bf16[1024,128]{1,0:T(8,128)(2,1)S(1)}, bf16[1024,128]{1,0:T(8,128)(2,1)S(1)}, u32[]{:S(2)}, u32[]{:S(2)}) collective-permute-start(bf16[1024,128]{1,0:T(8,128)(2,1)S(1)} %get-tuple-element.54.first), channel_id=1, source_target_pairs={{64,0},{80,16},{96,32},{112,48},{0,64},{16,80},{32,96},{48,112},{6... | collective-permute-start | bytes 786440 | tf_op jit(solution)/shard_map/ppermute | solution.py:365
  4.3 8.4 %collective-permute-start.1 = (bf16[1024,128]{1,0:T(8,128)(2,1)S(1)}, bf16[1024,128]{1,0:T(8,128)(2,1)S(1)}, u32[]{:S(2)}, u32[]{:S(2)}) collective-permute-start(bf16[1024,128]{1,0:T(8,128)(2,1)S(1)} %get-tuple-element.53.refs_0_), channel_id=1, source_target_pairs={{16,0},{32,16},{48,32},{0,48},{80,64},{96,80},{112,96},{64,112},{1... | collective-permute-start | bytes 786440 | tf_op jit(solution)/shard_map/ppermute | solution.py:365
  7.0 8.1 %collective-permute-start.2 = (bf16[1024,128]{1,0:T(8,128)(2,1)S(1)}, bf16[1024,128]{1,0:T(8,128)(2,1)S(1)}, u32[]{:S(2)}, u32[]{:S(2)}) collective-permute-start(bf16[1024,128]{1,0:T(8,128)(2,1)S(1)} %get-tuple-element.53.refs_0_), channel_id=1, source_target_pairs={{32,0},{48,16},{0,32},{16,48},{96,64},{112,80},{64,96},{80,112},{3... | collective-permute-start | bytes 786440 | tf_op jit(solution)/shard_map/ppermute | solution.py:365
  7.4 15.0 %collective-permute-start.3 = (bf16[1024,128]{1,0:T(8,128)(2,1)S(1)}, bf16[1024,128]{1,0:T(8,128)(2,1)S(1)}, u32[]{:S(2)}, u32[]{:S(2)}) collective-permute-start(bf16[1024,128]{1,0:T(8,128)(2,1)S(1)} %get-tuple-element.53.refs_0_), channel_id=1, source_target_pairs={{48,0},{0,16},{16,32},{32,48},{112,64},{64,80},{80,96},{96,112},{4... | collective-permute-start | bytes 786440 | tf_op jit(solution)/shard_map/ppermute | solution.py:365
  25.7 24.6 %collective-permute-start.7 = (bf16[4096,128]{1,0:T(8,128)(2,1)}, bf16[4096,128]{1,0:T(8,128)(2,1)S(1)}, u32[]{:S(2)}, u32[]{:S(2)}) collective-permute-start(bf16[4096,128]{1,0:T(8,128)(2,1)} %get-tuple-element.22.refs_5_), channel_id=1, source_target_pairs={{64,0},{80,16},{96,32},{112,48},{0,64},{16,80},{32,96},{48,112},{6... | collective-permute-start | bytes 3145736 | tf_op jit(solution)/shard_map/ppermute | solution.py:365
  25.7 13.0 %collective-permute-start.4 = (bf16[2048,128]{1,0:T(8,128)(2,1)}, bf16[2048,128]{1,0:T(8,128)(2,1)}, u32[]{:S(2)}, u32[]{:S(2)}) collective-permute-start(bf16[2048,128]{1,0:T(8,128)(2,1)} %get-tuple-element.21.refs_4_), channel_id=1, source_target_pairs={{16,0},{32,16},{48,32},{0,48},{80,64},{96,80},{112,96},{64,112},{1... | collective-permute-start | bytes 1572872 | tf_op jit(solution)/shard_map/ppermute | solution.py:365
  25.7 25.7 %collective-permute-start.5 = (bf16[2048,128]{1,0:T(8,128)(2,1)}, bf16[2048,128]{1,0:T(8,128)(2,1)}, u32[]{:S(2)}, u32[]{:S(2)}) collective-permute-start(bf16[2048,128]{1,0:T(8,128)(2,1)} %get-tuple-element.21.refs_4_), channel_id=1, source_target_pairs={{32,0},{48,16},{0,32},{16,48},{96,64},{112,80},{64,96},{80,112},{3... | collective-permute-start | bytes 1572872 | tf_op jit(solution)/shard_map/ppermute | solution.py:365
  26.1 26.6 %collective-permute-start.6 = (bf16[2048,128]{1,0:T(8,128)(2,1)}, bf16[2048,128]{1,0:T(8,128)(2,1)}, u32[]{:S(2)}, u32[]{:S(2)}) collective-permute-start(bf16[2048,128]{1,0:T(8,128)(2,1)} %get-tuple-element.21.refs_4_), channel_id=1, source_target_pairs={{48,0},{0,16},{16,32},{32,48},{112,64},{64,80},{80,96},{96,112},{4... | collective-permute-start | bytes 1572872 | tf_op jit(solution)/shard_map/ppermute | solution.py:365
  27.2 27.3 %collective-permute-start.9 = (bf16[4096,128]{1,0:T(8,128)(2,1)}, bf16[4096,128]{1,0:T(8,128)(2,1)S(1)}, u32[]{:S(2)}, u32[]{:S(2)}) collective-permute-start(bf16[4096,128]{1,0:T(8,128)(2,1)} %get-tuple-element.22.refs_5_), channel_id=1, source_target_pairs={{8,0},{0,8},{9,1},{1,9},{10,2},{2,10},{11,3},{3,11},{12,4},{4,12},... | collective-permute-start | bytes 3145736 | tf_op jit(solution)/shard_map/ppermute | solution.py:365
  38.7 14.4 %collective-permute-start.8 = (bf16[2048,128]{1,0:T(8,128)(2,1)}, bf16[2048,128]{1,0:T(8,128)(2,1)}, u32[]{:S(2)}, u32[]{:S(2)}) collective-permute-start(bf16[2048,128]{1,0:T(8,128)(2,1)} %get-tuple-element.21.refs_4_), channel_id=1, source_target_pairs={{8,0},{0,8},{9,1},{1,9},{10,2},{2,10},{11,3},{3,11},{12,4},{4,12},... | collective-permute-start | bytes 1572872 | tf_op jit(solution)/shard_map/ppermute | solution.py:365
  50.2 6.1 %collective-permute-start.13 = (bf16[4096,128]{1,0:T(8,128)(2,1)S(1)}, bf16[4096,128]{1,0:T(8,128)(2,1)S(1)}, u32[]{:S(2)}, u32[]{:S(2)}) collective-permute-start(bf16[4096,128]{1,0:T(8,128)(2,1)S(1)} %collective-permute-done.7.refs_9_), channel_id=1, source_target_pairs={{8,0},{0,8},{9,1},{1,9},{10,2},{2,10},{11,3},{3,11},{12,4},{4,12},... | collective-permute-start | bytes 3145736 | tf_op jit(solution)/shard_map/ppermute | solution.py:365
  51.4 3.4 %collective-permute-start.10 = (bf16[2048,128]{1,0:T(8,128)(2,1)}, bf16[2048,128]{1,0:T(8,128)(2,1)}, u32[]{:S(2)}, u32[]{:S(2)}) collective-permute-start(bf16[2048,128]{1,0:T(8,128)(2,1)} %collective-permute-done.4.refs_6_), channel_id=1, source_target_pairs={{8,0},{0,8},{9,1},{1,9},{10,2},{2,10},{11,3},{3,11},{12,4},{4,12},... | collective-permute-start | bytes 1572872 | tf_op jit(solution)/shard_map/ppermute | solution.py:365
  53.1 3.2 %collective-permute-start.12 = (bf16[2048,128]{1,0:T(8,128)(2,1)}, bf16[2048,128]{1,0:T(8,128)(2,1)}, u32[]{:S(2)}, u32[]{:S(2)}) collective-permute-start(bf16[2048,128]{1,0:T(8,128)(2,1)} %collective-permute-done.6.refs_8_), channel_id=1, source_target_pairs={{8,0},{0,8},{9,1},{1,9},{10,2},{2,10},{11,3},{3,11},{12,4},{4,12},... | collective-permute-start | bytes 1572872 | tf_op jit(solution)/shard_map/ppermute | solution.py:365
  67.4 33.7 %collective-permute-start.18 = (bf16[4096,128]{1,0:T(8,128)(2,1)}, bf16[4096,128]{1,0:T(8,128)(2,1)S(1)}, u32[]{:S(2)}, u32[]{:S(2)}) collective-permute-start(bf16[4096,128]{1,0:T(8,128)(2,1)} %get-tuple-element.28), channel_id=1, source_target_pairs={{4,0},{5,1},{6,2},{7,3},{0,4},{1,5},{2,6},{3,7},{12,8},{13,9},{14,... | collective-permute-start | bytes 3145736 | tf_op jit(solution)/shard_map/ppermute | solution.py:365
  69.7 19.3 %collective-permute-start.14 = (bf16[2048,128]{1,0:T(8,128)(2,1)}, bf16[2048,128]{1,0:T(8,128)(2,1)S(1)}, u32[]{:S(2)}, u32[]{:S(2)}) collective-permute-start(bf16[2048,128]{1,0:T(8,128)(2,1)} %get-tuple-element.24), channel_id=1, source_target_pairs={{3,0},{0,1},{1,2},{2,3},{7,4},{4,5},{5,6},{6,7},{11,8},{8,9},{9,10... | collective-permute-start | bytes 1572872 | tf_op jit(solution)/shard_map/ppermute | solution.py:365
  70.9 26.2 %collective-permute-start.15 = (bf16[2048,128]{1,0:T(8,128)(2,1)}, bf16[2048,128]{1,0:T(8,128)(2,1)S(1)}, u32[]{:S(2)}, u32[]{:S(2)}) collective-permute-start(bf16[2048,128]{1,0:T(8,128)(2,1)} %get-tuple-element.25), channel_id=1, source_target_pairs={{2,0},{3,1},{0,2},{1,3},{6,4},{7,5},{4,6},{5,7},{10,8},{11,9},{8,1... | collective-permute-start | bytes 1572872 | tf_op jit(solution)/shard_map/ppermute | solution.py:365
  76.2 21.8 %collective-permute-start.16 = (bf16[2048,128]{1,0:T(8,128)(2,1)}, bf16[2048,128]{1,0:T(8,128)(2,1)S(1)}, u32[]{:S(2)}, u32[]{:S(2)}) collective-permute-start(bf16[2048,128]{1,0:T(8,128)(2,1)} %get-tuple-element.26), channel_id=1, source_target_pairs={{1,0},{2,1},{3,2},{0,3},{5,4},{6,5},{7,6},{4,7},{9,8},{10,9},{11,1... | collective-permute-start | bytes 1572872 | tf_op jit(solution)/shard_map/ppermute | solution.py:365
  99.3 9.7 %collective-permute-start.17 = (bf16[1024,128]{1,0:T(8,128)(2,1)S(1)}, bf16[1024,128]{1,0:T(8,128)(2,1)S(1)}, u32[]{:S(2)}, u32[]{:S(2)}) collective-permute-start(bf16[1024,128]{1,0:T(8,128)(2,1)S(1)} %add_convert_fusion.13), channel_id=1, source_target_pairs={{4,0},{5,1},{6,2},{7,3},{0,4},{1,5},{2,6},{3,7},{12,8},{13,9},{14,... | collective-permute-start | bytes 786440 | tf_op jit(solution)/shard_map/ppermute | solution.py:365
  102.8 8.9 %collective-permute-start.19 = (bf16[1024,128]{1,0:T(8,128)(2,1)S(1)}, bf16[1024,128]{1,0:T(8,128)(2,1)S(1)}, u32[]{:S(2)}, u32[]{:S(2)}) collective-permute-start(bf16[1024,128]{1,0:T(8,128)(2,1)S(1)} %get-tuple-element.52), channel_id=1, source_target_pairs={{3,0},{0,1},{1,2},{2,3},{7,4},{4,5},{5,6},{6,7},{11,8},{8,9},{9,10... | collective-permute-start | bytes 786440 | tf_op jit(solution)/shard_map/ppermute | solution.py:365
  104.1 13.8 %collective-permute-start.20 = (bf16[1024,128]{1,0:T(8,128)(2,1)S(1)}, bf16[1024,128]{1,0:T(8,128)(2,1)S(1)}, u32[]{:S(2)}, u32[]{:S(2)}) collective-permute-start(bf16[1024,128]{1,0:T(8,128)(2,1)S(1)} %get-tuple-element.51), channel_id=1, source_target_pairs={{2,0},{3,1},{0,2},{1,3},{6,4},{7,5},{4,6},{5,7},{10,8},{11,9},{8,1... | collective-permute-start | bytes 786440 | tf_op jit(solution)/shard_map/ppermute | solution.py:365
  106.6 11.3 %collective-permute-start.21 = (bf16[1024,128]{1,0:T(8,128)(2,1)S(1)}, bf16[1024,128]{1,0:T(8,128)(2,1)S(1)}, u32[]{:S(2)}, u32[]{:S(2)}) collective-permute-start(bf16[1024,128]{1,0:T(8,128)(2,1)S(1)} %get-tuple-element.50), channel_id=1, source_target_pairs={{1,0},{2,1},{3,2},{0,3},{5,4},{6,5},{7,6},{4,7},{9,8},{10,9},{11,1... | collective-permute-start | bytes 786440 | tf_op jit(solution)/shard_map/ppermute | solution.py:365
  123.8 8.0 %collective-permute-start.22 = (bf16[1024,128]{1,0:T(8,128)(2,1)}, bf16[1024,128]{1,0:T(8,128)(2,1)S(1)}, u32[]{:S(2)}, u32[]{:S(2)}) collective-permute-start(bf16[1024,128]{1,0:T(8,128)(2,1)} %get-tuple-element.30.first), channel_id=1, source_target_pairs={{4,0},{5,1},{6,2},{7,3},{0,4},{1,5},{2,6},{3,7},{12,8},{13,9},{14,... | collective-permute-start | bytes 786440 | tf_op jit(solution)/shard_map/ppermute | solution.py:365
  125.3 9.8 %collective-permute-start.23 = (bf16[1024,128]{1,0:T(8,128)(2,1)}, bf16[1024,128]{1,0:T(8,128)(2,1)S(1)}, u32[]{:S(2)}, u32[]{:S(2)}) collective-permute-start(bf16[1024,128]{1,0:T(8,128)(2,1)} %get-tuple-element.31.refs_0_), channel_id=1, source_target_pairs={{1,0},{2,1},{3,2},{0,3},{5,4},{6,5},{7,6},{4,7},{9,8},{10,9},{11,1... | collective-permute-start | bytes 786440 | tf_op jit(solution)/shard_map/ppermute | solution.py:365
  128.1 8.5 %collective-permute-start.24 = (bf16[1024,128]{1,0:T(8,128)(2,1)}, bf16[1024,128]{1,0:T(8,128)(2,1)S(1)}, u32[]{:S(2)}, u32[]{:S(2)}) collective-permute-start(bf16[1024,128]{1,0:T(8,128)(2,1)} %get-tuple-element.31.refs_0_), channel_id=1, source_target_pairs={{2,0},{3,1},{0,2},{1,3},{6,4},{7,5},{4,6},{5,7},{10,8},{11,9},{8,1... | collective-permute-start | bytes 786440 | tf_op jit(solution)/shard_map/ppermute | solution.py:365
  128.8 14.9 %collective-permute-start.25 = (bf16[1024,128]{1,0:T(8,128)(2,1)}, bf16[1024,128]{1,0:T(8,128)(2,1)S(1)}, u32[]{:S(2)}, u32[]{:S(2)}) collective-permute-start(bf16[1024,128]{1,0:T(8,128)(2,1)} %get-tuple-element.31.refs_0_), channel_id=1, source_target_pairs={{3,0},{0,1},{1,2},{2,3},{7,4},{4,5},{5,6},{6,7},{11,8},{8,9},{9,10... | collective-permute-start | bytes 786440 | tf_op jit(solution)/shard_map/ppermute | solution.py:365
  147.0 26.5 %collective-permute-start.29 = (bf16[4096,128]{1,0:T(8,128)(2,1)}, bf16[4096,128]{1,0:T(8,128)(2,1)S(1)}, u32[]{:S(2)}, u32[]{:S(2)}) collective-permute-start(bf16[4096,128]{1,0:T(8,128)(2,1)} %get-tuple-element.33.refs_6_), channel_id=1, source_target_pairs={{4,0},{5,1},{6,2},{7,3},{0,4},{1,5},{2,6},{3,7},{12,8},{13,9},{14,... | collective-permute-start | bytes 3145736 | tf_op jit(solution)/shard_map/ppermute | solution.py:365
  148.6 9.8 %collective-permute-start.32 = (f32[256,256]{1,0:T(8,128)}, f32[256,256]{1,0:T(8,128)S(1)}, u32[]{:S(2)}, u32[]{:S(2)}) collective-permute-start(f32[256,256]{1,0:T(8,128)} %get-tuple-element.34), channel_id=1, source_target_pairs={{48,0},{0,16},{16,32},{32,48},{112,64},{64,80},{80,96},{96,112},{4... | collective-permute-start | bytes 786440 | tf_op jit(solution)/shard_map/ppermute | solution.py:365
  148.6 12.8 %collective-permute-start.31 = (f32[256,256]{1,0:T(8,128)}, f32[256,256]{1,0:T(8,128)S(1)}, u32[]{:S(2)}, u32[]{:S(2)}) collective-permute-start(f32[256,256]{1,0:T(8,128)} %get-tuple-element.34), channel_id=1, source_target_pairs={{32,0},{48,16},{0,32},{16,48},{96,64},{112,80},{64,96},{80,112},{3... | collective-permute-start | bytes 786440 | tf_op jit(solution)/shard_map/ppermute | solution.py:365
  150.0 18.9 %collective-permute-start.26 = (bf16[2048,128]{1,0:T(8,128)(2,1)}, bf16[2048,128]{1,0:T(8,128)(2,1)S(1)}, u32[]{:S(2)}, u32[]{:S(2)}) collective-permute-start(bf16[2048,128]{1,0:T(8,128)(2,1)} %get-tuple-element.32.refs_5_), channel_id=1, source_target_pairs={{1,0},{2,1},{3,2},{0,3},{5,4},{6,5},{7,6},{4,7},{9,8},{10,9},{11,1... | collective-permute-start | bytes 1572872 | tf_op jit(solution)/shard_map/ppermute | solution.py:365
  150.0 18.9 %collective-permute-start.27 = (bf16[2048,128]{1,0:T(8,128)(2,1)}, bf16[2048,128]{1,0:T(8,128)(2,1)S(1)}, u32[]{:S(2)}, u32[]{:S(2)}) collective-permute-start(bf16[2048,128]{1,0:T(8,128)(2,1)} %get-tuple-element.32.refs_5_), channel_id=1, source_target_pairs={{2,0},{3,1},{0,2},{1,3},{6,4},{7,5},{4,6},{5,7},{10,8},{11,9},{8,1... | collective-permute-start | bytes 1572872 | tf_op jit(solution)/shard_map/ppermute | solution.py:365
  158.3 15.1 %collective-permute-start.28 = (bf16[2048,128]{1,0:T(8,128)(2,1)}, bf16[2048,128]{1,0:T(8,128)(2,1)S(1)}, u32[]{:S(2)}, u32[]{:S(2)}) collective-permute-start(bf16[2048,128]{1,0:T(8,128)(2,1)} %get-tuple-element.32.refs_5_), channel_id=1, source_target_pairs={{3,0},{0,1},{1,2},{2,3},{7,4},{4,5},{5,6},{6,7},{11,8},{8,9},{9,10... | collective-permute-start | bytes 1572872 | tf_op jit(solution)/shard_map/ppermute | solution.py:365
  161.4 5.7 %collective-permute-start.30 = (f32[256,256]{1,0:T(8,128)}, f32[256,256]{1,0:T(8,128)S(1)}, u32[]{:S(2)}, u32[]{:S(2)}) collective-permute-start(f32[256,256]{1,0:T(8,128)} %get-tuple-element.34), channel_id=1, source_target_pairs={{16,0},{32,16},{48,32},{0,48},{80,64},{96,80},{112,96},{64,112},{1... | collective-permute-start | bytes 786440 | tf_op jit(solution)/shard_map/ppermute | solution.py:365
  183.9 9.4 %collective-permute-start.38 = (bf16[8192,128]{1,0:T(8,128)(2,1)}, bf16[8192,128]{1,0:T(8,128)(2,1)S(1)}, u32[]{:S(2)}, u32[]{:S(2)}) collective-permute-start(bf16[8192,128]{1,0:T(8,128)(2,1)} %get-tuple-element.38), channel_id=1, source_target_pairs={{8,0},{0,8},{9,1},{1,9},{10,2},{2,10},{11,3},{3,11},{12,4},{4,12},... | collective-permute-start | bytes 6291464 | tf_op jit(solution)/shard_map/ppermute | solution.py:365
  188.9 8.4 %collective-permute-start.33 = (bf16[8192,128]{1,0:T(8,128)(2,1)}, bf16[8192,128]{1,0:T(8,128)(2,1)S(1)}, u32[]{:S(2)}, u32[]{:S(2)}) collective-permute-start(bf16[8192,128]{1,0:T(8,128)(2,1)} %get-tuple-element.36), channel_id=1, source_target_pairs={{8,0},{0,8},{9,1},{1,9},{10,2},{2,10},{11,3},{3,11},{12,4},{4,12},... | collective-permute-start | bytes 6291464 | tf_op jit(solution)/shard_map/ppermute | solution.py:365
  189.0 11.0 %collective-permute-start.45 = (f32[256,256]{1,0:T(8,128)S(1)}, f32[256,256]{1,0:T(8,128)S(1)}, u32[]{:S(2)}, u32[]{:S(2)}) collective-permute-start(f32[256,256]{1,0:T(8,128)S(1)} %copy-done.4), channel_id=1, source_target_pairs={{3,0},{0,1},{1,2},{2,3},{7,4},{4,5},{5,6},{6,7},{11,8},{8,9},{9,10... | collective-permute-start | bytes 786440 | tf_op jit(solution)/shard_map/ppermute | solution.py:365
  189.0 16.4 %collective-permute-start.44 = (f32[256,256]{1,0:T(8,128)S(1)}, f32[256,256]{1,0:T(8,128)S(1)}, u32[]{:S(2)}, u32[]{:S(2)}) collective-permute-start(f32[256,256]{1,0:T(8,128)S(1)} %copy-done.4), channel_id=1, source_target_pairs={{2,0},{3,1},{0,2},{1,3},{6,4},{7,5},{4,6},{5,7},{10,8},{11,9},{8,1... | collective-permute-start | bytes 786440 | tf_op jit(solution)/shard_map/ppermute | solution.py:365
  193.3 13.4 %collective-permute-start.43 = (f32[256,256]{1,0:T(8,128)S(1)}, f32[256,256]{1,0:T(8,128)S(1)}, u32[]{:S(2)}, u32[]{:S(2)}) collective-permute-start(f32[256,256]{1,0:T(8,128)S(1)} %copy-done.4), channel_id=1, source_target_pairs={{1,0},{2,1},{3,2},{0,3},{5,4},{6,5},{7,6},{4,7},{9,8},{10,9},{11,1... | collective-permute-start | bytes 786440 | tf_op jit(solution)/shard_map/ppermute | solution.py:365
  195.6 32.7 %collective-permute-start.39 = (bf16[4096,128]{1,0:T(8,128)(2,1)S(1)}, bf16[4096,128]{1,0:T(8,128)(2,1)S(1)}, u32[]{:S(2)}, u32[]{:S(2)}) collective-permute-start(bf16[4096,128]{1,0:T(8,128)(2,1)S(1)} %get-tuple-element.41), channel_id=1, source_target_pairs={{64,0},{80,16},{96,32},{112,48},{0,64},{16,80},{32,96},{48,112},{6... | collective-permute-start | bytes 3145736 | tf_op jit(solution)/shard_map/ppermute | solution.py:365
  197.8 25.6 %collective-permute-start.34 = (bf16[2048,128]{1,0:T(8,128)(2,1)S(1)}, bf16[2048,128]{1,0:T(8,128)(2,1)S(1)}, u32[]{:S(2)}, u32[]{:S(2)}) collective-permute-start(bf16[2048,128]{1,0:T(8,128)(2,1)S(1)} %get-tuple-element.45), channel_id=1, source_target_pairs={{48,0},{0,16},{16,32},{32,48},{112,64},{64,80},{80,96},{96,112},{4... | collective-permute-start | bytes 1572872 | tf_op jit(solution)/shard_map/ppermute | solution.py:365
  199.9 24.4 %collective-permute-start.35 = (bf16[2048,128]{1,0:T(8,128)(2,1)S(1)}, bf16[2048,128]{1,0:T(8,128)(2,1)S(1)}, u32[]{:S(2)}, u32[]{:S(2)}) collective-permute-start(bf16[2048,128]{1,0:T(8,128)(2,1)S(1)} %get-tuple-element.44), channel_id=1, source_target_pairs={{32,0},{48,16},{0,32},{16,48},{96,64},{112,80},{64,96},{80,112},{3... | collective-permute-start | bytes 1572872 | tf_op jit(solution)/shard_map/ppermute | solution.py:365
  205.3 22.3 %collective-permute-start.36 = (bf16[2048,128]{1,0:T(8,128)(2,1)S(1)}, bf16[2048,128]{1,0:T(8,128)(2,1)S(1)}, u32[]{:S(2)}, u32[]{:S(2)}) collective-permute-start(bf16[2048,128]{1,0:T(8,128)(2,1)S(1)} %get-tuple-element.43), channel_id=1, source_target_pairs={{16,0},{32,16},{48,32},{0,48},{80,64},{96,80},{112,96},{64,112},{1... | collective-permute-start | bytes 1572872 | tf_op jit(solution)/shard_map/ppermute | solution.py:365
  209.5 19.2 %collective-permute-start.49 = (f32[256,256]{1,0:T(8,128)S(1)}, f32[256,256]{1,0:T(8,128)S(1)}, u32[]{:S(2)}, u32[]{:S(2)}) collective-permute-start(f32[256,256]{1,0:T(8,128)S(1)} %add.197), channel_id=1, source_target_pairs={{68,0},{64,4},{4,64},{0,68},{69,1},{65,5},{5,65},{1,69},{70,2},{66... | collective-permute-start | bytes 786440 | tf_op jit(solution)/shard_map/ppermute | solution.py:365
  223.4 8.7 %collective-permute-start.48 = (f32[256,256]{1,0:T(8,128)S(1)}, f32[256,256]{1,0:T(8,128)S(1)}, u32[]{:S(2)}, u32[]{:S(2)}) collective-permute-start(f32[256,256]{1,0:T(8,128)S(1)} %add.197), channel_id=1, source_target_pairs={{64,0},{68,4},{0,64},{4,68},{65,1},{69,5},{1,65},{5,69},{66,2},{70... | collective-permute-start | bytes 786440 | tf_op jit(solution)/shard_map/ppermute | solution.py:365
  224.4 10.3 %collective-permute-start.47 = (f32[256,256]{1,0:T(8,128)S(1)}, f32[256,256]{1,0:T(8,128)S(1)}, u32[]{:S(2)}, u32[]{:S(2)}) collective-permute-start(f32[256,256]{1,0:T(8,128)S(1)} %add.197), channel_id=1, source_target_pairs={{4,0},{0,4},{68,64},{64,68},{5,1},{1,5},{69,65},{65,69},{6,2},{2,6... | collective-permute-start | bytes 786440 | tf_op jit(solution)/shard_map/ppermute | solution.py:365
  227.7 13.4 %collective-permute-start.37 = (bf16[1024,128]{1,0:T(8,128)(2,1)S(1)}, bf16[1024,128]{1,0:T(8,128)(2,1)S(1)}, u32[]{:S(2)}, u32[]{:S(2)}) collective-permute-start(bf16[1024,128]{1,0:T(8,128)(2,1)S(1)} %add_convert_fusion.9), channel_id=1, source_target_pairs={{64,0},{80,16},{96,32},{112,48},{0,64},{16,80},{32,96},{48,112},{6... | collective-permute-start | bytes 786440 | tf_op jit(solution)/shard_map/ppermute | solution.py:365
  228.5 12.7 %collective-permute-start.40 = (bf16[1024,128]{1,0:T(8,128)(2,1)S(1)}, bf16[1024,128]{1,0:T(8,128)(2,1)S(1)}, u32[]{:S(2)}, u32[]{:S(2)}) collective-permute-start(bf16[1024,128]{1,0:T(8,128)(2,1)S(1)} %get-tuple-element.49), channel_id=1, source_target_pairs={{48,0},{0,16},{16,32},{32,48},{112,64},{64,80},{80,96},{96,112},{4... | collective-permute-start | bytes 786440 | tf_op jit(solution)/shard_map/ppermute | solution.py:365
  228.7 14.9 %collective-permute-start.41 = (bf16[1024,128]{1,0:T(8,128)(2,1)S(1)}, bf16[1024,128]{1,0:T(8,128)(2,1)S(1)}, u32[]{:S(2)}, u32[]{:S(2)}) collective-permute-start(bf16[1024,128]{1,0:T(8,128)(2,1)S(1)} %get-tuple-element.48), channel_id=1, source_target_pairs={{32,0},{48,16},{0,32},{16,48},{96,64},{112,80},{64,96},{80,112},{3... | collective-permute-start | bytes 786440 | tf_op jit(solution)/shard_map/ppermute | solution.py:365
  232.1 11.5 %collective-permute-start.42 = (bf16[1024,128]{1,0:T(8,128)(2,1)S(1)}, bf16[1024,128]{1,0:T(8,128)(2,1)S(1)}, u32[]{:S(2)}, u32[]{:S(2)}) collective-permute-start(bf16[1024,128]{1,0:T(8,128)(2,1)S(1)} %get-tuple-element.47), channel_id=1, source_target_pairs={{16,0},{32,16},{48,32},{0,48},{80,64},{96,80},{112,96},{64,112},{1... | collective-permute-start | bytes 786440 | tf_op jit(solution)/shard_map/ppermute | solution.py:365
  (41 other events, 468.6 us)

commit v4 on v3

--- a/solution.py
+++ b/solution.py
@@ -12,7 +12,9 @@
 F32 = jnp.float32
 ROW = ("zl", "y", "core")
 COL = ("zh", "x")
-VMEM_LIMIT = 58 * 2**20
+FORWARD_LIMIT = 40 * 2**20
+BACKWARD_LIMIT = 48 * 2**20
+SMALL_LIMIT = 14 * 2**20
 PARTS = 2
 BATCH = 48
 CHUNK = 48
@@ -139,7 +141,7 @@
         out_shape=[
             jax.ShapeDtypeStruct((len(slabs) * slab, part_width), BF16) for slabs, _ in result_plan
         ],
-        compiler_params=pltpu.CompilerParams(vmem_limit_bytes=VMEM_LIMIT),
+        compiler_params=pltpu.CompilerParams(vmem_limit_bytes=FORWARD_LIMIT),
         cost_estimate=pl.CostEstimate(flops=1024, bytes_accessed=1024, transcendentals=0),
         name="forward",
     )(count, src, dst, tiles, *sources)
@@ -251,7 +253,7 @@
             ],
         ),
         out_shape=[jax.ShapeDtypeStruct((slabs // 2 * slab, part_width), BF16)] * 4,
-        compiler_params=pltpu.CompilerParams(vmem_limit_bytes=VMEM_LIMIT),
+        compiler_params=pltpu.CompilerParams(vmem_limit_bytes=BACKWARD_LIMIT),
         cost_estimate=pl.CostEstimate(flops=1024, bytes_accessed=1024, transcendentals=0),
         name="backward",
     )(count, src, dst, slab_at, tiles, *sources)
@@ -304,7 +306,7 @@
 
 def middle(pieces, weight, bias, cotangent, parts):
     rows, width = cotangent.shape
-    steps = 4
+    steps = 2
     block = rows // steps
     part_spec = pl.BlockSpec((block, width // parts), lambda i: (i, 0))
     wide_spec = pl.BlockSpec((block, width), lambda i: (i, 0))
@@ -317,7 +319,7 @@
         out_shape=[jax.ShapeDtypeStruct((rows, width), BF16)]
         + [jax.ShapeDtypeStruct((rows, width // parts), BF16)] * parts
         + [jax.ShapeDtypeStruct((width, width), F32)],
-        compiler_params=pltpu.CompilerParams(vmem_limit_bytes=VMEM_LIMIT),
+        compiler_params=pltpu.CompilerParams(vmem_limit_bytes=SMALL_LIMIT),
         name="middle",
     )(*pieces, weight, bias.reshape(1, width), cotangent)
 
@@ -333,7 +335,7 @@
 def final(pieces, weight, parts):
     rows = pieces[-1].shape[0]
     width = weight.shape[0]
-    steps = 4
+    steps = 2
     block = rows // steps
     part_spec = pl.BlockSpec((block, width // parts), lambda i: (i, 0))
     return pl.pallas_call(
@@ -342,7 +344,7 @@
         in_specs=[part_spec] * len(pieces) + [pl.BlockSpec((width, width), lambda i: (0, 0))],
         out_specs=pl.BlockSpec((block, width), lambda i: (i, 0)),
         out_shape=jax.ShapeDtypeStruct((rows, width), BF16),
-        compiler_params=pltpu.CompilerParams(vmem_limit_bytes=VMEM_LIMIT),
+        compiler_params=pltpu.CompilerParams(vmem_limit_bytes=SMALL_LIMIT),
         name="final",
     )(*pieces, weight)
 
@@ -373,21 +375,42 @@
     return shift(value, axes, (2, 4), (dz, -dr))
 
 
-def scatter_ring_first(held, axes):
-    nodes = held[0].shape[0] // 2
-    arrived = [held[0]] + [toward(held[dr], axes, 0, dr) for dr in range(1, 4)]
-    other = add(*[piece[nodes:] for piece in arrived]).astype(BF16)
-    return arrived + [toward(other, axes, 1, 0)]
-
-
-def scatter_pair_first(held, axes):
-    nodes = held[0].shape[0] // 4
-    arrived = [held[0], toward(held[1], axes, 1, 0)]
-    terms = []
-    for dr in range(1, 4):
-        span = slice(dr * nodes, (dr + 1) * nodes)
-        terms.append(toward(add(arrived[0][span], arrived[1][span]).astype(BF16), axes, 0, dr))
-    return arrived + terms
+def relay_kernel(*refs):
+    ring, own, arrived = refs[:4], refs[4], refs[5]
+    other, *terms = refs[6:]
+    nodes = other.shape[0]
+    total = ring[0][...].astype(F32)
+    for piece in ring[1:]:
+        total = total + piece[...].astype(F32)
+    other[...] = total.astype(BF16)
+    for index, term in enumerate(terms):
+        span = slice((index + 1) * nodes, (index + 2) * nodes)
+        term[...] = (own[span, :].astype(F32) + arrived[span, :].astype(F32)).astype(BF16)
+
+
+def relay(ring, own, arrived):
+    nodes, width = own.shape[0] // 4, own.shape[1]
+    half = pl.BlockSpec((nodes, width), lambda i: (1, 0))
+    whole = pl.BlockSpec(own.shape, lambda i: (0, 0))
+    out = pl.BlockSpec((nodes, width), lambda i: (0, 0))
+    return pl.pallas_call(
+        relay_kernel,
+        grid=(1,),
+        in_specs=[half] * 4 + [whole] * 2,
+        out_specs=[out] * 4,
+        out_shape=[jax.ShapeDtypeStruct((nodes, width), BF16)] * 4,
+        compiler_params=pltpu.CompilerParams(vmem_limit_bytes=SMALL_LIMIT),
+        cost_estimate=pl.CostEstimate(flops=1024, bytes_accessed=1024, transcendentals=0),
+        name="relay",
+    )(*ring, own, arrived)
+
+
+def scatter(held, axes):
+    ring = [held[0]] + [toward(held[dr], axes, 0, dr) for dr in range(1, 4)]
+    arrived = toward(held[5], axes, 1, 0)
+    other, *terms = relay(ring, held[4], arrived)
+    first = ring + [toward(other, axes, 1, 0)]
+    return first + [held[4], arrived] + [toward(terms[dr - 1], axes, 0, dr) for dr in range(1, 4)]
 
 
 def join_kernel(first, first_pair, *refs):
@@ -408,7 +431,7 @@
             jax.ShapeDtypeStruct((2 * nodes, width), BF16),
             jax.ShapeDtypeStruct((4 * nodes, width), BF16),
         ],
-        compiler_params=pltpu.CompilerParams(vmem_limit_bytes=VMEM_LIMIT),
+        compiler_params=pltpu.CompilerParams(vmem_limit_bytes=SMALL_LIMIT),
         cost_estimate=pl.CostEstimate(flops=1024, bytes_accessed=1024, transcendentals=0),
         name="join",
     )(first, first_pair, *ring)
@@ -470,7 +493,7 @@
     held = forward_sweep(
         count, col_from, row_to, tiles, early + later + others, GATHERED + OTHER_CORE, plan, nodes, width
     )
-    arrived = scatter_ring_first(held[:4], col_axes) + scatter_pair_first(held[4:], col_axes)
+    arrived = scatter(held, col_axes)
     activations, first, second, weight_term = middle(arrived, weight, layer_bias, cotangent, PARTS)
 
     early, later = gather(first, second, col_axes)
@@ -478,17 +501,16 @@
     results = backward_sweep(
         count, row_at, col_to, slab_at, tiles, early + later + [weight_sum], GATHERED + [[]], nodes, width
     )
-    collected = []
+    held = []
     for part, plan in enumerate((RING_FIRST, PAIR_FIRST)):
         mine, theirs = results[part], results[2 + part]
         swapped = shift(theirs, "core", (2,), (1,))
-        held, done = [], 0
+        done = 0
         for slabs in plan:
             span = slice(done * nodes, (done + len(slabs)) * nodes)
             held.append(add(mine[span], swapped[span]).astype(BF16))
             done += len(slabs)
-        scatter = scatter_ring_first if part == 0 else scatter_pair_first
-        collected += scatter(held, row_axes)
+    collected = scatter(held, row_axes)
     grad_features = final(collected, weight, PARTS)
     weight_sum = add(*around(weight_sum, "x", (4,), [(1,), (2,), (3,)]))
     weight_sum = add(*around(weight_sum, "core", (2,), [(1,)]))

time: 254 us -> 235 us (0.925)
  starting transfers between devices: 65.6 us -> 52.8 us
  other arithmetic: 9.87 us -> 3.84 us
  waiting for transfers between devices: 132 us -> 138 us
  Pallas kernels: 33.7 us -> 30.6 us
    ppermute x50, starting transfers between devices: 65.6 us -> 52.8 us  [shift(): return lax.ppermute(value, axes, perm)]
    ppermute x50, waiting for transfers between devices: 132 us -> 138 us  [shift(): return lax.ppermute(value, axes, perm)]
    pallas_call x2, Pallas kernels: 5.08 us -> 0.21 us  [join(): pl.pallas_call(join_kernel, out_shape=[jax.ShapeDtypeStruct((2 * nodes, w...]
    pallas_call x1, Pallas kernels: 9.26 us -> 13.2 us  [backward_sweep(): pl.pallas_call(functools.partial(backward_kernel, source_plan, slab, batc...]
    convert_element_type x4 -> x0, other arithmetic: 3.29 us -> none  [the longest x2 1.9 us: scatter_pair_first(): add(arrived[0][span], arrived[1][span]).astype(BF16)]
    pallas_call x1, Pallas kernels: 5.13 us -> 2.2 us  [middle(): pl.pallas_call(functools.partial(middle_kernel, parts, len(pieces)), grid...]
    pallas_call x1, Pallas kernels: 10.1 us -> 13 us  [forward_sweep(): pl.pallas_call(functools.partial(forward_kernel, source_plan, result_plan...]
    pallas_call x1, Pallas kernels: 4.16 us -> 1.37 us  [final(): pl.pallas_call(functools.partial(final_kernel, parts, len(pieces)), grid=...]
  transfers between devices with their start and end apart: 50 -> 50, of which waited for: 30 -> 27; matrix products, arithmetic and copies ran while one was open for 4% -> 2% of each run, Pallas kernels for 0% -> 0%
where the time goes in v4:
time: 235 us; the launch traced here: 231 us
  waiting for transfers between devices  138 us (59%)
  starting transfers between devices  52.8 us (22%)
  Pallas kernels  30.6 us (13%)
  local copies, waits for them, and re-layouts  4.77 us (2%)
  other arithmetic  3.84 us (2%)
    ppermute x50, waiting for transfers between devices, shift(): return lax.ppermute(value, axes, perm)  138 us
    ppermute x50, starting transfers between devices, shift(): return lax.ppermute(value, axes, perm)  52.8 us
    pallas_call x1, Pallas kernels, backward_sweep(): pl.pallas_call(functools.partial(backward_kernel, source_plan, slab, batc...  13.2 us
    pallas_call x1, Pallas kernels, forward_sweep(): pl.pallas_call(functools.partial(forward_kernel, source_plan, result_plan...  13 us
  transfers between devices with their start and end apart: 50, of which 27 were waited for; matrix products, arithmetic and copies ran while one was open for 2% of the time, Pallas kernels for 0%

profile of v4, /device:TPU:1, one launch (start us, length us, event | category | flops | bytes accessed | tf_op | source)
XLA Modules:
  0.0 231.3 jit_solution(15531213235346827952)
XLA Ops:
  1.7 2.5 %collective-permute-start = (bf16[1024,128]{1,0:T(8,128)(2,1)S(1)}, bf16[1024,128]{1,0:T(8,128)(2,1)S(1)}, u32[]{:S(2)}, u32[]{:S(2)}) collective-permute-start(bf16[1024,128]{1,0:T(8,128)(2,1)S(1)} %get-tuple-element.64.first), channel_id=1, source_target_pairs={{64,0},{80,16},{96,32},{112,48},{0,64},{16,80},{32,96},{48,112},{6... | collective-permute-start | bytes 786440 | tf_op jit(solution)/shard_map/ppermute | solution.py:367
  4.3 2.7 %collective-permute-start.1 = (bf16[1024,128]{1,0:T(8,128)(2,1)S(1)}, bf16[1024,128]{1,0:T(8,128)(2,1)S(1)}, u32[]{:S(2)}, u32[]{:S(2)}) collective-permute-start(bf16[1024,128]{1,0:T(8,128)(2,1)S(1)} %get-tuple-element.63.refs_0_), channel_id=1, source_target_pairs={{16,0},{32,16},{48,32},{0,48},{80,64},{96,80},{112,96},{64,112},{1... | collective-permute-start | bytes 786440 | tf_op jit(solution)/shard_map/ppermute | solution.py:367
  8.1 2.2 collective-permute-done.first_pair
  10.3 2.4 %collective-permute-done.1.refs_1_ = bf16[1024,128]{1,0:T(8,128)(2,1)S(1)} collective-permute-done((bf16[1024,128]{1,0:T(8,128)(2,1)S(1)}, bf16[1024,128]{1,0:T(8,128)(2,1)S(1)}, u32[]{:S(2)}, u32[]{:S(2)}) %collective-permute-start.1) | collective-permute-done | bytes 262176 | tf_op jit(solution)/shard_map/ppermute | solution.py:367
  12.7 2.4 %collective-permute-done.2.refs_2_ = bf16[1024,128]{1,0:T(8,128)(2,1)S(1)} collective-permute-done((bf16[1024,128]{1,0:T(8,128)(2,1)S(1)}, bf16[1024,128]{1,0:T(8,128)(2,1)S(1)}, u32[]{:S(2)}, u32[]{:S(2)}) %collective-permute-start.2) | collective-permute-done | bytes 262176 | tf_op jit(solution)/shard_map/ppermute | solution.py:367
  15.1 7.2 %collective-permute-done.3.refs_3_ = bf16[1024,128]{1,0:T(8,128)(2,1)S(1)} collective-permute-done((bf16[1024,128]{1,0:T(8,128)(2,1)S(1)}, bf16[1024,128]{1,0:T(8,128)(2,1)S(1)}, u32[]{:S(2)}, u32[]{:S(2)}) %collective-permute-start.3) | collective-permute-done | bytes 262176 | tf_op jit(solution)/shard_map/ppermute | solution.py:367
  24.1 1.4 collective-permute-start.9
  25.5 10.0 %collective-permute-done.4.refs_6_ = bf16[2048,128]{1,0:T(8,128)(2,1)} collective-permute-done((bf16[2048,128]{1,0:T(8,128)(2,1)S(1)}, bf16[2048,128]{1,0:T(8,128)(2,1)}, u32[]{:S(2)}, u32[]{:S(2)}) %collective-permute-start.4) | collective-permute-done | bytes 524320 | tf_op jit(solution)/shard_map/ppermute | solution.py:367
  35.4 2.9 %collective-permute-start.8 = (bf16[2048,128]{1,0:T(8,128)(2,1)S(1)}, bf16[2048,128]{1,0:T(8,128)(2,1)S(1)}, u32[]{:S(2)}, u32[]{:S(2)}) collective-permute-start(bf16[2048,128]{1,0:T(8,128)(2,1)S(1)} %get-tuple-element.29.refs_4_), channel_id=1, source_target_pairs={{8,0},{0,8},{9,1},{1,9},{10,2},{2,10},{11,3},{3,11},{12,4},{4,12},... | collective-permute-start | bytes 1572872 | tf_op jit(solution)/shard_map/ppermute | solution.py:367
  39.1 7.8 %collective-permute-done.7.refs_9_ = bf16[4096,128]{1,0:T(8,128)(2,1)S(1)} collective-permute-done((bf16[4096,128]{1,0:T(8,128)(2,1)S(1)}, bf16[4096,128]{1,0:T(8,128)(2,1)S(1)}, u32[]{:S(2)}, u32[]{:S(2)}) %collective-permute-start.7) | collective-permute-done | bytes 1048608 | tf_op jit(solution)/shard_map/ppermute | solution.py:367
  46.9 1.2 collective-permute-start.13
  48.1 1.3 collective-permute-done.6.refs_8_
  55.1 13.0 %forward.1 = (bf16[2048,128]{1,0:T(8,128)(2,1)S(1)}, bf16[2048,128]{1,0:T(8,128)(2,1)S(1)}, bf16[2048,128]{1,0:T(8,128)(2,1)S(1)}, bf16[2048,128]{1,0:T(8,128)(2...) custom-call(s32[1]{0:T(128)} %bitcast.4.refs_0_, s32[384]{0:T(512)S(1)} %get-tuple-element.66.refs_1_, ...), custom_call_target="tpu_custom_call" | custom-call | flops 1024 | bytes 1024 | tf_op jit(solution)/shard_map/forward/pallas_call | solution.py:124
  68.1 3.4 %collective-permute-start.17 = (bf16[4096,128]{1,0:T(8,128)(2,1)S(1)}, bf16[4096,128]{1,0:T(8,128)(2,1)S(1)}, u32[]{:S(2)}, u32[]{:S(2)}) collective-permute-start(bf16[4096,128]{1,0:T(8,128)(2,1)S(1)} %get-tuple-element.36), channel_id=1, source_target_pairs={{4,0},{5,1},{6,2},{7,3},{0,4},{1,5},{2,6},{3,7},{12,8},{13,9},{14,... | collective-permute-start | bytes 3145736 | tf_op jit(solution)/shard_map/ppermute | solution.py:367
  71.5 1.2 collective-permute-start.14
  72.7 2.4 %collective-permute-start.16 = (bf16[2048,128]{1,0:T(8,128)(2,1)S(1)}, bf16[2048,128]{1,0:T(8,128)(2,1)S(1)}, u32[]{:S(2)}, u32[]{:S(2)}) collective-permute-start(bf16[2048,128]{1,0:T(8,128)(2,1)S(1)} %get-tuple-element.34), channel_id=1, source_target_pairs={{1,0},{2,1},{3,2},{0,3},{5,4},{6,5},{7,6},{4,7},{9,8},{10,9},{11,1... | collective-permute-start | bytes 1572872 | tf_op jit(solution)/shard_map/ppermute | solution.py:367
  75.1 19.6 %collective-permute-done.14.refs_1_ = bf16[2048,128]{1,0:T(8,128)(2,1)S(1)} collective-permute-done((bf16[2048,128]{1,0:T(8,128)(2,1)S(1)}, bf16[2048,128]{1,0:T(8,128)(2,1)S(1)}, u32[]{:S(2)}, u32[]{:S(2)}) %collective-permute-start.14) | collective-permute-done | bytes 524320 | tf_op jit(solution)/shard_map/ppermute | solution.py:367
  94.6 2.3 %collective-permute-done.16.refs_3_ = bf16[2048,128]{1,0:T(8,128)(2,1)S(1)} collective-permute-done((bf16[2048,128]{1,0:T(8,128)(2,1)S(1)}, bf16[2048,128]{1,0:T(8,128)(2,1)S(1)}, u32[]{:S(2)}, u32[]{:S(2)}) %collective-permute-start.16) | collective-permute-done | bytes 524320 | tf_op jit(solution)/shard_map/ppermute | solution.py:367
  97.4 2.5 %collective-permute-start.19 = (bf16[1024,128]{1,0:T(8,128)(2,1)S(1)}, bf16[1024,128]{1,0:T(8,128)(2,1)S(1)}, u32[]{:S(2)}, u32[]{:S(2)}) collective-permute-start(bf16[1024,128]{1,0:T(8,128)(2,1)S(1)} %get-tuple-element.38), channel_id=1, source_target_pairs={{3,0},{0,1},{1,2},{2,3},{7,4},{4,5},{5,6},{6,7},{11,8},{8,9},{9,10... | collective-permute-start | bytes 786440 | tf_op jit(solution)/shard_map/ppermute | solution.py:367
  99.9 1.3 collective-permute-start.20
  101.2 1.1 collective-permute-start.21
  102.3 4.8 %collective-permute-done.18.refs_4_ = bf16[1024,128]{1,0:T(8,128)(2,1)S(1)} collective-permute-done((bf16[1024,128]{1,0:T(8,128)(2,1)S(1)}, bf16[1024,128]{1,0:T(8,128)(2,1)S(1)}, u32[]{:S(2)}, u32[]{:S(2)}) %collective-permute-start.18) | collective-permute-done | bytes 262176 | tf_op jit(solution)/shard_map/ppermute | solution.py:367
  107.1 5.5 %collective-permute-done.20.refs_8_ = bf16[1024,128]{1,0:T(8,128)(2,1)S(1)} collective-permute-done((bf16[1024,128]{1,0:T(8,128)(2,1)S(1)}, bf16[1024,128]{1,0:T(8,128)(2,1)S(1)}, u32[]{:S(2)}, u32[]{:S(2)}) %collective-permute-start.20) | collective-permute-done | bytes 262176 | tf_op jit(solution)/shard_map/ppermute | solution.py:367
  112.6 2.2 middle.1
  114.8 2.7 %collective-permute-start.22 = (bf16[1024,128]{1,0:T(8,128)(2,1)S(1)}, bf16[1024,128]{1,0:T(8,128)(2,1)S(1)}, u32[]{:S(2)}, u32[]{:S(2)}) collective-permute-start(bf16[1024,128]{1,0:T(8,128)(2,1)S(1)} %get-tuple-element.42.first), channel_id=1, source_target_pairs={{4,0},{5,1},{6,2},{7,3},{0,4},{1,5},{2,6},{3,7},{12,8},{13,9},{14,... | collective-permute-start | bytes 786440 | tf_op jit(solution)/shard_map/ppermute | solution.py:367
  117.5 3.1 %collective-permute-start.23 = (bf16[1024,128]{1,0:T(8,128)(2,1)S(1)}, bf16[1024,128]{1,0:T(8,128)(2,1)S(1)}, u32[]{:S(2)}, u32[]{:S(2)}) collective-permute-start(bf16[1024,128]{1,0:T(8,128)(2,1)S(1)} %get-tuple-element.43.refs_0_), channel_id=1, source_target_pairs={{1,0},{2,1},{3,2},{0,3},{5,4},{6,5},{7,6},{4,7},{9,8},{10,9},{11,1... | collective-permute-start | bytes 786440 | tf_op jit(solution)/shard_map/ppermute | solution.py:367
  121.3 1.4 collective-permute-done.22.first_pair
  122.7 4.2 %collective-permute-done.23.refs_1_ = bf16[1024,128]{1,0:T(8,128)(2,1)S(1)} collective-permute-done((bf16[1024,128]{1,0:T(8,128)(2,1)S(1)}, bf16[1024,128]{1,0:T(8,128)(2,1)S(1)}, u32[]{:S(2)}, u32[]{:S(2)}) %collective-permute-start.23) | collective-permute-done | bytes 262176 | tf_op jit(solution)/shard_map/ppermute | solution.py:367
  126.9 2.0 collective-permute-done.24.refs_2_
  128.9 7.1 %collective-permute-done.25.refs_3_ = bf16[1024,128]{1,0:T(8,128)(2,1)S(1)} collective-permute-done((bf16[1024,128]{1,0:T(8,128)(2,1)S(1)}, bf16[1024,128]{1,0:T(8,128)(2,1)S(1)}, u32[]{:S(2)}, u32[]{:S(2)}) %collective-permute-start.25) | collective-permute-done | bytes 262176 | tf_op jit(solution)/shard_map/ppermute | solution.py:367
  137.2 13.3 %collective-permute-done.32 = f32[256,256]{1,0:T(8,128)S(1)} collective-permute-done((f32[256,256]{1,0:T(8,128)S(1)}, f32[256,256]{1,0:T(8,128)S(1)}, u32[]{:S(2)}, u32[]{:S(2)}) %collective-permute-start.32) | collective-permute-done | bytes 262176 | tf_op jit(solution)/shard_map/ppermute | solution.py:367
  150.5 6.5 %collective-permute-done.30 = f32[256,256]{1,0:T(8,128)S(1)} collective-permute-done((f32[256,256]{1,0:T(8,128)S(1)}, f32[256,256]{1,0:T(8,128)S(1)}, u32[]{:S(2)}, u32[]{:S(2)}) %collective-permute-start.30) | collective-permute-done | bytes 262176 | tf_op jit(solution)/shard_map/ppermute | solution.py:367
  157.1 6.7 %collective-permute-done.28.refs_9_ = bf16[2048,128]{1,0:T(8,128)(2,1)S(1)} collective-permute-done((bf16[2048,128]{1,0:T(8,128)(2,1)S(1)}, bf16[2048,128]{1,0:T(8,128)(2,1)S(1)}, u32[]{:S(2)}, u32[]{:S(2)}) %collective-permute-start.28) | collective-permute-done | bytes 524320 | tf_op jit(solution)/shard_map/ppermute | solution.py:367
  163.9 13.2 %backward.1 = (bf16[8192,128]{1,0:T(8,128)(2,1)}, bf16[8192,128]{1,0:T(8,128)(2,1)}, bf16[8192,128]{1,0:T(8,128)(2,1)}, bf16[8192,128]{1,0:T(8,128)(2,1)}) custom-call(s32[1]{0:T(128)} %bitcast.5.refs_0_, s32[384]{0:T(512)S(1)} %get-tuple-element.68.refs_1_, s32[384]{0:T(512)S(1)} %get-tuple-element.65.refs_2_, s32[16]{0:T(128)S(1)} %fusion.29.refs_3_, ...), custom_call_target="tpu_custom_call" | custom-call | flops 1024 | bytes 1024 | tf_op jit(solution)/shard_map/backward/pallas_call | solution.py:238
  177.6 2.7 %collective-permute-start.43 = (f32[256,256]{1,0:T(8,128)S(1)}, f32[256,256]{1,0:T(8,128)S(1)}, u32[]{:S(2)}, u32[]{:S(2)}) collective-permute-start(f32[256,256]{1,0:T(8,128)S(1)} %add_add_fusion.1.refs_11_), channel_id=1, source_target_pairs={{1,0},{2,1},{3,2},{0,3},{5,4},{6,5},{7,6},{4,7},{9,8},{10,9},{11,1... | collective-permute-start | bytes 786440 | tf_op jit(solution)/shard_map/ppermute | solution.py:367
  180.3 1.2 collective-permute-done.37
  181.5 2.2 add_convert_fusion
  183.7 2.7 %collective-permute-start.38 = (bf16[4096,128]{1,0:T(8,128)(2,1)S(1)}, bf16[4096,128]{1,0:T(8,128)(2,1)S(1)}, u32[]{:S(2)}, u32[]{:S(2)}) collective-permute-start(bf16[4096,128]{1,0:T(8,128)(2,1)S(1)} %get-tuple-element.57), channel_id=1, source_target_pairs={{64,0},{80,16},{96,32},{112,48},{0,64},{16,80},{32,96},{48,112},{6... | collective-permute-start | bytes 3145736 | tf_op jit(solution)/shard_map/ppermute | solution.py:367
  187.1 5.4 %collective-permute-done.45 = f32[256,256]{1,0:T(8,128)S(1)} collective-permute-done((f32[256,256]{1,0:T(8,128)S(1)}, f32[256,256]{1,0:T(8,128)S(1)}, u32[]{:S(2)}, u32[]{:S(2)}) %collective-permute-start.45) | collective-permute-done | bytes 262176 | tf_op jit(solution)/shard_map/ppermute | solution.py:367
  192.7 1.5 collective-permute-start.46
  194.2 1.2 collective-permute-done.46
  195.4 4.3 %collective-permute-start.49 = (f32[256,256]{1,0:T(8,128)S(1)}, f32[256,256]{1,0:T(8,128)S(1)}, u32[]{:S(2)}, u32[]{:S(2)}) collective-permute-start(f32[256,256]{1,0:T(8,128)S(1)} %add.149), channel_id=1, source_target_pairs={{68,0},{64,4},{4,64},{0,68},{69,1},{65,5},{5,65},{1,69},{70,2},{66... | collective-permute-start | bytes 786440 | tf_op jit(solution)/shard_map/ppermute | solution.py:367
  199.7 12.7 %collective-permute-done.34.refs_1_ = bf16[2048,128]{1,0:T(8,128)(2,1)S(1)} collective-permute-done((bf16[2048,128]{1,0:T(8,128)(2,1)S(1)}, bf16[2048,128]{1,0:T(8,128)(2,1)S(1)}, u32[]{:S(2)}, u32[]{:S(2)}) %collective-permute-start.34) | collective-permute-done | bytes 524320 | tf_op jit(solution)/shard_map/ppermute | solution.py:367
  214.8 2.9 %collective-permute-start.40 = (bf16[1024,128]{1,0:T(8,128)(2,1)S(1)}, bf16[1024,128]{1,0:T(8,128)(2,1)S(1)}, u32[]{:S(2)}, u32[]{:S(2)}) collective-permute-start(bf16[1024,128]{1,0:T(8,128)(2,1)S(1)} %get-tuple-element.52), channel_id=1, source_target_pairs={{48,0},{0,16},{16,32},{32,48},{112,64},{64,80},{80,96},{96,112},{4... | collective-permute-start | bytes 786440 | tf_op jit(solution)/shard_map/ppermute | solution.py:367
  218.6 1.4 collective-permute-start.42
  220.0 3.3 %collective-permute-done.47 = f32[256,256]{1,0:T(8,128)S(1)} collective-permute-done((f32[256,256]{1,0:T(8,128)S(1)}, f32[256,256]{1,0:T(8,128)S(1)}, u32[]{:S(2)}, u32[]{:S(2)}) %collective-permute-start.47) | collective-permute-done | bytes 262176 | tf_op jit(solution)/shard_map/ppermute | solution.py:367
  224.2 5.7 %collective-permute-done.39.refs_4_ = bf16[1024,128]{1,0:T(8,128)(2,1)S(1)} collective-permute-done((bf16[1024,128]{1,0:T(8,128)(2,1)S(1)}, bf16[1024,128]{1,0:T(8,128)(2,1)S(1)}, u32[]{:S(2)}, u32[]{:S(2)}) %collective-permute-start.39) | collective-permute-done | bytes 262176 | tf_op jit(solution)/shard_map/ppermute | solution.py:367
  229.9 1.4 final.1
  (91 shorter events, 17.8 us)
Async XLA Ops:
  1.7 8.6 %collective-permute-start = (bf16[1024,128]{1,0:T(8,128)(2,1)S(1)}, bf16[1024,128]{1,0:T(8,128)(2,1)S(1)}, u32[]{:S(2)}, u32[]{:S(2)}) collective-permute-start(bf16[1024,128]{1,0:T(8,128)(2,1)S(1)} %get-tuple-element.64.first), channel_id=1, source_target_pairs={{64,0},{80,16},{96,32},{112,48},{0,64},{16,80},{32,96},{48,112},{6... | collective-permute-start | bytes 786440 | tf_op jit(solution)/shard_map/ppermute | solution.py:367
  4.3 8.4 %collective-permute-start.1 = (bf16[1024,128]{1,0:T(8,128)(2,1)S(1)}, bf16[1024,128]{1,0:T(8,128)(2,1)S(1)}, u32[]{:S(2)}, u32[]{:S(2)}) collective-permute-start(bf16[1024,128]{1,0:T(8,128)(2,1)S(1)} %get-tuple-element.63.refs_0_), channel_id=1, source_target_pairs={{16,0},{32,16},{48,32},{0,48},{80,64},{96,80},{112,96},{64,112},{1... | collective-permute-start | bytes 786440 | tf_op jit(solution)/shard_map/ppermute | solution.py:367
  7.0 8.1 %collective-permute-start.2 = (bf16[1024,128]{1,0:T(8,128)(2,1)S(1)}, bf16[1024,128]{1,0:T(8,128)(2,1)S(1)}, u32[]{:S(2)}, u32[]{:S(2)}) collective-permute-start(bf16[1024,128]{1,0:T(8,128)(2,1)S(1)} %get-tuple-element.63.refs_0_), channel_id=1, source_target_pairs={{32,0},{48,16},{0,32},{16,48},{96,64},{112,80},{64,96},{80,112},{3... | collective-permute-start | bytes 786440 | tf_op jit(solution)/shard_map/ppermute | solution.py:367
  7.4 15.0 %collective-permute-start.3 = (bf16[1024,128]{1,0:T(8,128)(2,1)S(1)}, bf16[1024,128]{1,0:T(8,128)(2,1)S(1)}, u32[]{:S(2)}, u32[]{:S(2)}) collective-permute-start(bf16[1024,128]{1,0:T(8,128)(2,1)S(1)} %get-tuple-element.63.refs_0_), channel_id=1, source_target_pairs={{48,0},{0,16},{16,32},{32,48},{112,64},{64,80},{80,96},{96,112},{4... | collective-permute-start | bytes 786440 | tf_op jit(solution)/shard_map/ppermute | solution.py:367
  22.5 24.4 %collective-permute-start.7 = (bf16[4096,128]{1,0:T(8,128)(2,1)S(1)}, bf16[4096,128]{1,0:T(8,128)(2,1)S(1)}, u32[]{:S(2)}, u32[]{:S(2)}) collective-permute-start(bf16[4096,128]{1,0:T(8,128)(2,1)S(1)} %get-tuple-element.30.refs_5_), channel_id=1, source_target_pairs={{64,0},{80,16},{96,32},{112,48},{0,64},{16,80},{32,96},{48,112},{6... | collective-permute-start | bytes 3145736 | tf_op jit(solution)/shard_map/ppermute | solution.py:367
  22.6 12.8 %collective-permute-start.4 = (bf16[2048,128]{1,0:T(8,128)(2,1)S(1)}, bf16[2048,128]{1,0:T(8,128)(2,1)}, u32[]{:S(2)}, u32[]{:S(2)}) collective-permute-start(bf16[2048,128]{1,0:T(8,128)(2,1)S(1)} %get-tuple-element.29.refs_4_), channel_id=1, source_target_pairs={{16,0},{32,16},{48,32},{0,48},{80,64},{96,80},{112,96},{64,112},{1... | collective-permute-start | bytes 1572872 | tf_op jit(solution)/shard_map/ppermute | solution.py:367
  22.6 25.5 %collective-permute-start.5 = (bf16[2048,128]{1,0:T(8,128)(2,1)S(1)}, bf16[2048,128]{1,0:T(8,128)(2,1)}, u32[]{:S(2)}, u32[]{:S(2)}) collective-permute-start(bf16[2048,128]{1,0:T(8,128)(2,1)S(1)} %get-tuple-element.29.refs_4_), channel_id=1, source_target_pairs={{32,0},{48,16},{0,32},{16,48},{96,64},{112,80},{64,96},{80,112},{3... | collective-permute-start | bytes 1572872 | tf_op jit(solution)/shard_map/ppermute | solution.py:367
  23.1 26.3 %collective-permute-start.6 = (bf16[2048,128]{1,0:T(8,128)(2,1)S(1)}, bf16[2048,128]{1,0:T(8,128)(2,1)}, u32[]{:S(2)}, u32[]{:S(2)}) collective-permute-start(bf16[2048,128]{1,0:T(8,128)(2,1)S(1)} %get-tuple-element.29.refs_4_), channel_id=1, source_target_pairs={{48,0},{0,16},{16,32},{32,48},{112,64},{64,80},{80,96},{96,112},{4... | collective-permute-start | bytes 1572872 | tf_op jit(solution)/shard_map/ppermute | solution.py:367
  24.1 27.4 %collective-permute-start.9 = (bf16[4096,128]{1,0:T(8,128)(2,1)S(1)}, bf16[4096,128]{1,0:T(8,128)(2,1)S(1)}, u32[]{:S(2)}, u32[]{:S(2)}) collective-permute-start(bf16[4096,128]{1,0:T(8,128)(2,1)S(1)} %get-tuple-element.30.refs_5_), channel_id=1, source_target_pairs={{8,0},{0,8},{9,1},{1,9},{10,2},{2,10},{11,3},{3,11},{12,4},{4,12},... | collective-permute-start | bytes 3145736 | tf_op jit(solution)/shard_map/ppermute | solution.py:367
  35.4 14.5 %collective-permute-start.8 = (bf16[2048,128]{1,0:T(8,128)(2,1)S(1)}, bf16[2048,128]{1,0:T(8,128)(2,1)S(1)}, u32[]{:S(2)}, u32[]{:S(2)}) collective-permute-start(bf16[2048,128]{1,0:T(8,128)(2,1)S(1)} %get-tuple-element.29.refs_4_), channel_id=1, source_target_pairs={{8,0},{0,8},{9,1},{1,9},{10,2},{2,10},{11,3},{3,11},{12,4},{4,12},... | collective-permute-start | bytes 1572872 | tf_op jit(solution)/shard_map/ppermute | solution.py:367
  46.9 6.1 %collective-permute-start.13 = (bf16[4096,128]{1,0:T(8,128)(2,1)S(1)}, bf16[4096,128]{1,0:T(8,128)(2,1)}, u32[]{:S(2)}, u32[]{:S(2)}) collective-permute-start(bf16[4096,128]{1,0:T(8,128)(2,1)S(1)} %collective-permute-done.7.refs_9_), channel_id=1, source_target_pairs={{8,0},{0,8},{9,1},{1,9},{10,2},{2,10},{11,3},{3,11},{12,4},{4,12},... | collective-permute-start | bytes 3145736 | tf_op jit(solution)/shard_map/ppermute | solution.py:367
  48.1 3.4 %collective-permute-start.10 = (bf16[2048,128]{1,0:T(8,128)(2,1)}, bf16[2048,128]{1,0:T(8,128)(2,1)}, u32[]{:S(2)}, u32[]{:S(2)}) collective-permute-start(bf16[2048,128]{1,0:T(8,128)(2,1)} %collective-permute-done.4.refs_6_), channel_id=1, source_target_pairs={{8,0},{0,8},{9,1},{1,9},{10,2},{2,10},{11,3},{3,11},{12,4},{4,12},... | collective-permute-start | bytes 1572872 | tf_op jit(solution)/shard_map/ppermute | solution.py:367
  49.4 2.8 %collective-permute-start.11 = (bf16[2048,128]{1,0:T(8,128)(2,1)}, bf16[2048,128]{1,0:T(8,128)(2,1)}, u32[]{:S(2)}, u32[]{:S(2)}) collective-permute-start(bf16[2048,128]{1,0:T(8,128)(2,1)} %collective-permute-done.5.refs_7_), channel_id=1, source_target_pairs={{8,0},{0,8},{9,1},{1,9},{10,2},{2,10},{11,3},{3,11},{12,4},{4,12},... | collective-permute-start | bytes 1572872 | tf_op jit(solution)/shard_map/ppermute | solution.py:367
  68.1 28.9 %collective-permute-start.17 = (bf16[4096,128]{1,0:T(8,128)(2,1)S(1)}, bf16[4096,128]{1,0:T(8,128)(2,1)S(1)}, u32[]{:S(2)}, u32[]{:S(2)}) collective-permute-start(bf16[4096,128]{1,0:T(8,128)(2,1)S(1)} %get-tuple-element.36), channel_id=1, source_target_pairs={{4,0},{5,1},{6,2},{7,3},{0,4},{1,5},{2,6},{3,7},{12,8},{13,9},{14,... | collective-permute-start | bytes 3145736 | tf_op jit(solution)/shard_map/ppermute | solution.py:367
  71.5 23.2 %collective-permute-start.14 = (bf16[2048,128]{1,0:T(8,128)(2,1)S(1)}, bf16[2048,128]{1,0:T(8,128)(2,1)S(1)}, u32[]{:S(2)}, u32[]{:S(2)}) collective-permute-start(bf16[2048,128]{1,0:T(8,128)(2,1)S(1)} %get-tuple-element.32), channel_id=1, source_target_pairs={{3,0},{0,1},{1,2},{2,3},{7,4},{4,5},{5,6},{6,7},{11,8},{8,9},{9,10... | collective-permute-start | bytes 1572872 | tf_op jit(solution)/shard_map/ppermute | solution.py:367
  72.7 22.0 %collective-permute-start.15 = (bf16[2048,128]{1,0:T(8,128)(2,1)S(1)}, bf16[2048,128]{1,0:T(8,128)(2,1)S(1)}, u32[]{:S(2)}, u32[]{:S(2)}) collective-permute-start(bf16[2048,128]{1,0:T(8,128)(2,1)S(1)} %get-tuple-element.33), channel_id=1, source_target_pairs={{2,0},{3,1},{0,2},{1,3},{6,4},{7,5},{4,6},{5,7},{10,8},{11,9},{8,1... | collective-permute-start | bytes 1572872 | tf_op jit(solution)/shard_map/ppermute | solution.py:367
  72.7 24.3 %collective-permute-start.16 = (bf16[2048,128]{1,0:T(8,128)(2,1)S(1)}, bf16[2048,128]{1,0:T(8,128)(2,1)S(1)}, u32[]{:S(2)}, u32[]{:S(2)}) collective-permute-start(bf16[2048,128]{1,0:T(8,128)(2,1)S(1)} %get-tuple-element.34), channel_id=1, source_target_pairs={{1,0},{2,1},{3,2},{0,3},{5,4},{6,5},{7,6},{4,7},{9,8},{10,9},{11,1... | collective-permute-start | bytes 1572872 | tf_op jit(solution)/shard_map/ppermute | solution.py:367
  97.3 9.8 %collective-permute-start.18 = (bf16[1024,128]{1,0:T(8,128)(2,1)S(1)}, bf16[1024,128]{1,0:T(8,128)(2,1)S(1)}, u32[]{:S(2)}, u32[]{:S(2)}) collective-permute-start(bf16[1024,128]{1,0:T(8,128)(2,1)S(1)} %get-tuple-element.37), channel_id=1, source_target_pairs={{4,0},{5,1},{6,2},{7,3},{0,4},{1,5},{2,6},{3,7},{12,8},{13,9},{14,... | collective-permute-start | bytes 786440 | tf_op jit(solution)/shard_map/ppermute | solution.py:367
  97.4 9.7 %collective-permute-start.19 = (bf16[1024,128]{1,0:T(8,128)(2,1)S(1)}, bf16[1024,128]{1,0:T(8,128)(2,1)S(1)}, u32[]{:S(2)}, u32[]{:S(2)}) collective-permute-start(bf16[1024,128]{1,0:T(8,128)(2,1)S(1)} %get-tuple-element.38), channel_id=1, source_target_pairs={{3,0},{0,1},{1,2},{2,3},{7,4},{4,5},{5,6},{6,7},{11,8},{8,9},{9,10... | collective-permute-start | bytes 786440 | tf_op jit(solution)/shard_map/ppermute | solution.py:367
  99.9 12.7 %collective-permute-start.20 = (bf16[1024,128]{1,0:T(8,128)(2,1)S(1)}, bf16[1024,128]{1,0:T(8,128)(2,1)S(1)}, u32[]{:S(2)}, u32[]{:S(2)}) collective-permute-start(bf16[1024,128]{1,0:T(8,128)(2,1)S(1)} %get-tuple-element.39), channel_id=1, source_target_pairs={{2,0},{3,1},{0,2},{1,3},{6,4},{7,5},{4,6},{5,7},{10,8},{11,9},{8,1... | collective-permute-start | bytes 786440 | tf_op jit(solution)/shard_map/ppermute | solution.py:367
  101.2 11.4 %collective-permute-start.21 = (bf16[1024,128]{1,0:T(8,128)(2,1)S(1)}, bf16[1024,128]{1,0:T(8,128)(2,1)S(1)}, u32[]{:S(2)}, u32[]{:S(2)}) collective-permute-start(bf16[1024,128]{1,0:T(8,128)(2,1)S(1)} %get-tuple-element.40), channel_id=1, source_target_pairs={{1,0},{2,1},{3,2},{0,3},{5,4},{6,5},{7,6},{4,7},{9,8},{10,9},{11,1... | collective-permute-start | bytes 786440 | tf_op jit(solution)/shard_map/ppermute | solution.py:367
  114.8 7.9 %collective-permute-start.22 = (bf16[1024,128]{1,0:T(8,128)(2,1)S(1)}, bf16[1024,128]{1,0:T(8,128)(2,1)S(1)}, u32[]{:S(2)}, u32[]{:S(2)}) collective-permute-start(bf16[1024,128]{1,0:T(8,128)(2,1)S(1)} %get-tuple-element.42.first), channel_id=1, source_target_pairs={{4,0},{5,1},{6,2},{7,3},{0,4},{1,5},{2,6},{3,7},{12,8},{13,9},{14,... | collective-permute-start | bytes 786440 | tf_op jit(solution)/shard_map/ppermute | solution.py:367
  117.5 9.4 %collective-permute-start.23 = (bf16[1024,128]{1,0:T(8,128)(2,1)S(1)}, bf16[1024,128]{1,0:T(8,128)(2,1)S(1)}, u32[]{:S(2)}, u32[]{:S(2)}) collective-permute-start(bf16[1024,128]{1,0:T(8,128)(2,1)S(1)} %get-tuple-element.43.refs_0_), channel_id=1, source_target_pairs={{1,0},{2,1},{3,2},{0,3},{5,4},{6,5},{7,6},{4,7},{9,8},{10,9},{11,1... | collective-permute-start | bytes 786440 | tf_op jit(solution)/shard_map/ppermute | solution.py:367
  120.6 8.3 %collective-permute-start.24 = (bf16[1024,128]{1,0:T(8,128)(2,1)S(1)}, bf16[1024,128]{1,0:T(8,128)(2,1)S(1)}, u32[]{:S(2)}, u32[]{:S(2)}) collective-permute-start(bf16[1024,128]{1,0:T(8,128)(2,1)S(1)} %get-tuple-element.43.refs_0_), channel_id=1, source_target_pairs={{2,0},{3,1},{0,2},{1,3},{6,4},{7,5},{4,6},{5,7},{10,8},{11,9},{8,1... | collective-permute-start | bytes 786440 | tf_op jit(solution)/shard_map/ppermute | solution.py:367
  121.3 14.6 %collective-permute-start.25 = (bf16[1024,128]{1,0:T(8,128)(2,1)S(1)}, bf16[1024,128]{1,0:T(8,128)(2,1)S(1)}, u32[]{:S(2)}, u32[]{:S(2)}) collective-permute-start(bf16[1024,128]{1,0:T(8,128)(2,1)S(1)} %get-tuple-element.43.refs_0_), channel_id=1, source_target_pairs={{3,0},{0,1},{1,2},{2,3},{7,4},{4,5},{5,6},{6,7},{11,8},{8,9},{9,10... | collective-permute-start | bytes 786440 | tf_op jit(solution)/shard_map/ppermute | solution.py:367
  136.0 27.8 %collective-permute-start.29 = (bf16[4096,128]{1,0:T(8,128)(2,1)S(1)}, bf16[4096,128]{1,0:T(8,128)(2,1)S(1)}, u32[]{:S(2)}, u32[]{:S(2)}) collective-permute-start(bf16[4096,128]{1,0:T(8,128)(2,1)S(1)} %get-tuple-element.45.refs_6_), channel_id=1, source_target_pairs={{4,0},{5,1},{6,2},{7,3},{0,4},{1,5},{2,6},{3,7},{12,8},{13,9},{14,... | collective-permute-start | bytes 3145736 | tf_op jit(solution)/shard_map/ppermute | solution.py:367
  136.2 14.3 %collective-permute-start.32 = (f32[256,256]{1,0:T(8,128)S(1)}, f32[256,256]{1,0:T(8,128)S(1)}, u32[]{:S(2)}, u32[]{:S(2)}) collective-permute-start(f32[256,256]{1,0:T(8,128)S(1)} %get-tuple-element.46), channel_id=1, source_target_pairs={{48,0},{0,16},{16,32},{32,48},{112,64},{64,80},{80,96},{96,112},{4... | collective-permute-start | bytes 786440 | tf_op jit(solution)/shard_map/ppermute | solution.py:367
  136.2 14.3 %collective-permute-start.31 = (f32[256,256]{1,0:T(8,128)S(1)}, f32[256,256]{1,0:T(8,128)S(1)}, u32[]{:S(2)}, u32[]{:S(2)}) collective-permute-start(f32[256,256]{1,0:T(8,128)S(1)} %get-tuple-element.46), channel_id=1, source_target_pairs={{32,0},{48,16},{0,32},{16,48},{96,64},{112,80},{64,96},{80,112},{3... | collective-permute-start | bytes 786440 | tf_op jit(solution)/shard_map/ppermute | solution.py:367
  136.3 20.8 %collective-permute-start.26 = (bf16[2048,128]{1,0:T(8,128)(2,1)S(1)}, bf16[2048,128]{1,0:T(8,128)(2,1)S(1)}, u32[]{:S(2)}, u32[]{:S(2)}) collective-permute-start(bf16[2048,128]{1,0:T(8,128)(2,1)S(1)} %get-tuple-element.44.refs_5_), channel_id=1, source_target_pairs={{1,0},{2,1},{3,2},{0,3},{5,4},{6,5},{7,6},{4,7},{9,8},{10,9},{11,1... | collective-permute-start | bytes 1572872 | tf_op jit(solution)/shard_map/ppermute | solution.py:367
  136.4 20.7 %collective-permute-start.27 = (bf16[2048,128]{1,0:T(8,128)(2,1)S(1)}, bf16[2048,128]{1,0:T(8,128)(2,1)S(1)}, u32[]{:S(2)}, u32[]{:S(2)}) collective-permute-start(bf16[2048,128]{1,0:T(8,128)(2,1)S(1)} %get-tuple-element.44.refs_5_), channel_id=1, source_target_pairs={{2,0},{3,1},{0,2},{1,3},{6,4},{7,5},{4,6},{5,7},{10,8},{11,9},{8,1... | collective-permute-start | bytes 1572872 | tf_op jit(solution)/shard_map/ppermute | solution.py:367
  150.5 13.4 %collective-permute-start.28 = (bf16[2048,128]{1,0:T(8,128)(2,1)S(1)}, bf16[2048,128]{1,0:T(8,128)(2,1)S(1)}, u32[]{:S(2)}, u32[]{:S(2)}) collective-permute-start(bf16[2048,128]{1,0:T(8,128)(2,1)S(1)} %get-tuple-element.44.refs_5_), channel_id=1, source_target_pairs={{3,0},{0,1},{1,2},{2,3},{7,4},{4,5},{5,6},{6,7},{11,8},{8,9},{9,10... | collective-permute-start | bytes 1572872 | tf_op jit(solution)/shard_map/ppermute | solution.py:367
  150.5 6.5 %collective-permute-start.30 = (f32[256,256]{1,0:T(8,128)S(1)}, f32[256,256]{1,0:T(8,128)S(1)}, u32[]{:S(2)}, u32[]{:S(2)}) collective-permute-start(f32[256,256]{1,0:T(8,128)S(1)} %get-tuple-element.46), channel_id=1, source_target_pairs={{16,0},{32,16},{48,32},{0,48},{80,64},{96,80},{112,96},{64,112},{1... | collective-permute-start | bytes 786440 | tf_op jit(solution)/shard_map/ppermute | solution.py:367
  177.1 4.5 %collective-permute-start.37 = (bf16[8192,128]{1,0:T(8,128)(2,1)}, bf16[8192,128]{1,0:T(8,128)(2,1)S(1)}, u32[]{:S(2)}, u32[]{:S(2)}) collective-permute-start(bf16[8192,128]{1,0:T(8,128)(2,1)} %get-tuple-element.50), channel_id=1, source_target_pairs={{8,0},{0,8},{9,1},{1,9},{10,2},{2,10},{11,3},{3,11},{12,4},{4,12},... | collective-permute-start | bytes 6291464 | tf_op jit(solution)/shard_map/ppermute | solution.py:367
  177.1 9.3 %collective-permute-start.33 = (bf16[8192,128]{1,0:T(8,128)(2,1)}, bf16[8192,128]{1,0:T(8,128)(2,1)S(1)}, u32[]{:S(2)}, u32[]{:S(2)}) collective-permute-start(bf16[8192,128]{1,0:T(8,128)(2,1)} %get-tuple-element.48), channel_id=1, source_target_pairs={{8,0},{0,8},{9,1},{1,9},{10,2},{2,10},{11,3},{3,11},{12,4},{4,12},... | collective-permute-start | bytes 6291464 | tf_op jit(solution)/shard_map/ppermute | solution.py:367
  177.6 14.8 %collective-permute-start.45 = (f32[256,256]{1,0:T(8,128)S(1)}, f32[256,256]{1,0:T(8,128)S(1)}, u32[]{:S(2)}, u32[]{:S(2)}) collective-permute-start(f32[256,256]{1,0:T(8,128)S(1)} %add_add_fusion.1.refs_11_), channel_id=1, source_target_pairs={{3,0},{0,1},{1,2},{2,3},{7,4},{4,5},{5,6},{6,7},{11,8},{8,9},{9,10... | collective-permute-start | bytes 786440 | tf_op jit(solution)/shard_map/ppermute | solution.py:367
  177.6 14.8 %collective-permute-start.44 = (f32[256,256]{1,0:T(8,128)S(1)}, f32[256,256]{1,0:T(8,128)S(1)}, u32[]{:S(2)}, u32[]{:S(2)}) collective-permute-start(f32[256,256]{1,0:T(8,128)S(1)} %add_add_fusion.1.refs_11_), channel_id=1, source_target_pairs={{2,0},{3,1},{0,2},{1,3},{6,4},{7,5},{4,6},{5,7},{10,8},{11,9},{8,1... | collective-permute-start | bytes 786440 | tf_op jit(solution)/shard_map/ppermute | solution.py:367
  177.6 15.0 %collective-permute-start.43 = (f32[256,256]{1,0:T(8,128)S(1)}, f32[256,256]{1,0:T(8,128)S(1)}, u32[]{:S(2)}, u32[]{:S(2)}) collective-permute-start(f32[256,256]{1,0:T(8,128)S(1)} %add_add_fusion.1.refs_11_), channel_id=1, source_target_pairs={{1,0},{2,1},{3,2},{0,3},{5,4},{6,5},{7,6},{4,7},{9,8},{10,9},{11,1... | collective-permute-start | bytes 786440 | tf_op jit(solution)/shard_map/ppermute | solution.py:367
  183.7 30.3 %collective-permute-start.38 = (bf16[4096,128]{1,0:T(8,128)(2,1)S(1)}, bf16[4096,128]{1,0:T(8,128)(2,1)S(1)}, u32[]{:S(2)}, u32[]{:S(2)}) collective-permute-start(bf16[4096,128]{1,0:T(8,128)(2,1)S(1)} %get-tuple-element.57), channel_id=1, source_target_pairs={{64,0},{80,16},{96,32},{112,48},{0,64},{16,80},{32,96},{48,112},{6... | collective-permute-start | bytes 3145736 | tf_op jit(solution)/shard_map/ppermute | solution.py:367
  187.0 25.3 %collective-permute-start.34 = (bf16[2048,128]{1,0:T(8,128)(2,1)S(1)}, bf16[2048,128]{1,0:T(8,128)(2,1)S(1)}, u32[]{:S(2)}, u32[]{:S(2)}) collective-permute-start(bf16[2048,128]{1,0:T(8,128)(2,1)S(1)} %get-tuple-element.61), channel_id=1, source_target_pairs={{48,0},{0,16},{16,32},{32,48},{112,64},{64,80},{80,96},{96,112},{4... | collective-permute-start | bytes 1572872 | tf_op jit(solution)/shard_map/ppermute | solution.py:367
  192.5 20.9 %collective-permute-start.35 = (bf16[2048,128]{1,0:T(8,128)(2,1)S(1)}, bf16[2048,128]{1,0:T(8,128)(2,1)S(1)}, u32[]{:S(2)}, u32[]{:S(2)}) collective-permute-start(bf16[2048,128]{1,0:T(8,128)(2,1)S(1)} %get-tuple-element.60), channel_id=1, source_target_pairs={{32,0},{48,16},{0,32},{16,48},{96,64},{112,80},{64,96},{80,112},{3... | collective-permute-start | bytes 1572872 | tf_op jit(solution)/shard_map/ppermute | solution.py:367
  192.5 21.5 %collective-permute-start.36 = (bf16[2048,128]{1,0:T(8,128)(2,1)S(1)}, bf16[2048,128]{1,0:T(8,128)(2,1)S(1)}, u32[]{:S(2)}, u32[]{:S(2)}) collective-permute-start(bf16[2048,128]{1,0:T(8,128)(2,1)S(1)} %get-tuple-element.59), channel_id=1, source_target_pairs={{16,0},{32,16},{48,32},{0,48},{80,64},{96,80},{112,96},{64,112},{1... | collective-permute-start | bytes 1572872 | tf_op jit(solution)/shard_map/ppermute | solution.py:367
  195.4 22.2 %collective-permute-start.49 = (f32[256,256]{1,0:T(8,128)S(1)}, f32[256,256]{1,0:T(8,128)S(1)}, u32[]{:S(2)}, u32[]{:S(2)}) collective-permute-start(f32[256,256]{1,0:T(8,128)S(1)} %add.149), channel_id=1, source_target_pairs={{68,0},{64,4},{4,64},{0,68},{69,1},{65,5},{5,65},{1,69},{70,2},{66... | collective-permute-start | bytes 786440 | tf_op jit(solution)/shard_map/ppermute | solution.py:367
  212.4 6.3 %collective-permute-start.48 = (f32[256,256]{1,0:T(8,128)S(1)}, f32[256,256]{1,0:T(8,128)S(1)}, u32[]{:S(2)}, u32[]{:S(2)}) collective-permute-start(f32[256,256]{1,0:T(8,128)S(1)} %add.149), channel_id=1, source_target_pairs={{64,0},{68,4},{0,64},{4,68},{65,1},{69,5},{1,65},{5,69},{66,2},{70... | collective-permute-start | bytes 786440 | tf_op jit(solution)/shard_map/ppermute | solution.py:367
  213.4 10.0 %collective-permute-start.47 = (f32[256,256]{1,0:T(8,128)S(1)}, f32[256,256]{1,0:T(8,128)S(1)}, u32[]{:S(2)}, u32[]{:S(2)}) collective-permute-start(f32[256,256]{1,0:T(8,128)S(1)} %add.149), channel_id=1, source_target_pairs={{4,0},{0,4},{68,64},{64,68},{5,1},{1,5},{69,65},{65,69},{6,2},{2,6... | collective-permute-start | bytes 786440 | tf_op jit(solution)/shard_map/ppermute | solution.py:367
  214.3 15.6 %collective-permute-start.39 = (bf16[1024,128]{1,0:T(8,128)(2,1)S(1)}, bf16[1024,128]{1,0:T(8,128)(2,1)S(1)}, u32[]{:S(2)}, u32[]{:S(2)}) collective-permute-start(bf16[1024,128]{1,0:T(8,128)(2,1)S(1)} %get-tuple-element.51), channel_id=1, source_target_pairs={{64,0},{80,16},{96,32},{112,48},{0,64},{16,80},{32,96},{48,112},{6... | collective-permute-start | bytes 786440 | tf_op jit(solution)/shard_map/ppermute | solution.py:367
  214.8 15.1 %collective-permute-start.40 = (bf16[1024,128]{1,0:T(8,128)(2,1)S(1)}, bf16[1024,128]{1,0:T(8,128)(2,1)S(1)}, u32[]{:S(2)}, u32[]{:S(2)}) collective-permute-start(bf16[1024,128]{1,0:T(8,128)(2,1)S(1)} %get-tuple-element.52), channel_id=1, source_target_pairs={{48,0},{0,16},{16,32},{32,48},{112,64},{64,80},{80,96},{96,112},{4... | collective-permute-start | bytes 786440 | tf_op jit(solution)/shard_map/ppermute | solution.py:367
  217.6 12.2 %collective-permute-start.41 = (bf16[1024,128]{1,0:T(8,128)(2,1)S(1)}, bf16[1024,128]{1,0:T(8,128)(2,1)S(1)}, u32[]{:S(2)}, u32[]{:S(2)}) collective-permute-start(bf16[1024,128]{1,0:T(8,128)(2,1)S(1)} %get-tuple-element.53), channel_id=1, source_target_pairs={{32,0},{48,16},{0,32},{16,48},{96,64},{112,80},{64,96},{80,112},{3... | collective-permute-start | bytes 786440 | tf_op jit(solution)/shard_map/ppermute | solution.py:367
  218.6 11.2 %collective-permute-start.42 = (bf16[1024,128]{1,0:T(8,128)(2,1)S(1)}, bf16[1024,128]{1,0:T(8,128)(2,1)S(1)}, u32[]{:S(2)}, u32[]{:S(2)}) collective-permute-start(bf16[1024,128]{1,0:T(8,128)(2,1)S(1)} %get-tuple-element.54), channel_id=1, source_target_pairs={{16,0},{32,16},{48,32},{0,48},{80,64},{96,80},{112,96},{64,112},{1... | collective-permute-start | bytes 786440 | tf_op jit(solution)/shard_map/ppermute | solution.py:367
  (12 other events, 162.1 us)

commit v5 on v4

--- a/solution.py
+++ b/solution.py
@@ -367,6 +367,12 @@
     return lax.ppermute(value, axes, perm)
 
 
+def exchange(value, axis, pairs):
+    size = lax.axis_size(axis)
+    perm = [(((((index + pairs) ^ 1) - pairs) % size), index) for index in range(size)]
+    return lax.ppermute(value, axis, perm)
+
+
 def add(*terms):
     return functools.reduce(lambda a, b: a + b, [term.astype(F32) for term in terms])
 
@@ -497,7 +503,8 @@
     activations, first, second, weight_term = middle(arrived, weight, layer_bias, cotangent, PARTS)
 
     early, later = gather(first, second, col_axes)
-    weight_sum = add(*around(weight_term, row_axes, (2, 4), [(0, 1), (0, 2), (0, 3)]))
+    weight_sum = weight_term + exchange(weight_term, "y", 0)
+    weight_sum = weight_sum + exchange(weight_sum, "y", 1)
     results = backward_sweep(
         count, row_at, col_to, slab_at, tiles, early + later + [weight_sum], GATHERED + [[]], nodes, width
     )
@@ -512,11 +519,13 @@
             done += len(slabs)
     collected = scatter(held, row_axes)
     grad_features = final(collected, weight, PARTS)
-    weight_sum = add(*around(weight_sum, "x", (4,), [(1,), (2,), (3,)]))
-    weight_sum = add(*around(weight_sum, "core", (2,), [(1,)]))
-    grad_weight = add(*around(weight_sum, ("zl", "zh"), (2, 2), [(0, 1), (1, 0), (1, 1)]))
+    _, *others = around(weight_sum.astype(BF16), "x", (4,), [(1,), (2,), (3,)])
+    weight_sum = add(weight_sum, *others)
+    weight_sum = weight_sum + exchange(weight_sum, "core", 0)
+    _, *others = around(weight_sum.astype(BF16), ("zl", "zh"), (2, 2), [(0, 1), (1, 0), (1, 1)])
+    weight_sum = add(weight_sum, *others)
     total_nodes = nodes * 128
-    return activations, grad_features, grad_weight * float(total_nodes) ** -0.5
+    return activations, grad_features, weight_sum * float(total_nodes) ** -0.5
 
 
 def solution(mesh):

time: 235 us -> 230 us (0.979); the launches traced: 231 us -> 231 us
  starting transfers between devices: 52.8 us -> 67.7 us
  Pallas kernels: 30.6 us -> 18.9 us
  waiting for transfers between devices: 138 us -> 134 us
    ppermute x50 -> x46, waiting for transfers between devices: 138 us -> 123 us  [shift(): return lax.ppermute(value, axes, perm)]
    ppermute x50 -> x46, starting transfers between devices: 52.8 us -> 65.6 us  [shift(): return lax.ppermute(value, axes, perm)]
    ppermute x0 -> x3, waiting for transfers between devices: none -> 10.8 us  [exchange(): return lax.ppermute(value, axis, perm)]
    pallas_call x1, Pallas kernels: 13 us -> 6.94 us  [forward_sweep(): pl.pallas_call(functools.partial(forward_kernel, source_plan, result_plan...]
    pallas_call x1, Pallas kernels: 13.2 us -> 7.6 us  [backward_sweep(): pl.pallas_call(functools.partial(backward_kernel, source_plan, slab, batc...]
  transfers between devices with their start and end apart: 50 -> 49, of which waited for: 27 -> 26; matrix products, arithmetic and copies ran while one was open for 2% -> 2% of each run, Pallas kernels for 0% -> 0%
where the time goes in v5:
time: 230 us; the launch traced here: 231 us
  waiting for transfers between devices  134 us (58%)
  starting transfers between devices  67.7 us (29%)
  Pallas kernels  18.9 us (8%)
  local copies, waits for them, and re-layouts  4.77 us (2%)
  other arithmetic  3.83 us (2%)
    ppermute x46, waiting for transfers between devices, shift(): return lax.ppermute(value, axes, perm)  123 us
    ppermute x46, starting transfers between devices, shift(): return lax.ppermute(value, axes, perm)  65.6 us
    ppermute x3, waiting for transfers between devices, exchange(): return lax.ppermute(value, axis, perm)  10.8 us
    pallas_call x1, Pallas kernels, backward_sweep(): pl.pallas_call(functools.partial(backward_kernel, source_plan, slab, batc...  7.6 us
    pallas_call x1, Pallas kernels, forward_sweep(): pl.pallas_call(functools.partial(forward_kernel, source_plan, result_plan...  6.94 us
  transfers between devices with their start and end apart: 49, of which 26 were waited for; matrix products, arithmetic and copies ran while one was open for 2% of the time, Pallas kernels for 0%

profile of v5, /device:TPU:1, one launch (start us, length us, event | category | flops | bytes accessed | tf_op | source)
XLA Modules:
  0.0 230.6 jit_solution(5341843085774074088)
XLA Ops:
  0.7 1.1 fusion.38
  1.7 2.5 %collective-permute-start = (bf16[1024,128]{1,0:T(8,128)(2,1)S(1)}, bf16[1024,128]{1,0:T(8,128)(2,1)S(1)}, u32[]{:S(2)}, u32[]{:S(2)}) collective-permute-start(bf16[1024,128]{1,0:T(8,128)(2,1)S(1)} %get-tuple-element.68.first), channel_id=1, source_target_pairs={{64,0},{80,16},{96,32},{112,48},{0,64},{16,80},{32,96},{48,112},{6... | collective-permute-start | bytes 786440 | tf_op jit(solution)/shard_map/ppermute | solution.py:367
  4.3 2.7 %collective-permute-start.1 = (bf16[1024,128]{1,0:T(8,128)(2,1)S(1)}, bf16[1024,128]{1,0:T(8,128)(2,1)S(1)}, u32[]{:S(2)}, u32[]{:S(2)}) collective-permute-start(bf16[1024,128]{1,0:T(8,128)(2,1)S(1)} %get-tuple-element.67.refs_0_), channel_id=1, source_target_pairs={{16,0},{32,16},{48,32},{0,48},{80,64},{96,80},{112,96},{64,112},{1... | collective-permute-start | bytes 786440 | tf_op jit(solution)/shard_map/ppermute | solution.py:367
  8.1 2.2 collective-permute-done.first_pair
  10.3 2.4 %collective-permute-done.1.refs_1_ = bf16[1024,128]{1,0:T(8,128)(2,1)S(1)} collective-permute-done((bf16[1024,128]{1,0:T(8,128)(2,1)S(1)}, bf16[1024,128]{1,0:T(8,128)(2,1)S(1)}, u32[]{:S(2)}, u32[]{:S(2)}) %collective-permute-start.1) | collective-permute-done | bytes 262176 | tf_op jit(solution)/shard_map/ppermute | solution.py:367
  12.7 2.4 %collective-permute-done.2.refs_2_ = bf16[1024,128]{1,0:T(8,128)(2,1)S(1)} collective-permute-done((bf16[1024,128]{1,0:T(8,128)(2,1)S(1)}, bf16[1024,128]{1,0:T(8,128)(2,1)S(1)}, u32[]{:S(2)}, u32[]{:S(2)}) %collective-permute-start.2) | collective-permute-done | bytes 262176 | tf_op jit(solution)/shard_map/ppermute | solution.py:367
  15.1 7.2 %collective-permute-done.3.refs_3_ = bf16[1024,128]{1,0:T(8,128)(2,1)S(1)} collective-permute-done((bf16[1024,128]{1,0:T(8,128)(2,1)S(1)}, bf16[1024,128]{1,0:T(8,128)(2,1)S(1)}, u32[]{:S(2)}, u32[]{:S(2)}) %collective-permute-start.3) | collective-permute-done | bytes 262176 | tf_op jit(solution)/shard_map/ppermute | solution.py:367
  24.1 1.4 collective-permute-start.9
  25.5 10.0 %collective-permute-done.4.refs_6_ = bf16[2048,128]{1,0:T(8,128)(2,1)} collective-permute-done((bf16[2048,128]{1,0:T(8,128)(2,1)S(1)}, bf16[2048,128]{1,0:T(8,128)(2,1)}, u32[]{:S(2)}, u32[]{:S(2)}) %collective-permute-start.4) | collective-permute-done | bytes 524320 | tf_op jit(solution)/shard_map/ppermute | solution.py:367
  35.4 2.9 %collective-permute-start.8 = (bf16[2048,128]{1,0:T(8,128)(2,1)S(1)}, bf16[2048,128]{1,0:T(8,128)(2,1)S(1)}, u32[]{:S(2)}, u32[]{:S(2)}) collective-permute-start(bf16[2048,128]{1,0:T(8,128)(2,1)S(1)} %get-tuple-element.29.refs_4_), channel_id=1, source_target_pairs={{8,0},{0,8},{9,1},{1,9},{10,2},{2,10},{11,3},{3,11},{12,4},{4,12},... | collective-permute-start | bytes 1572872 | tf_op jit(solution)/shard_map/ppermute | solution.py:367
  39.1 7.8 %collective-permute-done.7.refs_9_ = bf16[4096,128]{1,0:T(8,128)(2,1)S(1)} collective-permute-done((bf16[4096,128]{1,0:T(8,128)(2,1)S(1)}, bf16[4096,128]{1,0:T(8,128)(2,1)S(1)}, u32[]{:S(2)}, u32[]{:S(2)}) %collective-permute-start.7) | collective-permute-done | bytes 1048608 | tf_op jit(solution)/shard_map/ppermute | solution.py:367
  46.9 1.2 collective-permute-start.13
  48.1 1.3 collective-permute-done.6.refs_8_
  55.1 6.9 %forward.1 = (bf16[2048,128]{1,0:T(8,128)(2,1)S(1)}, bf16[2048,128]{1,0:T(8,128)(2,1)S(1)}, bf16[2048,128]{1,0:T(8,128)(2,1)S(1)}, bf16[2048,128]{1,0:T(8,128)(2...) custom-call(s32[1]{0:T(128)} %bitcast.4.refs_0_, s32[384]{0:T(512)S(1)} %get-tuple-element.70.refs_1_, ...), custom_call_target="tpu_custom_call" | custom-call | flops 1024 | bytes 1024 | tf_op jit(solution)/shard_map/forward/pallas_call | solution.py:124
  62.0 3.4 %collective-permute-start.17 = (bf16[4096,128]{1,0:T(8,128)(2,1)S(1)}, bf16[4096,128]{1,0:T(8,128)(2,1)S(1)}, u32[]{:S(2)}, u32[]{:S(2)}) collective-permute-start(bf16[4096,128]{1,0:T(8,128)(2,1)S(1)} %get-tuple-element.36), channel_id=1, source_target_pairs={{4,0},{5,1},{6,2},{7,3},{0,4},{1,5},{2,6},{3,7},{12,8},{13,9},{14,... | collective-permute-start | bytes 3145736 | tf_op jit(solution)/shard_map/ppermute | solution.py:367
  65.4 1.2 collective-permute-start.14
  66.6 5.3 %collective-permute-start.15 = (bf16[2048,128]{1,0:T(8,128)(2,1)S(1)}, bf16[2048,128]{1,0:T(8,128)(2,1)S(1)}, u32[]{:S(2)}, u32[]{:S(2)}) collective-permute-start(bf16[2048,128]{1,0:T(8,128)(2,1)S(1)} %get-tuple-element.33), channel_id=1, source_target_pairs={{2,0},{3,1},{0,2},{1,3},{6,4},{7,5},{4,6},{5,7},{10,8},{11,9},{8,1... | collective-permute-start | bytes 1572872 | tf_op jit(solution)/shard_map/ppermute | solution.py:367
  71.9 6.7 %collective-permute-done.14.refs_1_ = bf16[2048,128]{1,0:T(8,128)(2,1)S(1)} collective-permute-done((bf16[2048,128]{1,0:T(8,128)(2,1)S(1)}, bf16[2048,128]{1,0:T(8,128)(2,1)S(1)}, u32[]{:S(2)}, u32[]{:S(2)}) %collective-permute-start.14) | collective-permute-done | bytes 524320 | tf_op jit(solution)/shard_map/ppermute | solution.py:367
  78.6 12.6 %collective-permute-done.15.refs_2_ = bf16[2048,128]{1,0:T(8,128)(2,1)S(1)} collective-permute-done((bf16[2048,128]{1,0:T(8,128)(2,1)S(1)}, bf16[2048,128]{1,0:T(8,128)(2,1)S(1)}, u32[]{:S(2)}, u32[]{:S(2)}) %collective-permute-start.15) | collective-permute-done | bytes 524320 | tf_op jit(solution)/shard_map/ppermute | solution.py:367
  91.2 2.8 %collective-permute-done.16.refs_3_ = bf16[2048,128]{1,0:T(8,128)(2,1)S(1)} collective-permute-done((bf16[2048,128]{1,0:T(8,128)(2,1)S(1)}, bf16[2048,128]{1,0:T(8,128)(2,1)S(1)}, u32[]{:S(2)}, u32[]{:S(2)}) %collective-permute-start.16) | collective-permute-done | bytes 524320 | tf_op jit(solution)/shard_map/ppermute | solution.py:367
  94.3 3.3 %collective-permute-start.18 = (bf16[1024,128]{1,0:T(8,128)(2,1)S(1)}, bf16[1024,128]{1,0:T(8,128)(2,1)S(1)}, u32[]{:S(2)}, u32[]{:S(2)}) collective-permute-start(bf16[1024,128]{1,0:T(8,128)(2,1)S(1)} %get-tuple-element.37), channel_id=1, source_target_pairs={{4,0},{5,1},{6,2},{7,3},{0,4},{1,5},{2,6},{3,7},{12,8},{13,9},{14,... | collective-permute-start | bytes 786440 | tf_op jit(solution)/shard_map/ppermute | solution.py:367
  98.2 3.6 %collective-permute-start.20 = (bf16[1024,128]{1,0:T(8,128)(2,1)S(1)}, bf16[1024,128]{1,0:T(8,128)(2,1)S(1)}, u32[]{:S(2)}, u32[]{:S(2)}) collective-permute-start(bf16[1024,128]{1,0:T(8,128)(2,1)S(1)} %get-tuple-element.39), channel_id=1, source_target_pairs={{2,0},{3,1},{0,2},{1,3},{6,4},{7,5},{4,6},{5,7},{10,8},{11,9},{8,1... | collective-permute-start | bytes 786440 | tf_op jit(solution)/shard_map/ppermute | solution.py:367
  102.2 3.0 %collective-permute-done.19.refs_7_ = bf16[1024,128]{1,0:T(8,128)(2,1)S(1)} collective-permute-done((bf16[1024,128]{1,0:T(8,128)(2,1)S(1)}, bf16[1024,128]{1,0:T(8,128)(2,1)S(1)}, u32[]{:S(2)}, u32[]{:S(2)}) %collective-permute-start.19) | collective-permute-done | bytes 262176 | tf_op jit(solution)/shard_map/ppermute | solution.py:367
  105.3 7.7 %collective-permute-done.20.refs_8_ = bf16[1024,128]{1,0:T(8,128)(2,1)S(1)} collective-permute-done((bf16[1024,128]{1,0:T(8,128)(2,1)S(1)}, bf16[1024,128]{1,0:T(8,128)(2,1)S(1)}, u32[]{:S(2)}, u32[]{:S(2)}) %collective-permute-start.20) | collective-permute-done | bytes 262176 | tf_op jit(solution)/shard_map/ppermute | solution.py:367
  113.0 2.2 middle.1
  115.4 3.0 %collective-permute-start.23 = (bf16[1024,128]{1,0:T(8,128)(2,1)S(1)}, bf16[1024,128]{1,0:T(8,128)(2,1)S(1)}, u32[]{:S(2)}, u32[]{:S(2)}) collective-permute-start(bf16[1024,128]{1,0:T(8,128)(2,1)S(1)} %get-tuple-element.43.refs_0_), channel_id=1, source_target_pairs={{1,0},{2,1},{3,2},{0,3},{5,4},{6,5},{7,6},{4,7},{9,8},{10,9},{11,1... | collective-permute-start | bytes 786440 | tf_op jit(solution)/shard_map/ppermute | solution.py:367
  118.9 3.9 %collective-permute-done.22.first_pair = bf16[1024,128]{1,0:T(8,128)(2,1)S(1)} collective-permute-done((bf16[1024,128]{1,0:T(8,128)(2,1)S(1)}, bf16[1024,128]{1,0:T(8,128)(2,1)S(1)}, u32[]{:S(2)}, u32[]{:S(2)}) %collective-permute-start.22) | collective-permute-done | bytes 262176 | tf_op jit(solution)/shard_map/ppermute | solution.py:367
  122.9 5.8 %collective-permute-done.23.refs_1_ = bf16[1024,128]{1,0:T(8,128)(2,1)S(1)} collective-permute-done((bf16[1024,128]{1,0:T(8,128)(2,1)S(1)}, bf16[1024,128]{1,0:T(8,128)(2,1)S(1)}, u32[]{:S(2)}, u32[]{:S(2)}) %collective-permute-start.23) | collective-permute-done | bytes 262176 | tf_op jit(solution)/shard_map/ppermute | solution.py:367
  128.7 4.4 %collective-permute-done.25.refs_3_ = bf16[1024,128]{1,0:T(8,128)(2,1)S(1)} collective-permute-done((bf16[1024,128]{1,0:T(8,128)(2,1)S(1)}, bf16[1024,128]{1,0:T(8,128)(2,1)S(1)}, u32[]{:S(2)}, u32[]{:S(2)}) %collective-permute-start.25) | collective-permute-done | bytes 262176 | tf_op jit(solution)/shard_map/ppermute | solution.py:367
  133.2 2.9 %collective-permute-start.29 = (bf16[4096,128]{1,0:T(8,128)(2,1)S(1)}, bf16[4096,128]{1,0:T(8,128)(2,1)S(1)}, u32[]{:S(2)}, u32[]{:S(2)}) collective-permute-start(bf16[4096,128]{1,0:T(8,128)(2,1)S(1)} %get-tuple-element.45.refs_6_), channel_id=1, source_target_pairs={{4,0},{5,1},{6,2},{7,3},{0,4},{1,5},{2,6},{3,7},{12,8},{13,9},{14,... | collective-permute-start | bytes 3145736 | tf_op jit(solution)/shard_map/ppermute | solution.py:367
  137.5 5.2 %collective-permute-done.30 = f32[256,256]{1,0:T(8,128)S(1)} collective-permute-done((f32[256,256]{1,0:T(8,128)S(1)}, f32[256,256]{1,0:T(8,128)S(1)}, u32[]{:S(2)}, u32[]{:S(2)}) %collective-permute-start.30) | collective-permute-done | bytes 262176 | tf_op jit(solution)/shard_map/ppermute | solution.py:373
  142.7 1.4 collective-permute-start.31
  144.1 5.6 %collective-permute-done.31 = f32[256,256]{1,0:T(8,128)S(1)} collective-permute-done((f32[256,256]{1,0:T(8,128)S(1)}, f32[256,256]{1,0:T(8,128)S(1)}, u32[]{:S(2)}, u32[]{:S(2)}) %collective-permute-start.31) | collective-permute-done | bytes 262176 | tf_op jit(solution)/shard_map/ppermute | solution.py:373
  149.8 12.8 %collective-permute-done.28.refs_9_ = bf16[2048,128]{1,0:T(8,128)(2,1)S(1)} collective-permute-done((bf16[2048,128]{1,0:T(8,128)(2,1)S(1)}, bf16[2048,128]{1,0:T(8,128)(2,1)S(1)}, u32[]{:S(2)}, u32[]{:S(2)}) %collective-permute-start.28) | collective-permute-done | bytes 524320 | tf_op jit(solution)/shard_map/ppermute | solution.py:367
  162.6 7.6 %backward.1 = (bf16[8192,128]{1,0:T(8,128)(2,1)}, bf16[8192,128]{1,0:T(8,128)(2,1)}, bf16[8192,128]{1,0:T(8,128)(2,1)}, bf16[8192,128]{1,0:T(8,128)(2,1)}) custom-call(s32[1]{0:T(128)} %bitcast.5.refs_0_, s32[384]{0:T(512)S(1)} %get-tuple-element.72.refs_1_, s32[384]{0:T(512)S(1)} %get-tuple-element.69.refs_2_, s32[16]{0:T(128)S(1)} %fusion.29.refs_3_, ...), custom_call_target="tpu_custom_call" | custom-call | flops 1024 | bytes 1024 | tf_op jit(solution)/shard_map/backward/pallas_call | solution.py:238
  170.8 6.1 %collective-permute-start.43 = (bf16[256,256]{1,0:T(8,128)(2,1)S(1)}, bf16[256,256]{1,0:T(8,128)(2,1)S(1)}, u32[]{:S(2)}, u32[]{:S(2)}) collective-permute-start(bf16[256,256]{1,0:T(8,128)(2,1)S(1)} %get-tuple-element.57), channel_id=1, source_target_pairs={{2,0},{3,1},{0,2},{1,3},{6,4},{7,5},{4,6},{5,7},{10,8},{11,9},{8,1... | collective-permute-start | bytes 393224 | tf_op jit(solution)/shard_map/ppermute | solution.py:367
  177.0 2.2 add_convert_fusion
  179.9 5.7 %collective-permute-start.33 = (bf16[2048,128]{1,0:T(8,128)(2,1)S(1)}, bf16[2048,128]{1,0:T(8,128)(2,1)S(1)}, u32[]{:S(2)}, u32[]{:S(2)}) collective-permute-start(bf16[2048,128]{1,0:T(8,128)(2,1)S(1)} %get-tuple-element.65), channel_id=1, source_target_pairs={{48,0},{0,16},{16,32},{32,48},{112,64},{64,80},{80,96},{96,112},{4... | collective-permute-start | bytes 1572872 | tf_op jit(solution)/shard_map/ppermute | solution.py:367
  186.4 3.3 %collective-permute-start.34 = (bf16[2048,128]{1,0:T(8,128)(2,1)S(1)}, bf16[2048,128]{1,0:T(8,128)(2,1)S(1)}, u32[]{:S(2)}, u32[]{:S(2)}) collective-permute-start(bf16[2048,128]{1,0:T(8,128)(2,1)S(1)} %get-tuple-element.64), channel_id=1, source_target_pairs={{32,0},{48,16},{0,32},{16,48},{96,64},{112,80},{64,96},{80,112},{3... | collective-permute-start | bytes 1572872 | tf_op jit(solution)/shard_map/ppermute | solution.py:367
  189.7 1.4 collective-permute-start.35
  191.3 6.5 %collective-permute-done.33.refs_1_ = bf16[2048,128]{1,0:T(8,128)(2,1)S(1)} collective-permute-done((bf16[2048,128]{1,0:T(8,128)(2,1)S(1)}, bf16[2048,128]{1,0:T(8,128)(2,1)S(1)}, u32[]{:S(2)}, u32[]{:S(2)}) %collective-permute-start.33) | collective-permute-done | bytes 524320 | tf_op jit(solution)/shard_map/ppermute | solution.py:367
  198.8 11.2 %collective-permute-done.34.refs_2_ = bf16[2048,128]{1,0:T(8,128)(2,1)S(1)} collective-permute-done((bf16[2048,128]{1,0:T(8,128)(2,1)S(1)}, bf16[2048,128]{1,0:T(8,128)(2,1)S(1)}, u32[]{:S(2)}, u32[]{:S(2)}) %collective-permute-start.34) | collective-permute-done | bytes 524320 | tf_op jit(solution)/shard_map/ppermute | solution.py:367
  210.0 2.7 %collective-permute-start.46 = (bf16[256,256]{1,0:T(8,128)(2,1)S(1)}, bf16[256,256]{1,0:T(8,128)(2,1)S(1)}, u32[]{:S(2)}, u32[]{:S(2)}) collective-permute-start(bf16[256,256]{1,0:T(8,128)(2,1)S(1)} %get-tuple-element.55), channel_id=1, source_target_pairs={{4,0},{0,4},{68,64},{64,68},{5,1},{1,5},{69,65},{65,69},{6,2},{2,6... | collective-permute-start | bytes 393224 | tf_op jit(solution)/shard_map/ppermute | solution.py:367
  212.9 1.2 collective-permute-start.38
  214.8 3.2 %collective-permute-start.40 = (bf16[1024,128]{1,0:T(8,128)(2,1)S(1)}, bf16[1024,128]{1,0:T(8,128)(2,1)S(1)}, u32[]{:S(2)}, u32[]{:S(2)}) collective-permute-start(bf16[1024,128]{1,0:T(8,128)(2,1)S(1)} %get-tuple-element.53), channel_id=1, source_target_pairs={{32,0},{48,16},{0,32},{16,48},{96,64},{112,80},{64,96},{80,112},{3... | collective-permute-start | bytes 786440 | tf_op jit(solution)/shard_map/ppermute | solution.py:367
  219.0 2.1 collective-permute-done.38.refs_4_
  222.1 7.2 %collective-permute-done.40.refs_8_ = bf16[1024,128]{1,0:T(8,128)(2,1)S(1)} collective-permute-done((bf16[1024,128]{1,0:T(8,128)(2,1)S(1)}, bf16[1024,128]{1,0:T(8,128)(2,1)S(1)}, u32[]{:S(2)}, u32[]{:S(2)}) %collective-permute-start.40) | collective-permute-done | bytes 262176 | tf_op jit(solution)/shard_map/ppermute | solution.py:367
  229.3 1.3 final.1
  (90 shorter events, 18.4 us)
Async XLA Ops:
  1.7 8.6 %collective-permute-start = (bf16[1024,128]{1,0:T(8,128)(2,1)S(1)}, bf16[1024,128]{1,0:T(8,128)(2,1)S(1)}, u32[]{:S(2)}, u32[]{:S(2)}) collective-permute-start(bf16[1024,128]{1,0:T(8,128)(2,1)S(1)} %get-tuple-element.68.first), channel_id=1, source_target_pairs={{64,0},{80,16},{96,32},{112,48},{0,64},{16,80},{32,96},{48,112},{6... | collective-permute-start | bytes 786440 | tf_op jit(solution)/shard_map/ppermute | solution.py:367
  4.3 8.4 %collective-permute-start.1 = (bf16[1024,128]{1,0:T(8,128)(2,1)S(1)}, bf16[1024,128]{1,0:T(8,128)(2,1)S(1)}, u32[]{:S(2)}, u32[]{:S(2)}) collective-permute-start(bf16[1024,128]{1,0:T(8,128)(2,1)S(1)} %get-tuple-element.67.refs_0_), channel_id=1, source_target_pairs={{16,0},{32,16},{48,32},{0,48},{80,64},{96,80},{112,96},{64,112},{1... | collective-permute-start | bytes 786440 | tf_op jit(solution)/shard_map/ppermute | solution.py:367
  7.0 8.1 %collective-permute-start.2 = (bf16[1024,128]{1,0:T(8,128)(2,1)S(1)}, bf16[1024,128]{1,0:T(8,128)(2,1)S(1)}, u32[]{:S(2)}, u32[]{:S(2)}) collective-permute-start(bf16[1024,128]{1,0:T(8,128)(2,1)S(1)} %get-tuple-element.67.refs_0_), channel_id=1, source_target_pairs={{32,0},{48,16},{0,32},{16,48},{96,64},{112,80},{64,96},{80,112},{3... | collective-permute-start | bytes 786440 | tf_op jit(solution)/shard_map/ppermute | solution.py:367
  7.4 15.0 %collective-permute-start.3 = (bf16[1024,128]{1,0:T(8,128)(2,1)S(1)}, bf16[1024,128]{1,0:T(8,128)(2,1)S(1)}, u32[]{:S(2)}, u32[]{:S(2)}) collective-permute-start(bf16[1024,128]{1,0:T(8,128)(2,1)S(1)} %get-tuple-element.67.refs_0_), channel_id=1, source_target_pairs={{48,0},{0,16},{16,32},{32,48},{112,64},{64,80},{80,96},{96,112},{4... | collective-permute-start | bytes 786440 | tf_op jit(solution)/shard_map/ppermute | solution.py:367
  22.5 24.4 %collective-permute-start.7 = (bf16[4096,128]{1,0:T(8,128)(2,1)S(1)}, bf16[4096,128]{1,0:T(8,128)(2,1)S(1)}, u32[]{:S(2)}, u32[]{:S(2)}) collective-permute-start(bf16[4096,128]{1,0:T(8,128)(2,1)S(1)} %get-tuple-element.30.refs_5_), channel_id=1, source_target_pairs={{64,0},{80,16},{96,32},{112,48},{0,64},{16,80},{32,96},{48,112},{6... | collective-permute-start | bytes 3145736 | tf_op jit(solution)/shard_map/ppermute | solution.py:367
  22.6 12.8 %collective-permute-start.4 = (bf16[2048,128]{1,0:T(8,128)(2,1)S(1)}, bf16[2048,128]{1,0:T(8,128)(2,1)}, u32[]{:S(2)}, u32[]{:S(2)}) collective-permute-start(bf16[2048,128]{1,0:T(8,128)(2,1)S(1)} %get-tuple-element.29.refs_4_), channel_id=1, source_target_pairs={{16,0},{32,16},{48,32},{0,48},{80,64},{96,80},{112,96},{64,112},{1... | collective-permute-start | bytes 1572872 | tf_op jit(solution)/shard_map/ppermute | solution.py:367
  22.6 25.5 %collective-permute-start.5 = (bf16[2048,128]{1,0:T(8,128)(2,1)S(1)}, bf16[2048,128]{1,0:T(8,128)(2,1)}, u32[]{:S(2)}, u32[]{:S(2)}) collective-permute-start(bf16[2048,128]{1,0:T(8,128)(2,1)S(1)} %get-tuple-element.29.refs_4_), channel_id=1, source_target_pairs={{32,0},{48,16},{0,32},{16,48},{96,64},{112,80},{64,96},{80,112},{3... | collective-permute-start | bytes 1572872 | tf_op jit(solution)/shard_map/ppermute | solution.py:367
  23.1 26.3 %collective-permute-start.6 = (bf16[2048,128]{1,0:T(8,128)(2,1)S(1)}, bf16[2048,128]{1,0:T(8,128)(2,1)}, u32[]{:S(2)}, u32[]{:S(2)}) collective-permute-start(bf16[2048,128]{1,0:T(8,128)(2,1)S(1)} %get-tuple-element.29.refs_4_), channel_id=1, source_target_pairs={{48,0},{0,16},{16,32},{32,48},{112,64},{64,80},{80,96},{96,112},{4... | collective-permute-start | bytes 1572872 | tf_op jit(solution)/shard_map/ppermute | solution.py:367
  24.1 27.4 %collective-permute-start.9 = (bf16[4096,128]{1,0:T(8,128)(2,1)S(1)}, bf16[4096,128]{1,0:T(8,128)(2,1)S(1)}, u32[]{:S(2)}, u32[]{:S(2)}) collective-permute-start(bf16[4096,128]{1,0:T(8,128)(2,1)S(1)} %get-tuple-element.30.refs_5_), channel_id=1, source_target_pairs={{8,0},{0,8},{9,1},{1,9},{10,2},{2,10},{11,3},{3,11},{12,4},{4,12},... | collective-permute-start | bytes 3145736 | tf_op jit(solution)/shard_map/ppermute | solution.py:367
  35.4 14.5 %collective-permute-start.8 = (bf16[2048,128]{1,0:T(8,128)(2,1)S(1)}, bf16[2048,128]{1,0:T(8,128)(2,1)S(1)}, u32[]{:S(2)}, u32[]{:S(2)}) collective-permute-start(bf16[2048,128]{1,0:T(8,128)(2,1)S(1)} %get-tuple-element.29.refs_4_), channel_id=1, source_target_pairs={{8,0},{0,8},{9,1},{1,9},{10,2},{2,10},{11,3},{3,11},{12,4},{4,12},... | collective-permute-start | bytes 1572872 | tf_op jit(solution)/shard_map/ppermute | solution.py:367
  46.9 6.1 %collective-permute-start.13 = (bf16[4096,128]{1,0:T(8,128)(2,1)S(1)}, bf16[4096,128]{1,0:T(8,128)(2,1)}, u32[]{:S(2)}, u32[]{:S(2)}) collective-permute-start(bf16[4096,128]{1,0:T(8,128)(2,1)S(1)} %collective-permute-done.7.refs_9_), channel_id=1, source_target_pairs={{8,0},{0,8},{9,1},{1,9},{10,2},{2,10},{11,3},{3,11},{12,4},{4,12},... | collective-permute-start | bytes 3145736 | tf_op jit(solution)/shard_map/ppermute | solution.py:367
  48.1 3.4 %collective-permute-start.10 = (bf16[2048,128]{1,0:T(8,128)(2,1)}, bf16[2048,128]{1,0:T(8,128)(2,1)}, u32[]{:S(2)}, u32[]{:S(2)}) collective-permute-start(bf16[2048,128]{1,0:T(8,128)(2,1)} %collective-permute-done.4.refs_6_), channel_id=1, source_target_pairs={{8,0},{0,8},{9,1},{1,9},{10,2},{2,10},{11,3},{3,11},{12,4},{4,12},... | collective-permute-start | bytes 1572872 | tf_op jit(solution)/shard_map/ppermute | solution.py:367
  49.4 2.8 %collective-permute-start.11 = (bf16[2048,128]{1,0:T(8,128)(2,1)}, bf16[2048,128]{1,0:T(8,128)(2,1)}, u32[]{:S(2)}, u32[]{:S(2)}) collective-permute-start(bf16[2048,128]{1,0:T(8,128)(2,1)} %collective-permute-done.5.refs_7_), channel_id=1, source_target_pairs={{8,0},{0,8},{9,1},{1,9},{10,2},{2,10},{11,3},{3,11},{12,4},{4,12},... | collective-permute-start | bytes 1572872 | tf_op jit(solution)/shard_map/ppermute | solution.py:367
  62.0 32.0 %collective-permute-start.17 = (bf16[4096,128]{1,0:T(8,128)(2,1)S(1)}, bf16[4096,128]{1,0:T(8,128)(2,1)S(1)}, u32[]{:S(2)}, u32[]{:S(2)}) collective-permute-start(bf16[4096,128]{1,0:T(8,128)(2,1)S(1)} %get-tuple-element.36), channel_id=1, source_target_pairs={{4,0},{5,1},{6,2},{7,3},{0,4},{1,5},{2,6},{3,7},{12,8},{13,9},{14,... | collective-permute-start | bytes 3145736 | tf_op jit(solution)/shard_map/ppermute | solution.py:367
  65.4 13.2 %collective-permute-start.14 = (bf16[2048,128]{1,0:T(8,128)(2,1)S(1)}, bf16[2048,128]{1,0:T(8,128)(2,1)S(1)}, u32[]{:S(2)}, u32[]{:S(2)}) collective-permute-start(bf16[2048,128]{1,0:T(8,128)(2,1)S(1)} %get-tuple-element.32), channel_id=1, source_target_pairs={{3,0},{0,1},{1,2},{2,3},{7,4},{4,5},{5,6},{6,7},{11,8},{8,9},{9,10... | collective-permute-start | bytes 1572872 | tf_op jit(solution)/shard_map/ppermute | solution.py:367
  66.6 24.6 %collective-permute-start.15 = (bf16[2048,128]{1,0:T(8,128)(2,1)S(1)}, bf16[2048,128]{1,0:T(8,128)(2,1)S(1)}, u32[]{:S(2)}, u32[]{:S(2)}) collective-permute-start(bf16[2048,128]{1,0:T(8,128)(2,1)S(1)} %get-tuple-element.33), channel_id=1, source_target_pairs={{2,0},{3,1},{0,2},{1,3},{6,4},{7,5},{4,6},{5,7},{10,8},{11,9},{8,1... | collective-permute-start | bytes 1572872 | tf_op jit(solution)/shard_map/ppermute | solution.py:367
  71.9 22.1 %collective-permute-start.16 = (bf16[2048,128]{1,0:T(8,128)(2,1)S(1)}, bf16[2048,128]{1,0:T(8,128)(2,1)S(1)}, u32[]{:S(2)}, u32[]{:S(2)}) collective-permute-start(bf16[2048,128]{1,0:T(8,128)(2,1)S(1)} %get-tuple-element.34), channel_id=1, source_target_pairs={{1,0},{2,1},{3,2},{0,3},{5,4},{6,5},{7,6},{4,7},{9,8},{10,9},{11,1... | collective-permute-start | bytes 1572872 | tf_op jit(solution)/shard_map/ppermute | solution.py:367
  94.3 7.9 %collective-permute-start.18 = (bf16[1024,128]{1,0:T(8,128)(2,1)S(1)}, bf16[1024,128]{1,0:T(8,128)(2,1)S(1)}, u32[]{:S(2)}, u32[]{:S(2)}) collective-permute-start(bf16[1024,128]{1,0:T(8,128)(2,1)S(1)} %get-tuple-element.37), channel_id=1, source_target_pairs={{4,0},{5,1},{6,2},{7,3},{0,4},{1,5},{2,6},{3,7},{12,8},{13,9},{14,... | collective-permute-start | bytes 786440 | tf_op jit(solution)/shard_map/ppermute | solution.py:367
  97.7 7.6 %collective-permute-start.19 = (bf16[1024,128]{1,0:T(8,128)(2,1)S(1)}, bf16[1024,128]{1,0:T(8,128)(2,1)S(1)}, u32[]{:S(2)}, u32[]{:S(2)}) collective-permute-start(bf16[1024,128]{1,0:T(8,128)(2,1)S(1)} %get-tuple-element.38), channel_id=1, source_target_pairs={{3,0},{0,1},{1,2},{2,3},{7,4},{4,5},{5,6},{6,7},{11,8},{8,9},{9,10... | collective-permute-start | bytes 786440 | tf_op jit(solution)/shard_map/ppermute | solution.py:367
  98.2 14.8 %collective-permute-start.20 = (bf16[1024,128]{1,0:T(8,128)(2,1)S(1)}, bf16[1024,128]{1,0:T(8,128)(2,1)S(1)}, u32[]{:S(2)}, u32[]{:S(2)}) collective-permute-start(bf16[1024,128]{1,0:T(8,128)(2,1)S(1)} %get-tuple-element.39), channel_id=1, source_target_pairs={{2,0},{3,1},{0,2},{1,3},{6,4},{7,5},{4,6},{5,7},{10,8},{11,9},{8,1... | collective-permute-start | bytes 786440 | tf_op jit(solution)/shard_map/ppermute | solution.py:367
  101.8 11.2 %collective-permute-start.21 = (bf16[1024,128]{1,0:T(8,128)(2,1)S(1)}, bf16[1024,128]{1,0:T(8,128)(2,1)S(1)}, u32[]{:S(2)}, u32[]{:S(2)}) collective-permute-start(bf16[1024,128]{1,0:T(8,128)(2,1)S(1)} %get-tuple-element.40), channel_id=1, source_target_pairs={{1,0},{2,1},{3,2},{0,3},{5,4},{6,5},{7,6},{4,7},{9,8},{10,9},{11,1... | collective-permute-start | bytes 786440 | tf_op jit(solution)/shard_map/ppermute | solution.py:367
  115.2 7.6 %collective-permute-start.22 = (bf16[1024,128]{1,0:T(8,128)(2,1)S(1)}, bf16[1024,128]{1,0:T(8,128)(2,1)S(1)}, u32[]{:S(2)}, u32[]{:S(2)}) collective-permute-start(bf16[1024,128]{1,0:T(8,128)(2,1)S(1)} %get-tuple-element.42.first), channel_id=1, source_target_pairs={{4,0},{5,1},{6,2},{7,3},{0,4},{1,5},{2,6},{3,7},{12,8},{13,9},{14,... | collective-permute-start | bytes 786440 | tf_op jit(solution)/shard_map/ppermute | solution.py:367
  115.4 13.3 %collective-permute-start.23 = (bf16[1024,128]{1,0:T(8,128)(2,1)S(1)}, bf16[1024,128]{1,0:T(8,128)(2,1)S(1)}, u32[]{:S(2)}, u32[]{:S(2)}) collective-permute-start(bf16[1024,128]{1,0:T(8,128)(2,1)S(1)} %get-tuple-element.43.refs_0_), channel_id=1, source_target_pairs={{1,0},{2,1},{3,2},{0,3},{5,4},{6,5},{7,6},{4,7},{9,8},{10,9},{11,1... | collective-permute-start | bytes 786440 | tf_op jit(solution)/shard_map/ppermute | solution.py:367
  118.3 10.3 %collective-permute-start.24 = (bf16[1024,128]{1,0:T(8,128)(2,1)S(1)}, bf16[1024,128]{1,0:T(8,128)(2,1)S(1)}, u32[]{:S(2)}, u32[]{:S(2)}) collective-permute-start(bf16[1024,128]{1,0:T(8,128)(2,1)S(1)} %get-tuple-element.43.refs_0_), channel_id=1, source_target_pairs={{2,0},{3,1},{0,2},{1,3},{6,4},{7,5},{4,6},{5,7},{10,8},{11,9},{8,1... | collective-permute-start | bytes 786440 | tf_op jit(solution)/shard_map/ppermute | solution.py:367
  118.3 14.7 %collective-permute-start.25 = (bf16[1024,128]{1,0:T(8,128)(2,1)S(1)}, bf16[1024,128]{1,0:T(8,128)(2,1)S(1)}, u32[]{:S(2)}, u32[]{:S(2)}) collective-permute-start(bf16[1024,128]{1,0:T(8,128)(2,1)S(1)} %get-tuple-element.43.refs_0_), channel_id=1, source_target_pairs={{3,0},{0,1},{1,2},{2,3},{7,4},{4,5},{5,6},{6,7},{11,8},{8,9},{9,10... | collective-permute-start | bytes 786440 | tf_op jit(solution)/shard_map/ppermute | solution.py:367
  133.2 29.5 %collective-permute-start.29 = (bf16[4096,128]{1,0:T(8,128)(2,1)S(1)}, bf16[4096,128]{1,0:T(8,128)(2,1)S(1)}, u32[]{:S(2)}, u32[]{:S(2)}) collective-permute-start(bf16[4096,128]{1,0:T(8,128)(2,1)S(1)} %get-tuple-element.45.refs_6_), channel_id=1, source_target_pairs={{4,0},{5,1},{6,2},{7,3},{0,4},{1,5},{2,6},{3,7},{12,8},{13,9},{14,... | collective-permute-start | bytes 3145736 | tf_op jit(solution)/shard_map/ppermute | solution.py:367
  136.0 6.7 %collective-permute-start.30 = (f32[256,256]{1,0:T(8,128)S(1)}, f32[256,256]{1,0:T(8,128)S(1)}, u32[]{:S(2)}, u32[]{:S(2)}) collective-permute-start(f32[256,256]{1,0:T(8,128)S(1)} %get-tuple-element.46), channel_id=1, source_target_pairs={{16,0},{0,16},{48,32},{32,48},{17,1},{1,17},{49,33},{33,49},{18,2}... | collective-permute-start | bytes 786440 | tf_op jit(solution)/shard_map/ppermute | solution.py:373
  136.0 13.8 %collective-permute-start.26 = (bf16[2048,128]{1,0:T(8,128)(2,1)S(1)}, bf16[2048,128]{1,0:T(8,128)(2,1)S(1)}, u32[]{:S(2)}, u32[]{:S(2)}) collective-permute-start(bf16[2048,128]{1,0:T(8,128)(2,1)S(1)} %get-tuple-element.44.refs_5_), channel_id=1, source_target_pairs={{1,0},{2,1},{3,2},{0,3},{5,4},{6,5},{7,6},{4,7},{9,8},{10,9},{11,1... | collective-permute-start | bytes 1572872 | tf_op jit(solution)/shard_map/ppermute | solution.py:367
  136.0 13.8 %collective-permute-start.27 = (bf16[2048,128]{1,0:T(8,128)(2,1)S(1)}, bf16[2048,128]{1,0:T(8,128)(2,1)S(1)}, u32[]{:S(2)}, u32[]{:S(2)}) collective-permute-start(bf16[2048,128]{1,0:T(8,128)(2,1)S(1)} %get-tuple-element.44.refs_5_), channel_id=1, source_target_pairs={{2,0},{3,1},{0,2},{1,3},{6,4},{7,5},{4,6},{5,7},{10,8},{11,9},{8,1... | collective-permute-start | bytes 1572872 | tf_op jit(solution)/shard_map/ppermute | solution.py:367
  136.7 25.9 %collective-permute-start.28 = (bf16[2048,128]{1,0:T(8,128)(2,1)S(1)}, bf16[2048,128]{1,0:T(8,128)(2,1)S(1)}, u32[]{:S(2)}, u32[]{:S(2)}) collective-permute-start(bf16[2048,128]{1,0:T(8,128)(2,1)S(1)} %get-tuple-element.44.refs_5_), channel_id=1, source_target_pairs={{3,0},{0,1},{1,2},{2,3},{7,4},{4,5},{5,6},{6,7},{11,8},{8,9},{9,10... | collective-permute-start | bytes 1572872 | tf_op jit(solution)/shard_map/ppermute | solution.py:367
  142.7 7.0 %collective-permute-start.31 = (f32[256,256]{1,0:T(8,128)S(1)}, f32[256,256]{1,0:T(8,128)S(1)}, u32[]{:S(2)}, u32[]{:S(2)}) collective-permute-start(f32[256,256]{1,0:T(8,128)S(1)} %add.134), channel_id=1, source_target_pairs={{48,0},{32,16},{16,32},{0,48},{49,1},{33,17},{17,33},{1,49},{50,2}... | collective-permute-start | bytes 786440 | tf_op jit(solution)/shard_map/ppermute | solution.py:373
  170.2 6.7 %collective-permute-start.36 = (bf16[8192,128]{1,0:T(8,128)(2,1)}, bf16[8192,128]{1,0:T(8,128)(2,1)S(1)}, u32[]{:S(2)}, u32[]{:S(2)}) collective-permute-start(bf16[8192,128]{1,0:T(8,128)(2,1)} %get-tuple-element.50), channel_id=1, source_target_pairs={{8,0},{0,8},{9,1},{1,9},{10,2},{2,10},{11,3},{3,11},{12,4},{4,12},... | collective-permute-start | bytes 6291464 | tf_op jit(solution)/shard_map/ppermute | solution.py:367
  170.5 8.8 %collective-permute-start.32 = (bf16[8192,128]{1,0:T(8,128)(2,1)}, bf16[8192,128]{1,0:T(8,128)(2,1)S(1)}, u32[]{:S(2)}, u32[]{:S(2)}) collective-permute-start(bf16[8192,128]{1,0:T(8,128)(2,1)} %get-tuple-element.48), channel_id=1, source_target_pairs={{8,0},{0,8},{9,1},{1,9},{10,2},{2,10},{11,3},{3,11},{12,4},{4,12},... | collective-permute-start | bytes 6291464 | tf_op jit(solution)/shard_map/ppermute | solution.py:367
  170.8 14.8 %collective-permute-start.44 = (bf16[256,256]{1,0:T(8,128)(2,1)S(1)}, bf16[256,256]{1,0:T(8,128)(2,1)S(1)}, u32[]{:S(2)}, u32[]{:S(2)}) collective-permute-start(bf16[256,256]{1,0:T(8,128)(2,1)S(1)} %get-tuple-element.57), channel_id=1, source_target_pairs={{3,0},{0,1},{1,2},{2,3},{7,4},{4,5},{5,6},{6,7},{11,8},{8,9},{9,10... | collective-permute-start | bytes 393224 | tf_op jit(solution)/shard_map/ppermute | solution.py:367
  170.8 14.8 %collective-permute-start.43 = (bf16[256,256]{1,0:T(8,128)(2,1)S(1)}, bf16[256,256]{1,0:T(8,128)(2,1)S(1)}, u32[]{:S(2)}, u32[]{:S(2)}) collective-permute-start(bf16[256,256]{1,0:T(8,128)(2,1)S(1)} %get-tuple-element.57), channel_id=1, source_target_pairs={{2,0},{3,1},{0,2},{1,3},{6,4},{7,5},{4,6},{5,7},{10,8},{11,9},{8,1... | collective-permute-start | bytes 393224 | tf_op jit(solution)/shard_map/ppermute | solution.py:367
  177.0 8.6 %collective-permute-start.42 = (bf16[256,256]{1,0:T(8,128)(2,1)S(1)}, bf16[256,256]{1,0:T(8,128)(2,1)S(1)}, u32[]{:S(2)}, u32[]{:S(2)}) collective-permute-start(bf16[256,256]{1,0:T(8,128)(2,1)S(1)} %get-tuple-element.57), channel_id=1, source_target_pairs={{1,0},{2,1},{3,2},{0,3},{5,4},{6,5},{7,6},{4,7},{9,8},{10,9},{11,1... | collective-permute-start | bytes 393224 | tf_op jit(solution)/shard_map/ppermute | solution.py:367
  179.2 33.4 %collective-permute-start.37 = (bf16[4096,128]{1,0:T(8,128)(2,1)S(1)}, bf16[4096,128]{1,0:T(8,128)(2,1)S(1)}, u32[]{:S(2)}, u32[]{:S(2)}) collective-permute-start(bf16[4096,128]{1,0:T(8,128)(2,1)S(1)} %get-tuple-element.61), channel_id=1, source_target_pairs={{64,0},{80,16},{96,32},{112,48},{0,64},{16,80},{32,96},{48,112},{6... | collective-permute-start | bytes 3145736 | tf_op jit(solution)/shard_map/ppermute | solution.py:367
  179.9 18.0 %collective-permute-start.33 = (bf16[2048,128]{1,0:T(8,128)(2,1)S(1)}, bf16[2048,128]{1,0:T(8,128)(2,1)S(1)}, u32[]{:S(2)}, u32[]{:S(2)}) collective-permute-start(bf16[2048,128]{1,0:T(8,128)(2,1)S(1)} %get-tuple-element.65), channel_id=1, source_target_pairs={{48,0},{0,16},{16,32},{32,48},{112,64},{64,80},{80,96},{96,112},{4... | collective-permute-start | bytes 1572872 | tf_op jit(solution)/shard_map/ppermute | solution.py:367
  185.7 5.5 %collective-permute-start.45 = (f32[256,256]{1,0:T(8,128)S(1)}, f32[256,256]{1,0:T(8,128)S(1)}, u32[]{:S(2)}, u32[]{:S(2)}) collective-permute-start(f32[256,256]{1,0:T(8,128)S(1)} %convert_add_fusion), channel_id=1, source_target_pairs={{8,0},{0,8},{9,1},{1,9},{10,2},{2,10},{11,3},{3,11},{12,4},{4,12},... | collective-permute-start | bytes 786440 | tf_op jit(solution)/shard_map/ppermute | solution.py:373
  186.4 23.5 %collective-permute-start.34 = (bf16[2048,128]{1,0:T(8,128)(2,1)S(1)}, bf16[2048,128]{1,0:T(8,128)(2,1)S(1)}, u32[]{:S(2)}, u32[]{:S(2)}) collective-permute-start(bf16[2048,128]{1,0:T(8,128)(2,1)S(1)} %get-tuple-element.64), channel_id=1, source_target_pairs={{32,0},{48,16},{0,32},{16,48},{96,64},{112,80},{64,96},{80,112},{3... | collective-permute-start | bytes 1572872 | tf_op jit(solution)/shard_map/ppermute | solution.py:367
  189.7 22.9 %collective-permute-start.35 = (bf16[2048,128]{1,0:T(8,128)(2,1)S(1)}, bf16[2048,128]{1,0:T(8,128)(2,1)S(1)}, u32[]{:S(2)}, u32[]{:S(2)}) collective-permute-start(bf16[2048,128]{1,0:T(8,128)(2,1)S(1)} %get-tuple-element.63), channel_id=1, source_target_pairs={{16,0},{32,16},{48,32},{0,48},{80,64},{96,80},{112,96},{64,112},{1... | collective-permute-start | bytes 1572872 | tf_op jit(solution)/shard_map/ppermute | solution.py:367
  191.2 23.6 %collective-permute-start.48 = (bf16[256,256]{1,0:T(8,128)(2,1)S(1)}, bf16[256,256]{1,0:T(8,128)(2,1)S(1)}, u32[]{:S(2)}, u32[]{:S(2)}) collective-permute-start(bf16[256,256]{1,0:T(8,128)(2,1)S(1)} %get-tuple-element.55), channel_id=1, source_target_pairs={{68,0},{64,4},{4,64},{0,68},{69,1},{65,5},{5,65},{1,69},{70,2},{66... | collective-permute-start | bytes 393224 | tf_op jit(solution)/shard_map/ppermute | solution.py:367
  197.9 20.2 %collective-permute-start.47 = (bf16[256,256]{1,0:T(8,128)(2,1)S(1)}, bf16[256,256]{1,0:T(8,128)(2,1)S(1)}, u32[]{:S(2)}, u32[]{:S(2)}) collective-permute-start(bf16[256,256]{1,0:T(8,128)(2,1)S(1)} %get-tuple-element.55), channel_id=1, source_target_pairs={{64,0},{68,4},{0,64},{4,68},{65,1},{69,5},{1,65},{5,69},{66,2},{70... | collective-permute-start | bytes 393224 | tf_op jit(solution)/shard_map/ppermute | solution.py:367
  210.0 8.2 %collective-permute-start.46 = (bf16[256,256]{1,0:T(8,128)(2,1)S(1)}, bf16[256,256]{1,0:T(8,128)(2,1)S(1)}, u32[]{:S(2)}, u32[]{:S(2)}) collective-permute-start(bf16[256,256]{1,0:T(8,128)(2,1)S(1)} %get-tuple-element.55), channel_id=1, source_target_pairs={{4,0},{0,4},{68,64},{64,68},{5,1},{1,5},{69,65},{65,69},{6,2},{2,6... | collective-permute-start | bytes 393224 | tf_op jit(solution)/shard_map/ppermute | solution.py:367
  212.9 8.1 %collective-permute-start.38 = (bf16[1024,128]{1,0:T(8,128)(2,1)S(1)}, bf16[1024,128]{1,0:T(8,128)(2,1)S(1)}, u32[]{:S(2)}, u32[]{:S(2)}) collective-permute-start(bf16[1024,128]{1,0:T(8,128)(2,1)S(1)} %get-tuple-element.51), channel_id=1, source_target_pairs={{64,0},{80,16},{96,32},{112,48},{0,64},{16,80},{32,96},{48,112},{6... | collective-permute-start | bytes 786440 | tf_op jit(solution)/shard_map/ppermute | solution.py:367
  214.1 8.0 %collective-permute-start.39 = (bf16[1024,128]{1,0:T(8,128)(2,1)S(1)}, bf16[1024,128]{1,0:T(8,128)(2,1)S(1)}, u32[]{:S(2)}, u32[]{:S(2)}) collective-permute-start(bf16[1024,128]{1,0:T(8,128)(2,1)S(1)} %get-tuple-element.52), channel_id=1, source_target_pairs={{48,0},{0,16},{16,32},{32,48},{112,64},{64,80},{80,96},{96,112},{4... | collective-permute-start | bytes 786440 | tf_op jit(solution)/shard_map/ppermute | solution.py:367
  214.8 14.5 %collective-permute-start.40 = (bf16[1024,128]{1,0:T(8,128)(2,1)S(1)}, bf16[1024,128]{1,0:T(8,128)(2,1)S(1)}, u32[]{:S(2)}, u32[]{:S(2)}) collective-permute-start(bf16[1024,128]{1,0:T(8,128)(2,1)S(1)} %get-tuple-element.53), channel_id=1, source_target_pairs={{32,0},{48,16},{0,32},{16,48},{96,64},{112,80},{64,96},{80,112},{3... | collective-permute-start | bytes 786440 | tf_op jit(solution)/shard_map/ppermute | solution.py:367
  218.1 11.2 %collective-permute-start.41 = (bf16[1024,128]{1,0:T(8,128)(2,1)S(1)}, bf16[1024,128]{1,0:T(8,128)(2,1)S(1)}, u32[]{:S(2)}, u32[]{:S(2)}) collective-permute-start(bf16[1024,128]{1,0:T(8,128)(2,1)S(1)} %get-tuple-element.54), channel_id=1, source_target_pairs={{16,0},{32,16},{48,32},{0,48},{80,64},{96,80},{112,96},{64,112},{1... | collective-permute-start | bytes 786440 | tf_op jit(solution)/shard_map/ppermute | solution.py:367
  (11 other events, 166.9 us)

commit v6 on v5

--- a/solution.py
+++ b/solution.py
@@ -12,12 +12,12 @@
 F32 = jnp.float32
 ROW = ("zl", "y", "core")
 COL = ("zh", "x")
-FORWARD_LIMIT = 40 * 2**20
+FORWARD_LIMIT = 46 * 2**20
 BACKWARD_LIMIT = 48 * 2**20
 SMALL_LIMIT = 14 * 2**20
 PARTS = 2
-BATCH = 48
-CHUNK = 48
+BATCH = 64
+CHUNK = 64
 
 
 def accumulate(source_buf, tile_buf, total, src, dst, contract, batch, base):

time: 230 us -> 229 us (level)
  Pallas kernels: 18.9 us -> 23.4 us
  waiting for transfers between devices: 134 us -> 130 us
    ppermute x46, waiting for transfers between devices: 123 us -> 120 us  [shift(): return lax.ppermute(value, axes, perm)]
    pallas_call x1, Pallas kernels: 6.94 us -> 9.8 us  [forward_sweep(): pl.pallas_call(functools.partial(forward_kernel, source_plan, result_plan...]
  transfers between devices with their start and end apart: 49 -> 49, of which waited for: 26 -> 25; matrix products, arithmetic and copies ran while one was open for 2% -> 2% of each run, Pallas kernels for 0% -> 0%
where the time goes in v6:
time: 229 us; the launch traced here: 228 us
  waiting for transfers between devices  130 us (57%)
  starting transfers between devices  66.8 us (29%)
  Pallas kernels  23.4 us (10%)
  other arithmetic  3.82 us (2%)
  local copies, waits for them, and re-layouts  2.94 us (1%)
    ppermute x46, waiting for transfers between devices, shift(): return lax.ppermute(value, axes, perm)  120 us
    ppermute x46, starting transfers between devices, shift(): return lax.ppermute(value, axes, perm)  64 us
    ppermute x3, waiting for transfers between devices, exchange(): return lax.ppermute(value, axis, perm)  10.5 us
    pallas_call x1, Pallas kernels, forward_sweep(): pl.pallas_call(functools.partial(forward_kernel, source_plan, result_plan...  9.8 us
    pallas_call x1, Pallas kernels, backward_sweep(): pl.pallas_call(functools.partial(backward_kernel, source_plan, slab, batc...  9.26 us
  transfers between devices with their start and end apart: 49, of which 25 were waited for; matrix products, arithmetic and copies ran while one was open for 2% of the time, Pallas kernels for 0%

profile of v6, /device:TPU:1, one launch (start us, length us, event | category | flops | bytes accessed | tf_op | source)
XLA Modules:
  0.0 228.5 jit_solution(14547760289136341802)
XLA Ops:
  1.7 2.5 %collective-permute-start = (bf16[1024,128]{1,0:T(8,128)(2,1)S(1)}, bf16[1024,128]{1,0:T(8,128)(2,1)S(1)}, u32[]{:S(2)}, u32[]{:S(2)}) collective-permute-start(bf16[1024,128]{1,0:T(8,128)(2,1)S(1)} %get-tuple-element.68.first), channel_id=1, source_target_pairs={{64,0},{80,16},{96,32},{112,48},{0,64},{16,80},{32,96},{48,112},{6... | collective-permute-start | bytes 786440 | tf_op jit(solution)/shard_map/ppermute | solution.py:367
  4.3 2.7 %collective-permute-start.1 = (bf16[1024,128]{1,0:T(8,128)(2,1)S(1)}, bf16[1024,128]{1,0:T(8,128)(2,1)S(1)}, u32[]{:S(2)}, u32[]{:S(2)}) collective-permute-start(bf16[1024,128]{1,0:T(8,128)(2,1)S(1)} %get-tuple-element.67.refs_0_), channel_id=1, source_target_pairs={{16,0},{32,16},{48,32},{0,48},{80,64},{96,80},{112,96},{64,112},{1... | collective-permute-start | bytes 786440 | tf_op jit(solution)/shard_map/ppermute | solution.py:367
  8.1 2.2 collective-permute-done.first_pair
  10.3 2.4 %collective-permute-done.1.refs_1_ = bf16[1024,128]{1,0:T(8,128)(2,1)S(1)} collective-permute-done((bf16[1024,128]{1,0:T(8,128)(2,1)S(1)}, bf16[1024,128]{1,0:T(8,128)(2,1)S(1)}, u32[]{:S(2)}, u32[]{:S(2)}) %collective-permute-start.1) | collective-permute-done | bytes 262176 | tf_op jit(solution)/shard_map/ppermute | solution.py:367
  12.7 2.4 %collective-permute-done.2.refs_2_ = bf16[1024,128]{1,0:T(8,128)(2,1)S(1)} collective-permute-done((bf16[1024,128]{1,0:T(8,128)(2,1)S(1)}, bf16[1024,128]{1,0:T(8,128)(2,1)S(1)}, u32[]{:S(2)}, u32[]{:S(2)}) %collective-permute-start.2) | collective-permute-done | bytes 262176 | tf_op jit(solution)/shard_map/ppermute | solution.py:367
  15.1 7.2 %collective-permute-done.3.refs_3_ = bf16[1024,128]{1,0:T(8,128)(2,1)S(1)} collective-permute-done((bf16[1024,128]{1,0:T(8,128)(2,1)S(1)}, bf16[1024,128]{1,0:T(8,128)(2,1)S(1)}, u32[]{:S(2)}, u32[]{:S(2)}) %collective-permute-start.3) | collective-permute-done | bytes 262176 | tf_op jit(solution)/shard_map/ppermute | solution.py:367
  24.1 1.4 collective-permute-start.9
  25.5 10.0 %collective-permute-done.4.refs_6_ = bf16[2048,128]{1,0:T(8,128)(2,1)S(1)} collective-permute-done((bf16[2048,128]{1,0:T(8,128)(2,1)S(1)}, bf16[2048,128]{1,0:T(8,128)(2,1)S(1)}, u32[]{:S(2)}, u32[]{:S(2)}) %collective-permute-start.4) | collective-permute-done | bytes 524320 | tf_op jit(solution)/shard_map/ppermute | solution.py:367
  35.4 2.8 %collective-permute-start.8 = (bf16[2048,128]{1,0:T(8,128)(2,1)S(1)}, bf16[2048,128]{1,0:T(8,128)(2,1)S(1)}, u32[]{:S(2)}, u32[]{:S(2)}) collective-permute-start(bf16[2048,128]{1,0:T(8,128)(2,1)S(1)} %get-tuple-element.29.refs_4_), channel_id=1, source_target_pairs={{8,0},{0,8},{9,1},{1,9},{10,2},{2,10},{11,3},{3,11},{12,4},{4,12},... | collective-permute-start | bytes 1572872 | tf_op jit(solution)/shard_map/ppermute | solution.py:367
  38.2 8.7 %collective-permute-done.7.refs_9_ = bf16[4096,128]{1,0:T(8,128)(2,1)} collective-permute-done((bf16[4096,128]{1,0:T(8,128)(2,1)S(1)}, bf16[4096,128]{1,0:T(8,128)(2,1)}, u32[]{:S(2)}, u32[]{:S(2)}) %collective-permute-start.7) | collective-permute-done | bytes 1048608 | tf_op jit(solution)/shard_map/ppermute | solution.py:367
  46.9 1.3 collective-permute-start.13
  54.0 9.8 %forward.1 = (bf16[2048,128]{1,0:T(8,128)(2,1)S(1)}, bf16[2048,128]{1,0:T(8,128)(2,1)S(1)}, bf16[2048,128]{1,0:T(8,128)(2,1)S(1)}, bf16[2048,128]{1,0:T(8,128)(2...) custom-call(s32[1]{0:T(128)} %bitcast.4.refs_0_, s32[384]{0:T(512)S(1)} %get-tuple-element.70.refs_1_, ...), custom_call_target="tpu_custom_call" | custom-call | flops 1024 | bytes 1024 | tf_op jit(solution)/shard_map/forward/pallas_call | solution.py:124
  63.8 2.1 collective-permute-start.17
  65.9 3.1 %collective-permute-start.14 = (bf16[2048,128]{1,0:T(8,128)(2,1)S(1)}, bf16[2048,128]{1,0:T(8,128)(2,1)S(1)}, u32[]{:S(2)}, u32[]{:S(2)}) collective-permute-start(bf16[2048,128]{1,0:T(8,128)(2,1)S(1)} %get-tuple-element.32), channel_id=1, source_target_pairs={{3,0},{0,1},{1,2},{2,3},{7,4},{4,5},{5,6},{6,7},{11,8},{8,9},{9,10... | collective-permute-start | bytes 1572872 | tf_op jit(solution)/shard_map/ppermute | solution.py:367
  69.0 2.5 %collective-permute-start.16 = (bf16[2048,128]{1,0:T(8,128)(2,1)S(1)}, bf16[2048,128]{1,0:T(8,128)(2,1)S(1)}, u32[]{:S(2)}, u32[]{:S(2)}) collective-permute-start(bf16[2048,128]{1,0:T(8,128)(2,1)S(1)} %get-tuple-element.34), channel_id=1, source_target_pairs={{1,0},{2,1},{3,2},{0,3},{5,4},{6,5},{7,6},{4,7},{9,8},{10,9},{11,1... | collective-permute-start | bytes 1572872 | tf_op jit(solution)/shard_map/ppermute | solution.py:367
  71.4 9.7 %collective-permute-done.14.refs_1_ = bf16[2048,128]{1,0:T(8,128)(2,1)S(1)} collective-permute-done((bf16[2048,128]{1,0:T(8,128)(2,1)S(1)}, bf16[2048,128]{1,0:T(8,128)(2,1)S(1)}, u32[]{:S(2)}, u32[]{:S(2)}) %collective-permute-start.14) | collective-permute-done | bytes 524320 | tf_op jit(solution)/shard_map/ppermute | solution.py:367
  81.2 10.0 %collective-permute-done.15.refs_2_ = bf16[2048,128]{1,0:T(8,128)(2,1)S(1)} collective-permute-done((bf16[2048,128]{1,0:T(8,128)(2,1)S(1)}, bf16[2048,128]{1,0:T(8,128)(2,1)S(1)}, u32[]{:S(2)}, u32[]{:S(2)}) %collective-permute-start.15) | collective-permute-done | bytes 524320 | tf_op jit(solution)/shard_map/ppermute | solution.py:367
  92.1 2.8 %collective-permute-start.18 = (bf16[1024,128]{1,0:T(8,128)(2,1)S(1)}, bf16[1024,128]{1,0:T(8,128)(2,1)S(1)}, u32[]{:S(2)}, u32[]{:S(2)}) collective-permute-start(bf16[1024,128]{1,0:T(8,128)(2,1)S(1)} %get-tuple-element.37), channel_id=1, source_target_pairs={{4,0},{5,1},{6,2},{7,3},{0,4},{1,5},{2,6},{3,7},{12,8},{13,9},{14,... | collective-permute-start | bytes 786440 | tf_op jit(solution)/shard_map/ppermute | solution.py:367
  94.9 3.3 %collective-permute-start.19 = (bf16[1024,128]{1,0:T(8,128)(2,1)S(1)}, bf16[1024,128]{1,0:T(8,128)(2,1)S(1)}, u32[]{:S(2)}, u32[]{:S(2)}) collective-permute-start(bf16[1024,128]{1,0:T(8,128)(2,1)S(1)} %get-tuple-element.38), channel_id=1, source_target_pairs={{3,0},{0,1},{1,2},{2,3},{7,4},{4,5},{5,6},{6,7},{11,8},{8,9},{9,10... | collective-permute-start | bytes 786440 | tf_op jit(solution)/shard_map/ppermute | solution.py:367
  100.5 3.0 %collective-permute-done.19.refs_7_ = bf16[1024,128]{1,0:T(8,128)(2,1)S(1)} collective-permute-done((bf16[1024,128]{1,0:T(8,128)(2,1)S(1)}, bf16[1024,128]{1,0:T(8,128)(2,1)S(1)}, u32[]{:S(2)}, u32[]{:S(2)}) %collective-permute-start.19) | collective-permute-done | bytes 262176 | tf_op jit(solution)/shard_map/ppermute | solution.py:367
  103.5 7.2 %collective-permute-done.20.refs_8_ = bf16[1024,128]{1,0:T(8,128)(2,1)S(1)} collective-permute-done((bf16[1024,128]{1,0:T(8,128)(2,1)S(1)}, bf16[1024,128]{1,0:T(8,128)(2,1)S(1)}, u32[]{:S(2)}, u32[]{:S(2)}) %collective-permute-start.20) | collective-permute-done | bytes 262176 | tf_op jit(solution)/shard_map/ppermute | solution.py:367
  110.7 2.2 middle.1
  113.1 2.5 %collective-permute-start.23 = (bf16[1024,128]{1,0:T(8,128)(2,1)S(1)}, bf16[1024,128]{1,0:T(8,128)(2,1)S(1)}, u32[]{:S(2)}, u32[]{:S(2)}) collective-permute-start(bf16[1024,128]{1,0:T(8,128)(2,1)S(1)} %get-tuple-element.43.refs_0_), channel_id=1, source_target_pairs={{1,0},{2,1},{3,2},{0,3},{5,4},{6,5},{7,6},{4,7},{9,8},{10,9},{11,1... | collective-permute-start | bytes 786440 | tf_op jit(solution)/shard_map/ppermute | solution.py:367
  115.6 1.4 collective-permute-start.24
  117.0 3.6 %collective-permute-done.22.first_pair = bf16[1024,128]{1,0:T(8,128)(2,1)S(1)} collective-permute-done((bf16[1024,128]{1,0:T(8,128)(2,1)S(1)}, bf16[1024,128]{1,0:T(8,128)(2,1)S(1)}, u32[]{:S(2)}, u32[]{:S(2)}) %collective-permute-start.22) | collective-permute-done | bytes 262176 | tf_op jit(solution)/shard_map/ppermute | solution.py:367
  120.5 2.9 %collective-permute-done.24.refs_2_ = bf16[1024,128]{1,0:T(8,128)(2,1)S(1)} collective-permute-done((bf16[1024,128]{1,0:T(8,128)(2,1)S(1)}, bf16[1024,128]{1,0:T(8,128)(2,1)S(1)}, u32[]{:S(2)}, u32[]{:S(2)}) %collective-permute-start.24) | collective-permute-done | bytes 262176 | tf_op jit(solution)/shard_map/ppermute | solution.py:367
  123.4 7.5 %collective-permute-done.25.refs_3_ = bf16[1024,128]{1,0:T(8,128)(2,1)S(1)} collective-permute-done((bf16[1024,128]{1,0:T(8,128)(2,1)S(1)}, bf16[1024,128]{1,0:T(8,128)(2,1)S(1)}, u32[]{:S(2)}, u32[]{:S(2)}) %collective-permute-start.25) | collective-permute-done | bytes 262176 | tf_op jit(solution)/shard_map/ppermute | solution.py:367
  131.0 2.8 %collective-permute-start.29 = (bf16[4096,128]{1,0:T(8,128)(2,1)S(1)}, bf16[4096,128]{1,0:T(8,128)(2,1)S(1)}, u32[]{:S(2)}, u32[]{:S(2)}) collective-permute-start(bf16[4096,128]{1,0:T(8,128)(2,1)S(1)} %get-tuple-element.45.refs_6_), channel_id=1, source_target_pairs={{4,0},{5,1},{6,2},{7,3},{0,4},{1,5},{2,6},{3,7},{12,8},{13,9},{14,... | collective-permute-start | bytes 3145736 | tf_op jit(solution)/shard_map/ppermute | solution.py:367
  136.1 4.7 %collective-permute-done.30 = f32[256,256]{1,0:T(8,128)S(1)} collective-permute-done((f32[256,256]{1,0:T(8,128)S(1)}, f32[256,256]{1,0:T(8,128)S(1)}, u32[]{:S(2)}, u32[]{:S(2)}) %collective-permute-start.30) | collective-permute-done | bytes 262176 | tf_op jit(solution)/shard_map/ppermute | solution.py:373
  140.9 1.7 collective-permute-start.31
  142.6 5.7 %collective-permute-done.31 = f32[256,256]{1,0:T(8,128)S(1)} collective-permute-done((f32[256,256]{1,0:T(8,128)S(1)}, f32[256,256]{1,0:T(8,128)S(1)}, u32[]{:S(2)}, u32[]{:S(2)}) %collective-permute-start.31) | collective-permute-done | bytes 262176 | tf_op jit(solution)/shard_map/ppermute | solution.py:373
  148.4 12.3 %collective-permute-done.28.refs_9_ = bf16[2048,128]{1,0:T(8,128)(2,1)S(1)} collective-permute-done((bf16[2048,128]{1,0:T(8,128)(2,1)S(1)}, bf16[2048,128]{1,0:T(8,128)(2,1)S(1)}, u32[]{:S(2)}, u32[]{:S(2)}) %collective-permute-start.28) | collective-permute-done | bytes 524320 | tf_op jit(solution)/shard_map/ppermute | solution.py:367
  160.7 9.3 %backward.1 = (bf16[8192,128]{1,0:T(8,128)(2,1)}, bf16[8192,128]{1,0:T(8,128)(2,1)}, bf16[8192,128]{1,0:T(8,128)(2,1)}, bf16[8192,128]{1,0:T(8,128)(2,1)}) custom-call(s32[1]{0:T(128)} %bitcast.5.refs_0_, s32[384]{0:T(512)S(1)} %get-tuple-element.72.refs_1_, s32[384]{0:T(512)S(1)} %get-tuple-element.69.refs_2_, s32[16]{0:T(128)S(1)} %fusion.29.refs_3_, ...), custom_call_target="tpu_custom_call" | custom-call | flops 1024 | bytes 1024 | tf_op jit(solution)/shard_map/backward/pallas_call | solution.py:238
  170.6 3.3 %collective-permute-start.44 = (bf16[256,256]{1,0:T(8,128)(2,1)S(1)}, bf16[256,256]{1,0:T(8,128)(2,1)S(1)}, u32[]{:S(2)}, u32[]{:S(2)}) collective-permute-start(bf16[256,256]{1,0:T(8,128)(2,1)S(1)} %get-tuple-element.57), channel_id=1, source_target_pairs={{3,0},{0,1},{1,2},{2,3},{7,4},{4,5},{5,6},{6,7},{11,8},{8,9},{9,10... | collective-permute-start | bytes 393224 | tf_op jit(solution)/shard_map/ppermute | solution.py:367
  173.9 1.5 collective-permute-start.43
  175.3 2.1 collective-permute-start.42
  177.4 2.2 add_convert_fusion
  179.6 3.1 %collective-permute-start.37 = (bf16[4096,128]{1,0:T(8,128)(2,1)S(1)}, bf16[4096,128]{1,0:T(8,128)(2,1)S(1)}, u32[]{:S(2)}, u32[]{:S(2)}) collective-permute-start(bf16[4096,128]{1,0:T(8,128)(2,1)S(1)} %get-tuple-element.61), channel_id=1, source_target_pairs={{64,0},{80,16},{96,32},{112,48},{0,64},{16,80},{32,96},{48,112},{6... | collective-permute-start | bytes 3145736 | tf_op jit(solution)/shard_map/ppermute | solution.py:367
  184.3 1.7 collective-permute-start.34
  185.9 2.4 %collective-permute-start.35 = (bf16[2048,128]{1,0:T(8,128)(2,1)S(1)}, bf16[2048,128]{1,0:T(8,128)(2,1)S(1)}, u32[]{:S(2)}, u32[]{:S(2)}) collective-permute-start(bf16[2048,128]{1,0:T(8,128)(2,1)S(1)} %get-tuple-element.63), channel_id=1, source_target_pairs={{16,0},{32,16},{48,32},{0,48},{80,64},{96,80},{112,96},{64,112},{1... | collective-permute-start | bytes 1572872 | tf_op jit(solution)/shard_map/ppermute | solution.py:367
  188.4 3.9 %collective-permute-start.48 = (bf16[256,256]{1,0:T(8,128)(2,1)S(1)}, bf16[256,256]{1,0:T(8,128)(2,1)S(1)}, u32[]{:S(2)}, u32[]{:S(2)}) collective-permute-start(bf16[256,256]{1,0:T(8,128)(2,1)S(1)} %get-tuple-element.55), channel_id=1, source_target_pairs={{68,0},{64,4},{4,64},{0,68},{69,1},{65,5},{5,65},{1,69},{70,2},{66... | collective-permute-start | bytes 393224 | tf_op jit(solution)/shard_map/ppermute | solution.py:367
  192.3 16.4 %collective-permute-done.33.refs_1_ = bf16[2048,128]{1,0:T(8,128)(2,1)S(1)} collective-permute-done((bf16[2048,128]{1,0:T(8,128)(2,1)S(1)}, bf16[2048,128]{1,0:T(8,128)(2,1)S(1)}, u32[]{:S(2)}, u32[]{:S(2)}) %collective-permute-start.33) | collective-permute-done | bytes 524320 | tf_op jit(solution)/shard_map/ppermute | solution.py:367
  209.7 2.4 %collective-permute-start.46 = (bf16[256,256]{1,0:T(8,128)(2,1)S(1)}, bf16[256,256]{1,0:T(8,128)(2,1)S(1)}, u32[]{:S(2)}, u32[]{:S(2)}) collective-permute-start(bf16[256,256]{1,0:T(8,128)(2,1)S(1)} %get-tuple-element.55), channel_id=1, source_target_pairs={{4,0},{0,4},{68,64},{64,68},{5,1},{1,5},{69,65},{65,69},{6,2},{2,6... | collective-permute-start | bytes 393224 | tf_op jit(solution)/shard_map/ppermute | solution.py:367
  213.0 2.5 %collective-permute-start.40 = (bf16[1024,128]{1,0:T(8,128)(2,1)S(1)}, bf16[1024,128]{1,0:T(8,128)(2,1)S(1)}, u32[]{:S(2)}, u32[]{:S(2)}) collective-permute-start(bf16[1024,128]{1,0:T(8,128)(2,1)S(1)} %get-tuple-element.53), channel_id=1, source_target_pairs={{32,0},{48,16},{0,32},{16,48},{96,64},{112,80},{64,96},{80,112},{3... | collective-permute-start | bytes 786440 | tf_op jit(solution)/shard_map/ppermute | solution.py:367
  215.5 1.6 collective-permute-done.46
  217.9 3.5 %collective-permute-done.38.refs_4_ = bf16[1024,128]{1,0:T(8,128)(2,1)S(1)} collective-permute-done((bf16[1024,128]{1,0:T(8,128)(2,1)S(1)}, bf16[1024,128]{1,0:T(8,128)(2,1)S(1)}, u32[]{:S(2)}, u32[]{:S(2)}) %collective-permute-start.38) | collective-permute-done | bytes 262176 | tf_op jit(solution)/shard_map/ppermute | solution.py:367
  221.4 5.3 %collective-permute-done.40.refs_8_ = bf16[1024,128]{1,0:T(8,128)(2,1)S(1)} collective-permute-done((bf16[1024,128]{1,0:T(8,128)(2,1)S(1)}, bf16[1024,128]{1,0:T(8,128)(2,1)S(1)}, u32[]{:S(2)}, u32[]{:S(2)}) %collective-permute-start.40) | collective-permute-done | bytes 262176 | tf_op jit(solution)/shard_map/ppermute | solution.py:367
  227.1 1.3 final.1
  (88 shorter events, 20.2 us)
Async XLA Ops:
  1.7 8.6 %collective-permute-start = (bf16[1024,128]{1,0:T(8,128)(2,1)S(1)}, bf16[1024,128]{1,0:T(8,128)(2,1)S(1)}, u32[]{:S(2)}, u32[]{:S(2)}) collective-permute-start(bf16[1024,128]{1,0:T(8,128)(2,1)S(1)} %get-tuple-element.68.first), channel_id=1, source_target_pairs={{64,0},{80,16},{96,32},{112,48},{0,64},{16,80},{32,96},{48,112},{6... | collective-permute-start | bytes 786440 | tf_op jit(solution)/shard_map/ppermute | solution.py:367
  4.3 8.4 %collective-permute-start.1 = (bf16[1024,128]{1,0:T(8,128)(2,1)S(1)}, bf16[1024,128]{1,0:T(8,128)(2,1)S(1)}, u32[]{:S(2)}, u32[]{:S(2)}) collective-permute-start(bf16[1024,128]{1,0:T(8,128)(2,1)S(1)} %get-tuple-element.67.refs_0_), channel_id=1, source_target_pairs={{16,0},{32,16},{48,32},{0,48},{80,64},{96,80},{112,96},{64,112},{1... | collective-permute-start | bytes 786440 | tf_op jit(solution)/shard_map/ppermute | solution.py:367
  7.0 8.1 %collective-permute-start.2 = (bf16[1024,128]{1,0:T(8,128)(2,1)S(1)}, bf16[1024,128]{1,0:T(8,128)(2,1)S(1)}, u32[]{:S(2)}, u32[]{:S(2)}) collective-permute-start(bf16[1024,128]{1,0:T(8,128)(2,1)S(1)} %get-tuple-element.67.refs_0_), channel_id=1, source_target_pairs={{32,0},{48,16},{0,32},{16,48},{96,64},{112,80},{64,96},{80,112},{3... | collective-permute-start | bytes 786440 | tf_op jit(solution)/shard_map/ppermute | solution.py:367
  7.4 15.0 %collective-permute-start.3 = (bf16[1024,128]{1,0:T(8,128)(2,1)S(1)}, bf16[1024,128]{1,0:T(8,128)(2,1)S(1)}, u32[]{:S(2)}, u32[]{:S(2)}) collective-permute-start(bf16[1024,128]{1,0:T(8,128)(2,1)S(1)} %get-tuple-element.67.refs_0_), channel_id=1, source_target_pairs={{48,0},{0,16},{16,32},{32,48},{112,64},{64,80},{80,96},{96,112},{4... | collective-permute-start | bytes 786440 | tf_op jit(solution)/shard_map/ppermute | solution.py:367
  22.5 24.4 %collective-permute-start.7 = (bf16[4096,128]{1,0:T(8,128)(2,1)S(1)}, bf16[4096,128]{1,0:T(8,128)(2,1)}, u32[]{:S(2)}, u32[]{:S(2)}) collective-permute-start(bf16[4096,128]{1,0:T(8,128)(2,1)S(1)} %get-tuple-element.30.refs_5_), channel_id=1, source_target_pairs={{64,0},{80,16},{96,32},{112,48},{0,64},{16,80},{32,96},{48,112},{6... | collective-permute-start | bytes 3145736 | tf_op jit(solution)/shard_map/ppermute | solution.py:367
  22.6 12.8 %collective-permute-start.4 = (bf16[2048,128]{1,0:T(8,128)(2,1)S(1)}, bf16[2048,128]{1,0:T(8,128)(2,1)S(1)}, u32[]{:S(2)}, u32[]{:S(2)}) collective-permute-start(bf16[2048,128]{1,0:T(8,128)(2,1)S(1)} %get-tuple-element.29.refs_4_), channel_id=1, source_target_pairs={{16,0},{32,16},{48,32},{0,48},{80,64},{96,80},{112,96},{64,112},{1... | collective-permute-start | bytes 1572872 | tf_op jit(solution)/shard_map/ppermute | solution.py:367
  22.7 25.6 %collective-permute-start.5 = (bf16[2048,128]{1,0:T(8,128)(2,1)S(1)}, bf16[2048,128]{1,0:T(8,128)(2,1)S(1)}, u32[]{:S(2)}, u32[]{:S(2)}) collective-permute-start(bf16[2048,128]{1,0:T(8,128)(2,1)S(1)} %get-tuple-element.29.refs_4_), channel_id=1, source_target_pairs={{32,0},{48,16},{0,32},{16,48},{96,64},{112,80},{64,96},{80,112},{3... | collective-permute-start | bytes 1572872 | tf_op jit(solution)/shard_map/ppermute | solution.py:367
  23.1 26.2 %collective-permute-start.6 = (bf16[2048,128]{1,0:T(8,128)(2,1)S(1)}, bf16[2048,128]{1,0:T(8,128)(2,1)S(1)}, u32[]{:S(2)}, u32[]{:S(2)}) collective-permute-start(bf16[2048,128]{1,0:T(8,128)(2,1)S(1)} %get-tuple-element.29.refs_4_), channel_id=1, source_target_pairs={{48,0},{0,16},{16,32},{32,48},{112,64},{64,80},{80,96},{96,112},{4... | collective-permute-start | bytes 1572872 | tf_op jit(solution)/shard_map/ppermute | solution.py:367
  24.1 27.3 %collective-permute-start.9 = (bf16[4096,128]{1,0:T(8,128)(2,1)S(1)}, bf16[4096,128]{1,0:T(8,128)(2,1)}, u32[]{:S(2)}, u32[]{:S(2)}) collective-permute-start(bf16[4096,128]{1,0:T(8,128)(2,1)S(1)} %get-tuple-element.30.refs_5_), channel_id=1, source_target_pairs={{8,0},{0,8},{9,1},{1,9},{10,2},{2,10},{11,3},{3,11},{12,4},{4,12},... | collective-permute-start | bytes 3145736 | tf_op jit(solution)/shard_map/ppermute | solution.py:367
  35.4 14.4 %collective-permute-start.8 = (bf16[2048,128]{1,0:T(8,128)(2,1)S(1)}, bf16[2048,128]{1,0:T(8,128)(2,1)S(1)}, u32[]{:S(2)}, u32[]{:S(2)}) collective-permute-start(bf16[2048,128]{1,0:T(8,128)(2,1)S(1)} %get-tuple-element.29.refs_4_), channel_id=1, source_target_pairs={{8,0},{0,8},{9,1},{1,9},{10,2},{2,10},{11,3},{3,11},{12,4},{4,12},... | collective-permute-start | bytes 1572872 | tf_op jit(solution)/shard_map/ppermute | solution.py:367
  46.9 6.0 %collective-permute-start.13 = (bf16[4096,128]{1,0:T(8,128)(2,1)}, bf16[4096,128]{1,0:T(8,128)(2,1)}, u32[]{:S(2)}, u32[]{:S(2)}) collective-permute-start(bf16[4096,128]{1,0:T(8,128)(2,1)} %collective-permute-done.7.refs_9_), channel_id=1, source_target_pairs={{8,0},{0,8},{9,1},{1,9},{10,2},{2,10},{11,3},{3,11},{12,4},{4,12},... | collective-permute-start | bytes 3145736 | tf_op jit(solution)/shard_map/ppermute | solution.py:367
  48.2 3.2 %collective-permute-start.10 = (bf16[2048,128]{1,0:T(8,128)(2,1)S(1)}, bf16[2048,128]{1,0:T(8,128)(2,1)}, u32[]{:S(2)}, u32[]{:S(2)}) collective-permute-start(bf16[2048,128]{1,0:T(8,128)(2,1)S(1)} %collective-permute-done.4.refs_6_), channel_id=1, source_target_pairs={{8,0},{0,8},{9,1},{1,9},{10,2},{2,10},{11,3},{3,11},{12,4},{4,12},... | collective-permute-start | bytes 1572872 | tf_op jit(solution)/shard_map/ppermute | solution.py:367
  49.3 2.8 %collective-permute-start.11 = (bf16[2048,128]{1,0:T(8,128)(2,1)S(1)}, bf16[2048,128]{1,0:T(8,128)(2,1)}, u32[]{:S(2)}, u32[]{:S(2)}) collective-permute-start(bf16[2048,128]{1,0:T(8,128)(2,1)S(1)} %collective-permute-done.5.refs_7_), channel_id=1, source_target_pairs={{8,0},{0,8},{9,1},{1,9},{10,2},{2,10},{11,3},{3,11},{12,4},{4,12},... | collective-permute-start | bytes 1572872 | tf_op jit(solution)/shard_map/ppermute | solution.py:367
  63.8 28.0 %collective-permute-start.17 = (bf16[4096,128]{1,0:T(8,128)(2,1)}, bf16[4096,128]{1,0:T(8,128)(2,1)S(1)}, u32[]{:S(2)}, u32[]{:S(2)}) collective-permute-start(bf16[4096,128]{1,0:T(8,128)(2,1)} %get-tuple-element.36), channel_id=1, source_target_pairs={{4,0},{5,1},{6,2},{7,3},{0,4},{1,5},{2,6},{3,7},{12,8},{13,9},{14,... | collective-permute-start | bytes 3145736 | tf_op jit(solution)/shard_map/ppermute | solution.py:367
  65.9 15.3 %collective-permute-start.14 = (bf16[2048,128]{1,0:T(8,128)(2,1)S(1)}, bf16[2048,128]{1,0:T(8,128)(2,1)S(1)}, u32[]{:S(2)}, u32[]{:S(2)}) collective-permute-start(bf16[2048,128]{1,0:T(8,128)(2,1)S(1)} %get-tuple-element.32), channel_id=1, source_target_pairs={{3,0},{0,1},{1,2},{2,3},{7,4},{4,5},{5,6},{6,7},{11,8},{8,9},{9,10... | collective-permute-start | bytes 1572872 | tf_op jit(solution)/shard_map/ppermute | solution.py:367
  69.0 22.2 %collective-permute-start.15 = (bf16[2048,128]{1,0:T(8,128)(2,1)S(1)}, bf16[2048,128]{1,0:T(8,128)(2,1)S(1)}, u32[]{:S(2)}, u32[]{:S(2)}) collective-permute-start(bf16[2048,128]{1,0:T(8,128)(2,1)S(1)} %get-tuple-element.33), channel_id=1, source_target_pairs={{2,0},{3,1},{0,2},{1,3},{6,4},{7,5},{4,6},{5,7},{10,8},{11,9},{8,1... | collective-permute-start | bytes 1572872 | tf_op jit(solution)/shard_map/ppermute | solution.py:367
  69.0 22.8 %collective-permute-start.16 = (bf16[2048,128]{1,0:T(8,128)(2,1)S(1)}, bf16[2048,128]{1,0:T(8,128)(2,1)S(1)}, u32[]{:S(2)}, u32[]{:S(2)}) collective-permute-start(bf16[2048,128]{1,0:T(8,128)(2,1)S(1)} %get-tuple-element.34), channel_id=1, source_target_pairs={{1,0},{2,1},{3,2},{0,3},{5,4},{6,5},{7,6},{4,7},{9,8},{10,9},{11,1... | collective-permute-start | bytes 1572872 | tf_op jit(solution)/shard_map/ppermute | solution.py:367
  92.1 8.5 %collective-permute-start.18 = (bf16[1024,128]{1,0:T(8,128)(2,1)S(1)}, bf16[1024,128]{1,0:T(8,128)(2,1)S(1)}, u32[]{:S(2)}, u32[]{:S(2)}) collective-permute-start(bf16[1024,128]{1,0:T(8,128)(2,1)S(1)} %get-tuple-element.37), channel_id=1, source_target_pairs={{4,0},{5,1},{6,2},{7,3},{0,4},{1,5},{2,6},{3,7},{12,8},{13,9},{14,... | collective-permute-start | bytes 786440 | tf_op jit(solution)/shard_map/ppermute | solution.py:367
  94.9 8.7 %collective-permute-start.19 = (bf16[1024,128]{1,0:T(8,128)(2,1)S(1)}, bf16[1024,128]{1,0:T(8,128)(2,1)S(1)}, u32[]{:S(2)}, u32[]{:S(2)}) collective-permute-start(bf16[1024,128]{1,0:T(8,128)(2,1)S(1)} %get-tuple-element.38), channel_id=1, source_target_pairs={{3,0},{0,1},{1,2},{2,3},{7,4},{4,5},{5,6},{6,7},{11,8},{8,9},{9,10... | collective-permute-start | bytes 786440 | tf_op jit(solution)/shard_map/ppermute | solution.py:367
  98.1 12.5 %collective-permute-start.20 = (bf16[1024,128]{1,0:T(8,128)(2,1)S(1)}, bf16[1024,128]{1,0:T(8,128)(2,1)S(1)}, u32[]{:S(2)}, u32[]{:S(2)}) collective-permute-start(bf16[1024,128]{1,0:T(8,128)(2,1)S(1)} %get-tuple-element.39), channel_id=1, source_target_pairs={{2,0},{3,1},{0,2},{1,3},{6,4},{7,5},{4,6},{5,7},{10,8},{11,9},{8,1... | collective-permute-start | bytes 786440 | tf_op jit(solution)/shard_map/ppermute | solution.py:367
  99.5 11.2 %collective-permute-start.21 = (bf16[1024,128]{1,0:T(8,128)(2,1)S(1)}, bf16[1024,128]{1,0:T(8,128)(2,1)S(1)}, u32[]{:S(2)}, u32[]{:S(2)}) collective-permute-start(bf16[1024,128]{1,0:T(8,128)(2,1)S(1)} %get-tuple-element.40), channel_id=1, source_target_pairs={{1,0},{2,1},{3,2},{0,3},{5,4},{6,5},{7,6},{4,7},{9,8},{10,9},{11,1... | collective-permute-start | bytes 786440 | tf_op jit(solution)/shard_map/ppermute | solution.py:367
  112.9 7.6 %collective-permute-start.22 = (bf16[1024,128]{1,0:T(8,128)(2,1)S(1)}, bf16[1024,128]{1,0:T(8,128)(2,1)S(1)}, u32[]{:S(2)}, u32[]{:S(2)}) collective-permute-start(bf16[1024,128]{1,0:T(8,128)(2,1)S(1)} %get-tuple-element.42.first), channel_id=1, source_target_pairs={{4,0},{5,1},{6,2},{7,3},{0,4},{1,5},{2,6},{3,7},{12,8},{13,9},{14,... | collective-permute-start | bytes 786440 | tf_op jit(solution)/shard_map/ppermute | solution.py:367
  113.1 7.4 %collective-permute-start.23 = (bf16[1024,128]{1,0:T(8,128)(2,1)S(1)}, bf16[1024,128]{1,0:T(8,128)(2,1)S(1)}, u32[]{:S(2)}, u32[]{:S(2)}) collective-permute-start(bf16[1024,128]{1,0:T(8,128)(2,1)S(1)} %get-tuple-element.43.refs_0_), channel_id=1, source_target_pairs={{1,0},{2,1},{3,2},{0,3},{5,4},{6,5},{7,6},{4,7},{9,8},{10,9},{11,1... | collective-permute-start | bytes 786440 | tf_op jit(solution)/shard_map/ppermute | solution.py:367
  115.6 7.8 %collective-permute-start.24 = (bf16[1024,128]{1,0:T(8,128)(2,1)S(1)}, bf16[1024,128]{1,0:T(8,128)(2,1)S(1)}, u32[]{:S(2)}, u32[]{:S(2)}) collective-permute-start(bf16[1024,128]{1,0:T(8,128)(2,1)S(1)} %get-tuple-element.43.refs_0_), channel_id=1, source_target_pairs={{2,0},{3,1},{0,2},{1,3},{6,4},{7,5},{4,6},{5,7},{10,8},{11,9},{8,1... | collective-permute-start | bytes 786440 | tf_op jit(solution)/shard_map/ppermute | solution.py:367
  117.0 14.0 %collective-permute-start.25 = (bf16[1024,128]{1,0:T(8,128)(2,1)S(1)}, bf16[1024,128]{1,0:T(8,128)(2,1)S(1)}, u32[]{:S(2)}, u32[]{:S(2)}) collective-permute-start(bf16[1024,128]{1,0:T(8,128)(2,1)S(1)} %get-tuple-element.43.refs_0_), channel_id=1, source_target_pairs={{3,0},{0,1},{1,2},{2,3},{7,4},{4,5},{5,6},{6,7},{11,8},{8,9},{9,10... | collective-permute-start | bytes 786440 | tf_op jit(solution)/shard_map/ppermute | solution.py:367
  131.0 29.7 %collective-permute-start.29 = (bf16[4096,128]{1,0:T(8,128)(2,1)S(1)}, bf16[4096,128]{1,0:T(8,128)(2,1)S(1)}, u32[]{:S(2)}, u32[]{:S(2)}) collective-permute-start(bf16[4096,128]{1,0:T(8,128)(2,1)S(1)} %get-tuple-element.45.refs_6_), channel_id=1, source_target_pairs={{4,0},{5,1},{6,2},{7,3},{0,4},{1,5},{2,6},{3,7},{12,8},{13,9},{14,... | collective-permute-start | bytes 3145736 | tf_op jit(solution)/shard_map/ppermute | solution.py:367
  133.8 7.1 %collective-permute-start.30 = (f32[256,256]{1,0:T(8,128)S(1)}, f32[256,256]{1,0:T(8,128)S(1)}, u32[]{:S(2)}, u32[]{:S(2)}) collective-permute-start(f32[256,256]{1,0:T(8,128)S(1)} %get-tuple-element.46), channel_id=1, source_target_pairs={{16,0},{0,16},{48,32},{32,48},{17,1},{1,17},{49,33},{33,49},{18,2}... | collective-permute-start | bytes 786440 | tf_op jit(solution)/shard_map/ppermute | solution.py:373
  134.2 14.2 %collective-permute-start.26 = (bf16[2048,128]{1,0:T(8,128)(2,1)S(1)}, bf16[2048,128]{1,0:T(8,128)(2,1)S(1)}, u32[]{:S(2)}, u32[]{:S(2)}) collective-permute-start(bf16[2048,128]{1,0:T(8,128)(2,1)S(1)} %get-tuple-element.44.refs_5_), channel_id=1, source_target_pairs={{1,0},{2,1},{3,2},{0,3},{5,4},{6,5},{7,6},{4,7},{9,8},{10,9},{11,1... | collective-permute-start | bytes 1572872 | tf_op jit(solution)/shard_map/ppermute | solution.py:367
  134.2 14.2 %collective-permute-start.27 = (bf16[2048,128]{1,0:T(8,128)(2,1)S(1)}, bf16[2048,128]{1,0:T(8,128)(2,1)S(1)}, u32[]{:S(2)}, u32[]{:S(2)}) collective-permute-start(bf16[2048,128]{1,0:T(8,128)(2,1)S(1)} %get-tuple-element.44.refs_5_), channel_id=1, source_target_pairs={{2,0},{3,1},{0,2},{1,3},{6,4},{7,5},{4,6},{5,7},{10,8},{11,9},{8,1... | collective-permute-start | bytes 1572872 | tf_op jit(solution)/shard_map/ppermute | solution.py:367
  135.3 25.5 %collective-permute-start.28 = (bf16[2048,128]{1,0:T(8,128)(2,1)S(1)}, bf16[2048,128]{1,0:T(8,128)(2,1)S(1)}, u32[]{:S(2)}, u32[]{:S(2)}) collective-permute-start(bf16[2048,128]{1,0:T(8,128)(2,1)S(1)} %get-tuple-element.44.refs_5_), channel_id=1, source_target_pairs={{3,0},{0,1},{1,2},{2,3},{7,4},{4,5},{5,6},{6,7},{11,8},{8,9},{9,10... | collective-permute-start | bytes 1572872 | tf_op jit(solution)/shard_map/ppermute | solution.py:367
  140.9 7.4 %collective-permute-start.31 = (f32[256,256]{1,0:T(8,128)S(1)}, f32[256,256]{1,0:T(8,128)S(1)}, u32[]{:S(2)}, u32[]{:S(2)}) collective-permute-start(f32[256,256]{1,0:T(8,128)S(1)} %add.134), channel_id=1, source_target_pairs={{48,0},{32,16},{16,32},{0,48},{49,1},{33,17},{17,33},{1,49},{50,2}... | collective-permute-start | bytes 786440 | tf_op jit(solution)/shard_map/ppermute | solution.py:373
  170.0 7.4 %collective-permute-start.36 = (bf16[8192,128]{1,0:T(8,128)(2,1)}, bf16[8192,128]{1,0:T(8,128)(2,1)S(1)}, u32[]{:S(2)}, u32[]{:S(2)}) collective-permute-start(bf16[8192,128]{1,0:T(8,128)(2,1)} %get-tuple-element.50), channel_id=1, source_target_pairs={{8,0},{0,8},{9,1},{1,9},{10,2},{2,10},{11,3},{3,11},{12,4},{4,12},... | collective-permute-start | bytes 6291464 | tf_op jit(solution)/shard_map/ppermute | solution.py:367
  170.1 12.7 %collective-permute-start.32 = (bf16[8192,128]{1,0:T(8,128)(2,1)}, bf16[8192,128]{1,0:T(8,128)(2,1)S(1)}, u32[]{:S(2)}, u32[]{:S(2)}) collective-permute-start(bf16[8192,128]{1,0:T(8,128)(2,1)} %get-tuple-element.48), channel_id=1, source_target_pairs={{8,0},{0,8},{9,1},{1,9},{10,2},{2,10},{11,3},{3,11},{12,4},{4,12},... | collective-permute-start | bytes 6291464 | tf_op jit(solution)/shard_map/ppermute | solution.py:367
  170.6 12.8 %collective-permute-start.44 = (bf16[256,256]{1,0:T(8,128)(2,1)S(1)}, bf16[256,256]{1,0:T(8,128)(2,1)S(1)}, u32[]{:S(2)}, u32[]{:S(2)}) collective-permute-start(bf16[256,256]{1,0:T(8,128)(2,1)S(1)} %get-tuple-element.57), channel_id=1, source_target_pairs={{3,0},{0,1},{1,2},{2,3},{7,4},{4,5},{5,6},{6,7},{11,8},{8,9},{9,10... | collective-permute-start | bytes 393224 | tf_op jit(solution)/shard_map/ppermute | solution.py:367
  173.9 9.6 %collective-permute-start.43 = (bf16[256,256]{1,0:T(8,128)(2,1)S(1)}, bf16[256,256]{1,0:T(8,128)(2,1)S(1)}, u32[]{:S(2)}, u32[]{:S(2)}) collective-permute-start(bf16[256,256]{1,0:T(8,128)(2,1)S(1)} %get-tuple-element.57), channel_id=1, source_target_pairs={{2,0},{3,1},{0,2},{1,3},{6,4},{7,5},{4,6},{5,7},{10,8},{11,9},{8,1... | collective-permute-start | bytes 393224 | tf_op jit(solution)/shard_map/ppermute | solution.py:367
  175.3 8.1 %collective-permute-start.42 = (bf16[256,256]{1,0:T(8,128)(2,1)S(1)}, bf16[256,256]{1,0:T(8,128)(2,1)S(1)}, u32[]{:S(2)}, u32[]{:S(2)}) collective-permute-start(bf16[256,256]{1,0:T(8,128)(2,1)S(1)} %get-tuple-element.57), channel_id=1, source_target_pairs={{1,0},{2,1},{3,2},{0,3},{5,4},{6,5},{7,6},{4,7},{9,8},{10,9},{11,1... | collective-permute-start | bytes 393224 | tf_op jit(solution)/shard_map/ppermute | solution.py:367
  179.6 32.4 %collective-permute-start.37 = (bf16[4096,128]{1,0:T(8,128)(2,1)S(1)}, bf16[4096,128]{1,0:T(8,128)(2,1)S(1)}, u32[]{:S(2)}, u32[]{:S(2)}) collective-permute-start(bf16[4096,128]{1,0:T(8,128)(2,1)S(1)} %get-tuple-element.61), channel_id=1, source_target_pairs={{64,0},{80,16},{96,32},{112,48},{0,64},{16,80},{32,96},{48,112},{6... | collective-permute-start | bytes 3145736 | tf_op jit(solution)/shard_map/ppermute | solution.py:367
  183.3 25.3 %collective-permute-start.33 = (bf16[2048,128]{1,0:T(8,128)(2,1)S(1)}, bf16[2048,128]{1,0:T(8,128)(2,1)S(1)}, u32[]{:S(2)}, u32[]{:S(2)}) collective-permute-start(bf16[2048,128]{1,0:T(8,128)(2,1)S(1)} %get-tuple-element.65), channel_id=1, source_target_pairs={{48,0},{0,16},{16,32},{32,48},{112,64},{64,80},{80,96},{96,112},{4... | collective-permute-start | bytes 1572872 | tf_op jit(solution)/shard_map/ppermute | solution.py:367
  183.5 4.8 %collective-permute-start.45 = (f32[256,256]{1,0:T(8,128)S(1)}, f32[256,256]{1,0:T(8,128)S(1)}, u32[]{:S(2)}, u32[]{:S(2)}) collective-permute-start(f32[256,256]{1,0:T(8,128)S(1)} %convert_add_fusion), channel_id=1, source_target_pairs={{8,0},{0,8},{9,1},{1,9},{10,2},{2,10},{11,3},{3,11},{12,4},{4,12},... | collective-permute-start | bytes 786440 | tf_op jit(solution)/shard_map/ppermute | solution.py:373
  184.3 25.4 %collective-permute-start.34 = (bf16[2048,128]{1,0:T(8,128)(2,1)S(1)}, bf16[2048,128]{1,0:T(8,128)(2,1)S(1)}, u32[]{:S(2)}, u32[]{:S(2)}) collective-permute-start(bf16[2048,128]{1,0:T(8,128)(2,1)S(1)} %get-tuple-element.64), channel_id=1, source_target_pairs={{32,0},{48,16},{0,32},{16,48},{96,64},{112,80},{64,96},{80,112},{3... | collective-permute-start | bytes 1572872 | tf_op jit(solution)/shard_map/ppermute | solution.py:367
  185.9 26.1 %collective-permute-start.35 = (bf16[2048,128]{1,0:T(8,128)(2,1)S(1)}, bf16[2048,128]{1,0:T(8,128)(2,1)S(1)}, u32[]{:S(2)}, u32[]{:S(2)}) collective-permute-start(bf16[2048,128]{1,0:T(8,128)(2,1)S(1)} %get-tuple-element.63), channel_id=1, source_target_pairs={{16,0},{32,16},{48,32},{0,48},{80,64},{96,80},{112,96},{64,112},{1... | collective-permute-start | bytes 1572872 | tf_op jit(solution)/shard_map/ppermute | solution.py:367
  188.4 24.7 %collective-permute-start.48 = (bf16[256,256]{1,0:T(8,128)(2,1)S(1)}, bf16[256,256]{1,0:T(8,128)(2,1)S(1)}, u32[]{:S(2)}, u32[]{:S(2)}) collective-permute-start(bf16[256,256]{1,0:T(8,128)(2,1)S(1)} %get-tuple-element.55), channel_id=1, source_target_pairs={{68,0},{64,4},{4,64},{0,68},{69,1},{65,5},{5,65},{1,69},{70,2},{66... | collective-permute-start | bytes 393224 | tf_op jit(solution)/shard_map/ppermute | solution.py:367
  208.7 6.8 %collective-permute-start.47 = (bf16[256,256]{1,0:T(8,128)(2,1)S(1)}, bf16[256,256]{1,0:T(8,128)(2,1)S(1)}, u32[]{:S(2)}, u32[]{:S(2)}) collective-permute-start(bf16[256,256]{1,0:T(8,128)(2,1)S(1)} %get-tuple-element.55), channel_id=1, source_target_pairs={{64,0},{68,4},{0,64},{4,68},{65,1},{69,5},{1,65},{5,69},{66,2},{70... | collective-permute-start | bytes 393224 | tf_op jit(solution)/shard_map/ppermute | solution.py:367
  209.7 7.5 %collective-permute-start.46 = (bf16[256,256]{1,0:T(8,128)(2,1)S(1)}, bf16[256,256]{1,0:T(8,128)(2,1)S(1)}, u32[]{:S(2)}, u32[]{:S(2)}) collective-permute-start(bf16[256,256]{1,0:T(8,128)(2,1)S(1)} %get-tuple-element.55), channel_id=1, source_target_pairs={{4,0},{0,4},{68,64},{64,68},{5,1},{1,5},{69,65},{65,69},{6,2},{2,6... | collective-permute-start | bytes 393224 | tf_op jit(solution)/shard_map/ppermute | solution.py:367
  212.4 9.0 %collective-permute-start.38 = (bf16[1024,128]{1,0:T(8,128)(2,1)S(1)}, bf16[1024,128]{1,0:T(8,128)(2,1)S(1)}, u32[]{:S(2)}, u32[]{:S(2)}) collective-permute-start(bf16[1024,128]{1,0:T(8,128)(2,1)S(1)} %get-tuple-element.51), channel_id=1, source_target_pairs={{64,0},{80,16},{96,32},{112,48},{0,64},{16,80},{32,96},{48,112},{6... | collective-permute-start | bytes 786440 | tf_op jit(solution)/shard_map/ppermute | solution.py:367
  212.4 8.9 %collective-permute-start.39 = (bf16[1024,128]{1,0:T(8,128)(2,1)S(1)}, bf16[1024,128]{1,0:T(8,128)(2,1)S(1)}, u32[]{:S(2)}, u32[]{:S(2)}) collective-permute-start(bf16[1024,128]{1,0:T(8,128)(2,1)S(1)} %get-tuple-element.52), channel_id=1, source_target_pairs={{48,0},{0,16},{16,32},{32,48},{112,64},{64,80},{80,96},{96,112},{4... | collective-permute-start | bytes 786440 | tf_op jit(solution)/shard_map/ppermute | solution.py:367
  213.0 13.7 %collective-permute-start.40 = (bf16[1024,128]{1,0:T(8,128)(2,1)S(1)}, bf16[1024,128]{1,0:T(8,128)(2,1)S(1)}, u32[]{:S(2)}, u32[]{:S(2)}) collective-permute-start(bf16[1024,128]{1,0:T(8,128)(2,1)S(1)} %get-tuple-element.53), channel_id=1, source_target_pairs={{32,0},{48,16},{0,32},{16,48},{96,64},{112,80},{64,96},{80,112},{3... | collective-permute-start | bytes 786440 | tf_op jit(solution)/shard_map/ppermute | solution.py:367
  215.5 11.7 %collective-permute-start.41 = (bf16[1024,128]{1,0:T(8,128)(2,1)S(1)}, bf16[1024,128]{1,0:T(8,128)(2,1)S(1)}, u32[]{:S(2)}, u32[]{:S(2)}) collective-permute-start(bf16[1024,128]{1,0:T(8,128)(2,1)S(1)} %get-tuple-element.54), channel_id=1, source_target_pairs={{16,0},{32,16},{48,32},{0,48},{80,64},{96,80},{112,96},{64,112},{1... | collective-permute-start | bytes 786440 | tf_op jit(solution)/shard_map/ppermute | solution.py:367
  (10 other events, 198.1 us)
